TPU v7x, 32 devices: a whole 2x2x4 slice. The times are simulated.
32 devices in a mesh: ctx: 8 (over z, y), fsdp: 4 (over x, core).
Axes of the slice: x: 2, y: 2, z: 4, core: 2. Of those that a mesh axis runs over, the one named last changes fastest.
Arguments:
- tokens: bfloat16 [8, 1024, 1536], P('fsdp', 'ctx'), may hold values from -6 to 6
- segments: int32 [8, 1024], P('fsdp'), may hold values from 0 to 6, as said below
- valid: int32 [8, 1024], P('fsdp'), may hold values from 0 to 1, as said below
- expert_ids: int32 [8, 1024, 8], P('fsdp', 'ctx'), may hold values from 0 to 15, all different within a row
- slot_order: int32 [8, 1024], P('fsdp', 'ctx'), may hold values from 0 to 127, as said below
- cotangent: bfloat16 [8, 1024, 1536], P('fsdp', 'ctx'), may hold values from -6 to 6
- norm1_gain: bfloat16 [1536], P('fsdp'), may hold values from 0.5 to 1.5
- w_query: bfloat16 [1536, 1536], P('fsdp'), may hold values from -0.15625 to 0.15625
- key_weight: bfloat16 [1536, 512], P('fsdp'), may hold values from -0.15625 to 0.15625
- value_weight: bfloat16 [1536, 512], P('fsdp'), may hold values from -0.15625 to 0.15625
- w_output: bfloat16 [1536, 1536], P('fsdp'), may hold values from -2.5 to 2.5
- norm2_gain: bfloat16 [1536], P('fsdp'), may hold values from 0.5 to 1.5
- w_router: bfloat16 [1536, 16], P('fsdp'), may hold values from -0.078125 to 0.078125
- w_gate: bfloat16 [1536, 16, 512], P('fsdp'), may hold values from -0.15625 to 0.15625
- w_up: bfloat16 [1536, 16, 512], P('fsdp'), may hold values from -0.15625 to 0.15625
- w_down: bfloat16 [1536, 16, 512], P('fsdp'), may hold values from -0.75 to 0.75
Outputs:
- layer_out: bfloat16 [8, 1024, 1536], P('fsdp', 'ctx')
- input_grad: bfloat16 [8, 1024, 1536], P('fsdp', 'ctx')
- grad_norm1_gain: float32 [1536], P(('ctx', 'fsdp'))
- grad_query: float32 [1536, 1536], P(('ctx', 'fsdp'))
- grad_key: float32 [1536, 512], P(('ctx', 'fsdp'))
- grad_value: float32 [1536, 512], P(('ctx', 'fsdp'))
- grad_output: float32 [1536, 1536], P(('ctx', 'fsdp'))
- grad_norm2_gain: float32 [1536], P(('ctx', 'fsdp'))
- grad_router: float32 [1536, 16], P(('ctx', 'fsdp'))
- grad_gate: float32 [1536, 16, 512], P(('ctx', 'fsdp'))
- grad_up: float32 [1536, 16, 512], P(('ctx', 'fsdp'))
- grad_down: float32 [1536, 16, 512], P(('ctx', 'fsdp'))
Inputs may be any that keep to these rules, and one draw needn't show every extreme that they name: `segments`: segment numbers of a sequence start at 0 and never fall; documents hold 200 to 2000 tokens, the last one before padding possibly fewer; padding tokens carry 7 - 1; in each aligned run of 2 sequences one, drawn from the seed, is a single document. `valid`: each sequence is 1 on a leading run and 0 after it; the single-document sequences have no 0, every other one ends in at least one 0. `expert_ids`: the 8 experts of a token are different. `slot_order`: each aligned block of 128 tokens of a sequence holds a permutation of 0 to 127.
All inputs are finite; a program needn't handle non-finite values.
Results may differ from a plain program's by a relative error of at most 0.018.
Values may be sent and summed in bfloat16 or wider, within the bound.
A program may use at most 640 MiB of HBM per device.

v0:
```python
import jax
import jax.numpy as jnp
from jax import lax
from jax.sharding import PartitionSpec as P

D = 1536
QUERY_HEADS = 24
KEY_VALUE_HEADS = 8
HEAD_SIZE = 64
FF = 512
EXPERTS = 16
CAP = 80


EPS = 1e-05
ROPE_BASE = 10000.0
MASKED = -1e30


def rope_tables(positions):
    half_dim = HEAD_SIZE // 2
    frequency = ROPE_BASE ** (-jnp.arange(half_dim, dtype=jnp.float32) * 2.0 / HEAD_SIZE)
    angle = positions.astype(jnp.float32)[:, None] * frequency[None, :]
    angle = jnp.concatenate([angle, angle], axis=1)
    return (jnp.cos(angle), jnp.sin(angle))


def apply_rotation(field, cosine, sine_table):
    half_dim = field.shape[-1] // 2
    turned = jnp.concatenate([-field[..., half_dim:], field[..., :half_dim]], axis=-1)
    return field * cosine + turned * sine_table


def on_device(
    tokens,
    segments,
    valid,
    expert_ids,
    slot_order,
    cotangent,
    norm1_gain,
    w_query,
    key_weight,
    value_weight,
    w_output,
    norm2_gain,
    w_router,
    w_gate,
    w_up,
    w_down,
):
    sequence_count, group_length, _ = tokens.shape
    queries_per_group = QUERY_HEADS // KEY_VALUE_HEADS
    full_len = segments.shape[1]
    offset = lax.axis_index("ctx") * group_length
    positions = offset + jnp.arange(group_length, dtype=jnp.int32)
    cosine, sine_table = rope_tables(positions)
    cosine_heads = cosine[:, None, :]
    sine_heads = sine_table[:, None, :]
    scale = HEAD_SIZE ** (-0.5)
    attn_set = (
        lax.all_gather(norm1_gain, "fsdp", axis=0, tiled=True),
        lax.all_gather(w_query, "fsdp", axis=0, tiled=True),
        lax.all_gather(key_weight, "fsdp", axis=0, tiled=True),
        lax.all_gather(value_weight, "fsdp", axis=0, tiled=True),
        lax.all_gather(w_output, "fsdp", axis=0, tiled=True),
        lax.all_gather(norm2_gain, "fsdp", axis=0, tiled=True),
        lax.all_gather(w_router, "fsdp", axis=0, tiled=True),
    )
    gain_first, full_query, full_key, full_value, full_output, gain_second, full_router = attn_set
    inputs_f = tokens.astype(jnp.float32)
    scale_one = lax.rsqrt(jnp.mean(inputs_f * inputs_f, axis=-1, keepdims=True) + EPS)
    normalized_input = (inputs_f * scale_one * gain_first).astype(jnp.bfloat16)
    query_pre = jnp.dot(normalized_input, full_query, preferred_element_type=jnp.float32)
    key_unrotated = jnp.dot(normalized_input, full_key, preferred_element_type=jnp.float32)
    value_pre = jnp.dot(normalized_input, full_value, preferred_element_type=jnp.float32)
    query_rot = apply_rotation(
        query_pre.reshape(sequence_count, group_length, QUERY_HEADS, HEAD_SIZE),
        cosine_heads,
        sine_heads,
    )
    query_rot = query_rot.astype(jnp.bfloat16).reshape(
        sequence_count, group_length, QUERY_HEADS * HEAD_SIZE
    )
    key_rotated = apply_rotation(
        key_unrotated.reshape(sequence_count, group_length, KEY_VALUE_HEADS, HEAD_SIZE),
        cosine_heads,
        sine_heads,
    )
    key_rotated = key_rotated.astype(jnp.bfloat16).reshape(
        sequence_count, group_length, KEY_VALUE_HEADS * HEAD_SIZE
    )
    value_low = value_pre.astype(jnp.bfloat16)
    key_all, value_all = (
        lax.all_gather(key_rotated, "ctx", axis=1, tiled=True),
        lax.all_gather(value_low, "ctx", axis=1, tiled=True),
    )
    seg_local = lax.dynamic_slice_in_dim(segments, offset, group_length, 1)
    key_pos = jnp.arange(full_len, dtype=jnp.int32)
    allowed_mask = (seg_local[:, :, None] == segments[:, None, :]) & (
        key_pos[None, None, :] <= positions[None, :, None]
    )
    allowed_mask = allowed_mask & (
        (valid[:, None, :] > 0) | (key_pos[None, None, :] == positions[None, :, None])
    )
    allowed_mask = allowed_mask[:, None]

    def head_inputs(head_index):
        query_head = lax.dynamic_slice_in_dim(
            query_rot, head_index * queries_per_group * HEAD_SIZE, queries_per_group * HEAD_SIZE, 2
        )
        query_head = query_head.reshape(sequence_count, group_length, queries_per_group, HEAD_SIZE)
        key_head = lax.dynamic_slice_in_dim(key_all, head_index * HEAD_SIZE, HEAD_SIZE, 2)
        value_head = lax.dynamic_slice_in_dim(value_all, head_index * HEAD_SIZE, HEAD_SIZE, 2)
        return (query_head, key_head, value_head)

    def head_scores(query_head, key_head):
        raw_scores = (
            jnp.einsum("sgrd,skd->srgk", query_head, key_head, preferred_element_type=jnp.float32)
            * scale
        )
        return jnp.where(allowed_mask, raw_scores, MASKED)

    def head_forward_pass(head_index):
        query_head, key_head, value_head = head_inputs(head_index)
        scores = head_scores(query_head, key_head)
        largest = jnp.max(scores, axis=-1, keepdims=True)
        exp_scores = jnp.exp(scores - largest)
        total = jnp.sum(exp_scores, axis=-1, keepdims=True)
        weights_soft = (exp_scores / total).astype(jnp.bfloat16)
        head_output = jnp.einsum(
            "srgk,skd->sgrd", weights_soft, value_head, preferred_element_type=jnp.float32
        )
        return (head_output.astype(jnp.bfloat16), largest[..., 0] + jnp.log(total[..., 0]))

    head_outputs, log_sum_totals = lax.map(
        head_forward_pass, jnp.arange(KEY_VALUE_HEADS, dtype=jnp.int32)
    )
    attn_out = head_outputs.transpose(1, 2, 0, 3, 4).reshape(
        sequence_count, group_length, QUERY_HEADS * HEAD_SIZE
    )
    attn_proj = jnp.einsum("sgq,dq->sgd", attn_out, full_output, preferred_element_type=jnp.float32)
    residual = inputs_f + attn_proj
    scale_two = lax.rsqrt(jnp.mean(residual * residual, axis=-1, keepdims=True) + EPS)
    normed_mid = (residual * scale_two * gain_second).astype(jnp.bfloat16)
    logits = jnp.dot(normed_mid, full_router, preferred_element_type=jnp.float32)
    onehot = (expert_ids[..., None] == jnp.arange(EXPERTS, dtype=jnp.int32)).astype(jnp.int32)
    picked = jnp.sum(onehot, axis=2)
    before = (slot_order[:, None, :] < slot_order[:, :, None]).astype(jnp.int32)
    counts = jnp.matmul(before, picked)
    place_in = jnp.sum(onehot * counts[:, :, None, :], axis=-1)
    is_kept = place_in < CAP
    target = expert_ids * CAP + place_in
    slot_table = (target[..., None] == jnp.arange(EXPERTS * CAP, dtype=jnp.int32)) & is_kept[
        ..., None
    ]
    slot_table = slot_table.astype(jnp.float32)
    onehot_f = onehot.astype(jnp.float32)
    chosen = jnp.sum(onehot_f * logits[:, :, None, :], axis=-1)
    gate_weights = jax.nn.softmax(chosen, axis=-1)
    dispatch = jnp.sum(slot_table, axis=2).astype(jnp.bfloat16)
    combine = jnp.sum(gate_weights[..., None] * slot_table, axis=2).astype(jnp.bfloat16)
    expert_in = jnp.einsum("sgx,sgd->sxd", dispatch, normed_mid, preferred_element_type=jnp.float32)
    expert_in = expert_in.astype(jnp.bfloat16).reshape(sequence_count, EXPERTS, CAP, D)
    expert_set = (
        lax.all_gather(w_gate, "fsdp", axis=0, tiled=True),
        lax.all_gather(w_up, "fsdp", axis=0, tiled=True),
        lax.all_gather(w_down, "fsdp", axis=0, tiled=True),
    )
    full_gate, full_up, full_down = expert_set
    gate_pre = jnp.einsum(
        "secd,def->secf", expert_in, full_gate, preferred_element_type=jnp.float32
    )
    up_pre = jnp.einsum("secd,def->secf", expert_in, full_up, preferred_element_type=jnp.float32)
    sigmoid_gate = jax.nn.sigmoid(gate_pre)
    activated = gate_pre * sigmoid_gate
    hidden = (activated * up_pre).astype(jnp.bfloat16)
    expert_out = jnp.einsum("secf,def->secd", hidden, full_down, preferred_element_type=jnp.float32)
    expert_out = expert_out.astype(jnp.bfloat16).reshape(sequence_count, EXPERTS * CAP, D)
    expert_mix = jnp.einsum("sgx,sxd->sgd", combine, expert_out, preferred_element_type=jnp.float32)
    layer_out = (residual + expert_mix).astype(jnp.bfloat16)
    back_attn = (
        lax.all_gather(norm1_gain, "fsdp", axis=0, tiled=True),
        lax.all_gather(w_query, "fsdp", axis=0, tiled=True),
        lax.all_gather(key_weight, "fsdp", axis=0, tiled=True),
        lax.all_gather(value_weight, "fsdp", axis=0, tiled=True),
        lax.all_gather(w_output, "fsdp", axis=0, tiled=True),
        lax.all_gather(norm2_gain, "fsdp", axis=0, tiled=True),
        lax.all_gather(w_router, "fsdp", axis=0, tiled=True),
    )
    back_expert = (
        lax.all_gather(w_gate, "fsdp", axis=0, tiled=True),
        lax.all_gather(w_up, "fsdp", axis=0, tiled=True),
        lax.all_gather(w_down, "fsdp", axis=0, tiled=True),
    )
    gain_first, full_query, full_key, full_value, full_output, gain_second, full_router = back_attn
    full_gate, full_up, full_down = back_expert
    grad_f = cotangent.astype(jnp.float32)
    grad_expert_out = jnp.einsum(
        "sgx,sgd->sxd", combine, cotangent, preferred_element_type=jnp.float32
    )
    grad_expert_out = grad_expert_out.astype(jnp.bfloat16).reshape(sequence_count, EXPERTS, CAP, D)
    grad_combine = jnp.einsum(
        "sgd,sxd->sgx", cotangent, expert_out, preferred_element_type=jnp.float32
    )
    grad_gates = jnp.sum(slot_table * grad_combine[:, :, None, :], axis=-1)
    grad_hidden = jnp.einsum(
        "secd,def->secf", grad_expert_out, full_down, preferred_element_type=jnp.float32
    )
    silu_slope = sigmoid_gate * (1.0 + gate_pre * (1.0 - sigmoid_gate))
    grad_gate_pre = (grad_hidden * up_pre * silu_slope).astype(jnp.bfloat16)
    grad_up_pre = (grad_hidden * activated).astype(jnp.bfloat16)
    grad_expert_in = jnp.einsum(
        "secf,def->secd", grad_gate_pre, full_gate, preferred_element_type=jnp.float32
    )
    grad_expert_in = grad_expert_in + jnp.einsum(
        "secf,def->secd", grad_up_pre, full_up, preferred_element_type=jnp.float32
    )
    grad_expert_in = grad_expert_in.astype(jnp.bfloat16).reshape(sequence_count, EXPERTS * CAP, D)
    grad_mid = jnp.einsum(
        "sgx,sxd->sgd", dispatch, grad_expert_in, preferred_element_type=jnp.float32
    )
    grad_chosen = gate_weights * (
        grad_gates - jnp.sum(gate_weights * grad_gates, axis=-1, keepdims=True)
    )
    grad_logits = jnp.sum(onehot_f * grad_chosen[..., None], axis=2).astype(jnp.bfloat16)
    grad_mid = grad_mid + jnp.einsum(
        "sge,de->sgd", grad_logits, full_router, preferred_element_type=jnp.float32
    )
    grad_router = jnp.einsum(
        "sgd,sge->de", normed_mid, grad_logits, preferred_element_type=jnp.float32
    )
    gate_part = jnp.einsum(
        "secd,secf->def", expert_in, grad_gate_pre, preferred_element_type=jnp.float32
    )
    up_part = jnp.einsum(
        "secd,secf->def", expert_in, grad_up_pre, preferred_element_type=jnp.float32
    )
    down_part = jnp.einsum(
        "secd,secf->def", grad_expert_out, hidden, preferred_element_type=jnp.float32
    )
    expert_grads = lax.psum_scatter(
        jnp.concatenate([gate_part, up_part, down_part], axis=2),
        ("ctx", "fsdp"),
        scatter_dimension=0,
        tiled=True,
    )
    grad_gate_w = expert_grads[:, :, :FF]
    grad_up_w = expert_grads[:, :, FF : 2 * FF]
    grad_down_w = expert_grads[:, :, 2 * FF :]
    weighted_two = gain_second * grad_mid
    grad_gain_second = jnp.sum(grad_mid * residual * scale_two, axis=(0, 1))
    cube_two = scale_two * scale_two * scale_two
    grad_resid = (
        grad_f
        + scale_two * weighted_two
        - residual * cube_two * jnp.mean(weighted_two * residual, axis=-1, keepdims=True)
    )
    grad_resid_low = grad_resid.astype(jnp.bfloat16)
    grad_attn = jnp.einsum(
        "sgd,dq->sgq", grad_resid_low, full_output, preferred_element_type=jnp.float32
    )
    grad_attn = grad_attn.astype(jnp.bfloat16)
    grad_output_w = jnp.einsum(
        "sgd,sgq->dq", grad_resid_low, attn_out, preferred_element_type=jnp.float32
    )

    def head_backward_pass(item_rows):
        head_index, log_total = item_rows
        query_head, key_head, value_head = head_inputs(head_index)
        grad_head = lax.dynamic_slice_in_dim(
            grad_attn, head_index * queries_per_group * HEAD_SIZE, queries_per_group * HEAD_SIZE, 2
        )
        grad_head = grad_head.reshape(sequence_count, group_length, queries_per_group, HEAD_SIZE)
        scores = head_scores(query_head, key_head)
        probs_full = jnp.exp(scores - log_total[..., None])
        grad_probs = jnp.einsum(
            "sgrd,skd->srgk", grad_head, value_head, preferred_element_type=jnp.float32
        )
        grad_value_head = jnp.einsum(
            "srgk,sgrd->skd",
            probs_full.astype(jnp.bfloat16),
            grad_head,
            preferred_element_type=jnp.float32,
        )
        inner = jnp.sum(grad_probs * probs_full, axis=-1, keepdims=True)
        grad_scores = jnp.where(allowed_mask, probs_full * (grad_probs - inner), 0.0).astype(
            jnp.bfloat16
        )
        grad_query_head = (
            jnp.einsum("srgk,skd->sgrd", grad_scores, key_head, preferred_element_type=jnp.float32)
            * scale
        )
        grad_key_head = (
            jnp.einsum(
                "srgk,sgrd->skd", grad_scores, query_head, preferred_element_type=jnp.float32
            )
            * scale
        )
        return (grad_query_head, grad_key_head, grad_value_head)

    grad_queries, grad_keys_all, grad_values_all = lax.map(
        head_backward_pass, (jnp.arange(KEY_VALUE_HEADS, dtype=jnp.int32), log_sum_totals)
    )
    grad_key_local, grad_value_device = (
        lax.psum_scatter(
            grad_keys_all.astype(jnp.bfloat16), "ctx", scatter_dimension=2, tiled=True
        ).astype(jnp.float32),
        lax.psum_scatter(
            grad_values_all.astype(jnp.bfloat16), "ctx", scatter_dimension=2, tiled=True
        ).astype(jnp.float32),
    )
    grad_query_rot = grad_queries.transpose(1, 2, 0, 3, 4).reshape(
        sequence_count, group_length, QUERY_HEADS, HEAD_SIZE
    )
    grad_query_low = apply_rotation(grad_query_rot, cosine_heads, -sine_heads).astype(jnp.bfloat16)
    grad_query_low = grad_query_low.reshape(sequence_count, group_length, QUERY_HEADS * HEAD_SIZE)
    grad_key_reduced = apply_rotation(
        grad_key_local.transpose(1, 2, 0, 3), cosine_heads, -sine_heads
    ).astype(jnp.bfloat16)
    grad_key_reduced = grad_key_reduced.reshape(
        sequence_count, group_length, KEY_VALUE_HEADS * HEAD_SIZE
    )
    grad_value_reduced = grad_value_device.transpose(1, 2, 0, 3).reshape(
        sequence_count, group_length, KEY_VALUE_HEADS * HEAD_SIZE
    )
    grad_value_reduced = grad_value_reduced.astype(jnp.bfloat16)
    grad_in = jnp.einsum(
        "sgq,dq->sgd", grad_query_low, full_query, preferred_element_type=jnp.float32
    )
    grad_in = grad_in + jnp.einsum(
        "sgq,dq->sgd", grad_key_reduced, full_key, preferred_element_type=jnp.float32
    )
    grad_in = grad_in + jnp.einsum(
        "sgq,dq->sgd", grad_value_reduced, full_value, preferred_element_type=jnp.float32
    )
    grad_query_w = jnp.einsum(
        "sgd,sgq->dq", normalized_input, grad_query_low, preferred_element_type=jnp.float32
    )
    grad_key_w = jnp.einsum(
        "sgd,sgq->dq", normalized_input, grad_key_reduced, preferred_element_type=jnp.float32
    )
    grad_value_w = jnp.einsum(
        "sgd,sgq->dq", normalized_input, grad_value_reduced, preferred_element_type=jnp.float32
    )
    weighted_one = gain_first * grad_in
    grad_gain_first = jnp.sum(grad_in * inputs_f * scale_one, axis=(0, 1))
    cube_one = scale_one * scale_one * scale_one
    grad_tokens = (
        grad_resid
        + scale_one * weighted_one
        - inputs_f * cube_one * jnp.mean(weighted_one * inputs_f, axis=-1, keepdims=True)
    )
    input_grad = grad_tokens.astype(jnp.bfloat16)
    summed = (
        lax.psum_scatter(grad_gain_first, ("ctx", "fsdp"), scatter_dimension=0, tiled=True),
        lax.psum_scatter(grad_query_w, ("ctx", "fsdp"), scatter_dimension=0, tiled=True),
        lax.psum_scatter(grad_key_w, ("ctx", "fsdp"), scatter_dimension=0, tiled=True),
        lax.psum_scatter(grad_value_w, ("ctx", "fsdp"), scatter_dimension=0, tiled=True),
        lax.psum_scatter(grad_output_w, ("ctx", "fsdp"), scatter_dimension=0, tiled=True),
        lax.psum_scatter(grad_gain_second, ("ctx", "fsdp"), scatter_dimension=0, tiled=True),
        lax.psum_scatter(grad_router, ("ctx", "fsdp"), scatter_dimension=0, tiled=True),
    )
    return (
        layer_out,
        input_grad,
        summed[0],
        summed[1],
        summed[2],
        summed[3],
        summed[4],
        summed[5],
        summed[6],
        grad_gate_w,
        grad_up_w,
        grad_down_w,
    )


def solution(mesh):
    placed = (
        P("fsdp", "ctx", None),
        P("fsdp", None),
        P("fsdp", None),
        P("fsdp", "ctx", None),
        P("fsdp", "ctx"),
        P("fsdp", "ctx", None),
        P("fsdp"),
        P("fsdp", None),
        P("fsdp", None),
        P("fsdp", None),
        P("fsdp", None),
        P("fsdp"),
        P("fsdp", None),
        P("fsdp", None, None),
        P("fsdp", None, None),
        P("fsdp", None, None),
    )
    return jax.shard_map(
        on_device,
        mesh=mesh,
        in_specs=placed,
        out_specs=(
            P("fsdp", "ctx", None),
            P("fsdp", "ctx", None),
            P(("ctx", "fsdp")),
            P(("ctx", "fsdp"), None),
            P(("ctx", "fsdp"), None),
            P(("ctx", "fsdp"), None),
            P(("ctx", "fsdp"), None),
            P(("ctx", "fsdp")),
            P(("ctx", "fsdp"), None),
            P(("ctx", "fsdp"), None, None),
            P(("ctx", "fsdp"), None, None),
            P(("ctx", "fsdp"), None, None),
        ),
        check_vma=False,
    )
```

profile of v0, /device:TPU:0, one launch (start us, length us, event | category | flops | bytes accessed | tf_op | source)
XLA Modules:
  0.0 3098.4 jit_solution(10667225785497842288)
XLA Ops:
  17.5 14.6 all-gather.12.cloned.1.call-done
  36.8 16.4 all-gather.16.cloned.1.call-done
  57.8 9.0 copy.204
  66.9 9.0 copy.206
  75.9 10.6 all-gather.28.cloned.1.call-start
  86.4 9.1 copy.208
  119.1 36.6 %all-gather.18.cloned.1.call-done = bf16[2,1024,512]{2,1,0:T(8,128)(2,1)} async-done(((bf16[2,128,512]{2,1,0:T(8,128)(2,1)}), bf16[2,1024,512]{2,1,0:T(8,128)(2,1)}) %all-gather.18.cloned.1.call-update) | async-done | bytes 2097168 | tf_op jit(solution)/shard_map/all_gather | solution.py:95
  159.7 33.4 %all-gather.20.cloned.1.call-done = bf16[1536,1536]{1,0:T(8,128)(2,1)} async-done(((bf16[384,1536]{1,0:T(8,128)(2,1)}), bf16[1536,1536]{1,0:T(8,128)(2,1)}) %all-gather.20.cloned.1.call-update) | async-done | bytes 4718608 | tf_op jit(solution)/shard_map/all_gather | solution.py:63
  212.8 73.6 %while.32 = (s32[]{:T(128)}, bf16[8,2,128,3,64]{2,4,3,0,1:T(8,128)(2,1)}, f32[8,2,3,128]{3,2,1,0:T(4,128)}, s32[8]{0:T(128)S(1)}, bf16[2,1024,512]{1,2,0:T(8,128...) while((s32[]{:T(128)}, ...), condition=%wide.region_4.5_spmd.clone, body=%wide.region_1.4_spmd.clone.sunk | while | flops 211860736 | bytes 11702569 | solution.py:136
  298.3 89.8 %all-gather.24.cloned.1.call-done = bf16[1536,16,512]{2,0,1:T(8,128)(2,1)} async-done(((bf16[384,16,512]{2,0,1:T(8,128)(2,1)}), bf16[1536,16,512]{2,0,1:T(8,128)(2,1)}) %all-gather.24.cloned.1.call-update) | async-done | bytes 25165840 | tf_op jit(solution)/shard_map/all_gather | solution.py:166
  388.1 20.6 fusion.62
  408.7 135.5 %all-gather.26.cloned.1.call-done = bf16[1536,16,512]{2,0,1:T(8,128)(2,1)} async-done(((bf16[384,16,512]{2,0,1:T(8,128)(2,1)}), bf16[1536,16,512]{2,0,1:T(8,128)(2,1)}) %all-gather.26.cloned.1.call-update) | async-done | bytes 25165840 | tf_op jit(solution)/shard_map/all_gather | solution.py:167
  544.2 23.0 fusion.79
  567.2 133.1 %all-gather.28.cloned.1.call-done = bf16[1536,16,512]{2,0,1:T(8,128)(2,1)} async-done(((bf16[384,16,512]{2,0,1:T(8,128)(2,1)}), bf16[1536,16,512]{2,0,1:T(8,128)(2,1)}) %all-gather.28.cloned.1.call-update) | async-done | bytes 25165840 | tf_op jit(solution)/shard_map/all_gather | solution.py:168
  700.3 17.0 convert_bitcast_fusion
  731.4 7.4 select_reduce_fusion
  745.4 21.7 fusion.77
  767.1 19.6 fusion.56
  786.7 20.3 fusion.69
  820.9 164.1 %while.33 = (s32[]{:T(128)}, f32[8,2,128,3,64]{2,4,3,0,1:T(8,128)}, bf16[8,2,1024,64]{2,3,0,1:T(8,128)(2,1)}, bf16[8,2,1024,64]{2,3,0,1:T(8,128)(2,1)}, s32[8]{0...) while((s32[]{:T(128)}, f32[8,2,128,3,64]{2,4,3,0,1:T(8,128)}, ...), condition=%wide.region_19.20_spmd.clone, body=%wide.region_17.19_spmd.clone.sunk | while | flops 515558912 | bytes 52384132 | solution.py:302
  1004.4 6.5 reshape.365
  1013.5 22.2 convolution_bitcast_fusion
  1035.6 21.1 convolution_bitcast_fusion.2
  1056.7 21.8 convolution_bitcast_fusion.1
  1078.6 101.0 %pad_maximum_fusion = f32[1536,16,1536]{0,2,1:T(8,128)} fusion(f32[1536,16,512]{0,2,1:T(8,128)} %convolution_bitcast_fusion, f32[1536,16,512]{0,2,1:T(8,128)} %convolution_bitcast_fusion.1, f32[1536,16,512]{0,2,1:T(8,128)} %convolution_bitcast_fusion.2), kind=kLoop, calls=%fused_computation.63 | loop fusion | flops 75497472 | bytes 301989888 | tf_op jit(solution)/shard_map/concatenate | solution.py:243
  1179.6 149.5 %copy.238 = f32[1536,16,1536]{2,1,0:T(8,128)} copy(f32[1536,16,1536]{0,2,1:T(8,128)} %pad_maximum_fusion) | data formatting | bytes 301989888 | tf_op jit(solution)/shard_map/concatenate | solution.py:243
  1387.9 39.6 %all-reduce.2 = (f32[1536]{0:T(1024)S(1)}, f32[1536]{0:T(1024)S(1)}) all-reduce(f32[1536]{0:T(1024)S(1)} %get-tuple-element.460, f32[1536]{0:T(1024)S(1)} %copy-done.44), channel_id=4, replica_groups=mesh['ctx'=8,'fsdp'=4] {'ctx','fsdp'}, use_global_device_ids=true, to_apply=%region_24.25.clone | all-reduce | flops 3072 | bytes 24576
  1431.6 1162.4 %reduce-scatter.23.cloned.1.call-done = f32[48,16,1536]{2,1,0:T(8,128)} async-done(((f32[1536,16,1536]{2,1,0:T(8,128)}), f32[48,16,1536]{2,1,0:T(8,128)}) %reduce-scatter.23.cloned.1.call-update) | async-done | bytes 4718608 | tf_op jit(solution)/shard_map/reduce_scatter | solution.py:242
  2598.9 102.7 %reduce-scatter.19.cloned.1.call-done = f32[48,512]{1,0:T(8,128)} async-done(((f32[1536,512]{1,0:T(8,128)}), f32[48,512]{1,0:T(8,128)}) %reduce-scatter.19.cloned.1.call-update) | async-done | bytes 98320 | tf_op jit(solution)/shard_map/reduce_scatter | solution.py:359
  2701.5 107.3 %reduce-scatter.17.cloned.1.call-done = f32[48,512]{1,0:T(8,128)} async-done(((f32[1536,512]{1,0:T(8,128)}), f32[48,512]{1,0:T(8,128)}) %reduce-scatter.17.cloned.1.call-update) | async-done | bytes 98320 | tf_op jit(solution)/shard_map/reduce_scatter | solution.py:358
  2808.8 142.0 %reduce-scatter.21.cloned.1.call-done = f32[48,1536]{1,0:T(8,128)} async-done(((f32[1536,1536]{1,0:T(8,128)}), f32[48,1536]{1,0:T(8,128)}) %reduce-scatter.21.cloned.1.call-update) | async-done | bytes 294928 | tf_op jit(solution)/shard_map/reduce_scatter | solution.py:360
  2950.8 140.9 %reduce-scatter.15.cloned.1.call-done = f32[48,1536]{1,0:T(8,128)} async-done(((f32[1536,1536]{1,0:T(8,128)}), f32[48,1536]{1,0:T(8,128)}) %reduce-scatter.15.cloned.1.call-update) | async-done | bytes 294928 | tf_op jit(solution)/shard_map/reduce_scatter | solution.py:357
  (413 shorter events, 418.6 us)
Async XLA Ops:
  7.2 24.9 all-gather.12.cloned.1.call-start
  7.9 45.3 %all-gather.16.cloned.1.call-start = ((), (), s32[]{:S(2)}) async-start(), calls=%async_computation.10 | async-start | bytes 1966080 | tf_op jit(solution)/shard_map/all_gather | solution.py:64
  8.7 106.3 %all-gather.14.cloned.1.call-start = ((), (), s32[]{:S(2)}) async-start(), calls=%async_computation.9 | async-start | bytes 2359296 | tf_op jit(solution)/shard_map/all_gather | solution.py:96
  15.5 177.6 %copy-start.30 = (f32[1536]{0:T(1024)}, f32[1536]{0:T(1024)S(1)}, u32[]{:S(2)}) copy-start(f32[1536]{0:T(1024)S(1)} %reshape.338) | copy-start | bytes 18436
  17.5 175.6 %copy-start.42 = (f32[2,128]{1,0:T(2,128)}, f32[2,128]{1,0:T(2,128)S(1)}, u32[]{:S(2)}) copy-start(f32[2,128]{1,0:T(2,128)S(1)} %get-tuple-element.541) | copy-start | bytes 3076
  32.0 21.2 copy-start.4
  35.1 120.6 %all-gather.18.cloned.1.call-start = ((), (), s32[]{:S(2)}) async-start(), calls=%async_computation.11 | async-start | bytes 2359296 | tf_op jit(solution)/shard_map/all_gather | solution.py:95
  36.5 67.5 %copy-start.28 = (f32[128,64]{0,1:T(8,128)}, f32[128,64]{0,1:T(8,128)S(1)}, u32[]{:S(2)}) copy-start(f32[128,64]{0,1:T(8,128)S(1)} %get-tuple-element.539) | copy-start | bytes 98308
  56.6 136.5 %all-gather.20.cloned.1.call-start = ((), (), s32[]{:S(2)}) async-start(), calls=%async_computation.12 | async-start | bytes 5898240 | tf_op jit(solution)/shard_map/all_gather | solution.py:63
  57.2 229.1 %all-gather.22.cloned.1.call-start = ((), (), s32[]{:S(2)}) async-start(), calls=%async_computation.13 | async-start | bytes 5898240 | tf_op jit(solution)/shard_map/all_gather | solution.py:66
  57.8 330.3 %all-gather.24.cloned.1.call-start = ((), (), s32[]{:S(2)}) async-start(), calls=%async_computation.14 | async-start | bytes 31457280 | tf_op jit(solution)/shard_map/all_gather | solution.py:166
  66.8 477.4 %all-gather.26.cloned.1.call-start = ((), (), s32[]{:S(2)}) async-start(), calls=%async_computation.15 | async-start | bytes 31457280 | tf_op jit(solution)/shard_map/all_gather | solution.py:167
  75.9 624.5 %all-gather.28.cloned.1.call-start = ((), (), s32[]{:S(2)}) async-start(), calls=%async_computation.16 | async-start | bytes 31457280 | tf_op jit(solution)/shard_map/all_gather | solution.py:168
  95.5 8.8 copy-start.47
  95.5 14.0 copy-start.26
  95.6 14.0 copy-start.48
  95.6 1233.6 %reduce-scatter.27.cloned.1.call-start = ((), (), s32[]{:S(2)}) async-start(), calls=%async_computation.23 | async-start | bytes 2359296
  104.3 102.9 %copy-start.16 = (f32[128,1536]{1,0:T(8,128)}, f32[128,1536]{1,0:T(8,128)S(1)}, u32[]{:S(2)}) copy-start(f32[128,1536]{1,0:T(8,128)S(1)} %copy.191) | copy-start | bytes 2359300
  114.9 178.1 %copy-start.8 = (bf16[2,128,1280]{2,1,0:T(8,128)(2,1)}, bf16[2,128,1280]{2,1,0:T(8,128)(2,1)S(1)}, u32[]{:S(2)}) copy-start(bf16[2,128,1280]{2,1,0:T(8,128)(2,1)S(1)} %convert_reduce_fusion) | copy-start | bytes 1966084
  290.5 523.9 %copy-start.2 = (f32[2,128,1536]{2,1,0:T(8,128)}, f32[2,128,1536]{2,1,0:T(8,128)S(1)}, u32[]{:S(2)}) copy-start(f32[2,128,1536]{2,1,0:T(8,128)S(1)} %get-tuple-element.547) | copy-start | bytes 4718596
  728.5 11.3 copy-start.41
  728.5 11.4 copy-start.37
  728.5 11.4 copy-start.14
  997.6 336.2 %reduce-scatter.25.cloned.1.call-start = ((), (), s32[]{:S(2)}) async-start(), calls=%async_computation.22 | async-start | bytes 2359296
  1011.0 370.2 %reduce-scatter.29.cloned.1.call-start = ((), (), s32[]{:S(2)}) async-start(), calls=%async_computation.24 | async-start | bytes 811008
  1013.5 22.2 copy-start.11
  1078.6 1515.5 %reduce-scatter.23.cloned.1.call-start = ((), (), s32[]{:S(2)}) async-start(), calls=%async_computation.21 | async-start | bytes 155713536 | tf_op jit(solution)/shard_map/reduce_scatter | solution.py:242
  1329.2 1372.4 %reduce-scatter.19.cloned.1.call-start = ((), (), s32[]{:S(2)}) async-start(), calls=%async_computation.19 | async-start | bytes 3244032 | tf_op jit(solution)/shard_map/reduce_scatter | solution.py:359
  1333.6 1475.2 %reduce-scatter.17.cloned.1.call-start = ((), (), s32[]{:S(2)}) async-start(), calls=%async_computation.18 | async-start | bytes 3244032 | tf_op jit(solution)/shard_map/reduce_scatter | solution.py:358
  1338.3 1612.4 %reduce-scatter.21.cloned.1.call-start = ((), (), s32[]{:S(2)}) async-start(), calls=%async_computation.20 | async-start | bytes 9732096 | tf_op jit(solution)/shard_map/reduce_scatter | solution.py:360
  1346.5 1745.2 %reduce-scatter.15.cloned.1.call-start = ((), (), s32[]{:S(2)}) async-start(), calls=%async_computation.17 | async-start | bytes 9732096 | tf_op jit(solution)/shard_map/reduce_scatter | solution.py:357
  1385.9 42.8 %copy-start.49 = (f32[2,128]{1,0:T(2,128)S(1)}, f32[2,128]{1,0:T(2,128)}, u32[]{:S(2)}) copy-start(f32[2,128]{1,0:T(2,128)} %get-tuple-element.540) | copy-start | bytes 3076
  (52 other events, 131.7 us)
Sparse Core Ops, SparseCore 0:
  9.6 22.4 all-gather.11
  33.6 19.5 all-gather.15
  56.0 49.2 all-gather.13
  107.9 47.7 all-gather.17
  157.1 35.9 all-gather.19
  194.5 37.4 all-gather.21
  233.6 154.4 all-gather.23
  389.7 154.4 all-gather.25
  545.8 154.4 all-gather.27
  997.8 67.5 reduce-scatter.26
  1068.9 66.8 reduce-scatter.24
  1140.8 94.5 reduce-scatter.28
  1329.3 1264.7 reduce-scatter.22
  2600.8 100.6 reduce-scatter.18
  2708.3 100.4 reduce-scatter.16
  2816.1 134.5 reduce-scatter.20
  2957.1 134.5 reduce-scatter.14
where the time goes:
time: 3110 us; the launch traced here: 3100 us
  waiting for transfers between devices  2120 us (68%)
  matrix products  404 us (13%)
  local copies, waits for them, and re-layouts  314 us (10%)
  other arithmetic  159 us (5%)
  blocking collectives  56 us (2%)
    reduce_scatter x1, waiting for transfers between devices, on_device(): lax.psum_scatter(jnp.concatenate([gate_part, up_part, down_part], axis=2)...  1160 us
    concatenate x1, local copies, waits for them, and re-layouts, on_device(): jnp.concatenate([gate_part, up_part, down_part], axis=2)  150 us
    reduce_scatter x1, waiting for transfers between devices, on_device(): lax.psum_scatter(grad_output_w, ('ctx', 'fsdp'), scatter_dimension=0, til...  142 us
    reduce_scatter x1, waiting for transfers between devices, on_device(): lax.psum_scatter(grad_query_w, ('ctx', 'fsdp'), scatter_dimension=0, tile...  141 us
    all_gather x1, waiting for transfers between devices, on_device(): lax.all_gather(w_up, 'fsdp', axis=0, tiled=True)  135 us
    all_gather x1, waiting for transfers between devices, on_device(): lax.all_gather(w_down, 'fsdp', axis=0, tiled=True)  133 us
    reduce_scatter x1, waiting for transfers between devices, on_device(): lax.psum_scatter(grad_key_w, ('ctx', 'fsdp'), scatter_dimension=0, tiled=...  107 us
    reduce_scatter x1, waiting for transfers between devices, on_device(): lax.psum_scatter(grad_value_w, ('ctx', 'fsdp'), scatter_dimension=0, tile...  103 us
  transfers between devices with their start and end apart: 17, of which 12 were waited for; matrix products, arithmetic and copies ran while one was open for 19% of the time, Pallas kernels for 0%

commit v1 on v0

v1 whole, which is shorter than its diff:
```python
import functools

import jax
import jax.numpy as jnp
from jax import lax
from jax.experimental import pallas as pl
from jax.experimental.pallas import tpu as pltpu
from jax.sharding import PartitionSpec as P

D = 1536
QUERY_HEADS = 24
KEY_VALUE_HEADS = 8
REP = QUERY_HEADS // KEY_VALUE_HEADS
HEAD_SIZE = 64
FF = 512
EXPERTS = 16
CAP = 80
RANKS = 8
OWN = EXPERTS // RANKS
SEQS = 2
BLOCK = 128
KEYS = 256

EPS = 1e-05
ROPE_BASE = 10000.0
MASKED = -1e30
SCALE = HEAD_SIZE ** (-0.5)
MESH = pl.DeviceIdType.MESH
BF16 = jnp.bfloat16
F32 = jnp.float32


def flip(index, constant):
    result, bit = index, 1
    while bit <= constant:
        if constant & bit:
            result = result + bit - 2 * bit * lax.rem(lax.div(index, bit), 2)
        bit *= 2
    return result


def lasting(microseconds):
    return pl.CostEstimate(flops=0, bytes_accessed=int(microseconds * 3.3e6), transcendentals=0)


def exchange(cid, name, routes, operands, outs, microseconds=30):
    remote = [r for r in routes if r[0] or r[1]]
    local = [r for r in routes if not (r[0] or r[1])]
    amount = sum(len(r[2]) for r in remote)
    local_amount = sum(len(r[2]) for r in local)

    def kernel(*refs):
        ins = refs[: len(operands)]
        out = refs[len(operands) : len(operands) + len(outs)]
        send, recv, own = refs[len(operands) + len(outs) :]
        c, f = lax.axis_index("ctx"), lax.axis_index("fsdp")
        barrier = pltpu.get_barrier_semaphore()
        for dc, df, _ in remote:
            pl.semaphore_signal(
                barrier, inc=1, device_id=(flip(c, dc), flip(f, df)), device_id_type=MESH
            )
        copies = []
        for dc, df, moves in local:
            for a, src, b, dst in moves:
                copy = pltpu.make_async_copy(
                    ins[a].at[src(c, f)], out[b].at[dst(c, f)], own.at[len(copies)]
                )
                copy.start()
                copies.append(copy)
        pl.semaphore_wait(barrier, len(remote))
        number = 0
        for dc, df, moves in remote:
            for a, src, b, dst in moves:
                copy = pltpu.make_async_remote_copy(
                    ins[a].at[src(c, f)],
                    out[b].at[dst(c, f)],
                    send.at[number],
                    recv.at[number],
                    device_id=(flip(c, dc), flip(f, df)),
                    device_id_type=MESH,
                )
                copy.start()
                copies.append(copy)
                number += 1
        for copy in copies:
            copy.wait()

    anywhere = pl.BlockSpec(memory_space=pl.ANY)
    return pl.pallas_call(
        kernel,
        name=name,
        out_shape=[jax.ShapeDtypeStruct(shape, dtype) for shape, dtype in outs],
        in_specs=[anywhere] * len(operands),
        out_specs=[anywhere] * len(outs),
        scratch_shapes=[
            pltpu.SemaphoreType.DMA((amount,)),
            pltpu.SemaphoreType.DMA((amount,)),
            pltpu.SemaphoreType.DMA((max(local_amount, 1),)),
        ],
        compiler_params=pltpu.CompilerParams(collective_id=cid, has_side_effects=True),
        cost_estimate=lasting(microseconds),
    )(*operands)


PAY = D + 128
GROUPS = 4
ROWS = GROUPS * CAP


def other_chip(c, f, k):
    pair, x = lax.div(k, 2), lax.rem(k, 2)
    return (
        c + pair * (1 - 2 * lax.rem(c, 2)),
        f + 2 * x * (1 - 2 * lax.rem(lax.div(f, 2), 2)),
    )


def plane_order(replicas):
    order = [0]
    while len(order) < replicas:
        order = [2 * i for i in order] + [2 * i + 1 for i in order]
    return order


def experts_kernel(
    replicas, pay, cot, gate_own, up_own, down_own, after,
    back, mix, grads, pay_in, cot_in,
    weights, total, pay_now, cot_now, xs, gs, eo, gi, hid, dgate, dup, disp, comb,
    own, out, sib, ret, mix_now,
    send_first, recv_first, send_fwd, recv_fwd, send_sib, recv_sib, send_chip, recv_chip,
    load_w, load, store, piece_sem,
):
    c, f = lax.axis_index("ctx"), lax.axis_index("fsdp")
    rank = lax.rem(c, 2) * 4 + f
    sibling = (c, flip(f, 1))
    barrier = pltpu.get_barrier_semaphore()
    pl.semaphore_signal(barrier, inc=1, device_id=sibling, device_id_type=MESH)
    for k in range(1, 4):
        pl.semaphore_signal(barrier, inc=1, device_id=other_chip(c, f, k), device_id_type=MESH)
    bring = []
    for m, own_weight in enumerate((gate_own, up_own, down_own)):
        bring.append(pltpu.make_async_copy(own_weight, weights.at[m], load_w.at[m]))
        bring[-1].start()
    pl.semaphore_wait(barrier, 4)
    sources, landed = (pay, cot), (pay_in, cot_in)

    def push(k, a):
        slot = 1 if k == 0 else 2 * k
        return pltpu.make_async_remote_copy(
            sources[a], landed[a].at[slot - 1], send_first.at[k, a], recv_first.at[k, a],
            device_id=sibling if k == 0 else other_chip(c, f, k), device_id_type=MESH,
        )

    def forward(k, a):
        return pltpu.make_async_remote_copy(
            landed[a].at[2 * k - 1], landed[a].at[2 * k], send_fwd.at[k - 1, a], recv_fwd.at[k - 1, a],
            device_id=sibling, device_id_type=MESH,
        )

    def to_sibling(k):
        return pltpu.make_async_remote_copy(
            out.at[lax.rem(k, 2)], sib.at[k], send_sib.at[k], recv_sib.at[k],
            device_id=sibling, device_id_type=MESH,
        )

    def to_chip(k):
        return pltpu.make_async_remote_copy(
            sib.at[k], ret.at[k - 1], send_chip.at[k - 1], recv_chip.at[k - 1],
            device_id=other_chip(c, f, k), device_id_type=MESH,
        )

    def store_mix(k, s):
        return pltpu.make_async_copy(mix_now.at[s], mix.at[2 * k + s], store.at[s])

    for k, a in ((0, 0), (0, 1), (1, 0), (2, 0), (1, 1), (2, 1), (3, 0), (3, 1)):
        push(k, a).start()

    def clear(i, carry):
        total[lax.div(i, OWN), lax.rem(i, OWN)] = jnp.zeros((FF, D), F32)
        return carry

    lax.fori_loop(0, 3 * OWN, clear, 0)
    lane = lax.broadcasted_iota(jnp.int32, (BLOCK, 128), 1)
    wide = lax.broadcasted_iota(jnp.int32, (BLOCK, 2 * BLOCK), 1).astype(F32)
    both = lax.broadcasted_iota(jnp.int32, (BLOCK, OWN * CAP), 1)

    def chunk(k, carry):
        now = (pay_now, cot_now)

        def fetch(a, s, source):
            copy = pltpu.make_async_copy(source, now[a].at[s], load.at[a, s])
            copy.start()
            return copy

        @pl.when(k == 0)
        def _():
            copies = [fetch(a, 0, sources[a]) for a in range(2)]
            for a in range(2):
                push(0, a).wait_recv()
            copies += [fetch(a, 1, landed[a].at[0]) for a in range(2)]
            for copy in copies:
                copy.wait()
            for copy in bring:
                copy.wait()

        @pl.when(k > 0)
        def _():
            for a in range(2):
                pltpu.make_async_remote_copy(
                    sources[a], landed[a].at[2 * k - 1], send_first.at[k, a], recv_first.at[k, a],
                    device_id=other_chip(c, f, k), device_id_type=MESH,
                ).wait_recv()
                forward(k, a).start()
            copies = [fetch(a, 0, landed[a].at[2 * k - 1]) for a in range(2)]
            for a in range(2):
                forward(k, a).wait_recv()
            copies += [fetch(a, 1, landed[a].at[2 * k]) for a in range(2)]
            for copy in copies:
                copy.wait()

        for g in range(GROUPS):
            s, at = g // 2, (g % 2) * BLOCK
            tail = pay_now[s, at : at + BLOCK, D:].astype(F32)

            def column(index):
                return jnp.sum(jnp.where(lane == index, tail, 0.0), axis=1, keepdims=True)

            table = jnp.zeros((BLOCK, 2 * BLOCK), F32)
            gated = jnp.zeros((BLOCK, 2 * BLOCK), F32)
            for e in range(OWN):
                place = column(rank * OWN + e)
                place = jnp.where(place < 0.0, -1000.0, place + e * CAP)
                here = wide == place
                table = jnp.where(here, 1.0, table)
                gated = jnp.where(here, column(EXPERTS + rank * OWN + e), gated)
            table, gated = table.astype(BF16), gated.astype(BF16)
            disp[g] = table
            comb[g] = gated
            for weight, source, keep in (
                (table, pay_now[s, at : at + BLOCK, :D], xs),
                (gated, cot_now[s, at : at + BLOCK], gs),
            ):
                moved = lax.dot_general(
                    weight, source, (((0,), (0,)), ((), ())), preferred_element_type=F32
                ).astype(BF16)
                for e in range(OWN):
                    keep[e, g * CAP : (g + 1) * CAP] = moved[e * CAP : (e + 1) * CAP]

        def expert(e, carry):
            at = pl.multiple_of(e * CAP, 16)
            gate_pre = jnp.dot(xs[e], weights[0, e], preferred_element_type=F32)
            up_pre = jnp.dot(xs[e], weights[1, e], preferred_element_type=F32)
            sigmoid = 1.0 / (1.0 + jnp.exp(-gate_pre))
            activated = gate_pre * sigmoid
            hidden = (activated * up_pre).astype(BF16)
            hid[e] = hidden
            made = lax.dot_general(
                hidden, weights[2, e], (((1,), (1,)), ((), ())), preferred_element_type=F32
            ).astype(BF16)
            for g in range(GROUPS):
                eo[pl.ds(pl.multiple_of(g * OWN * CAP + at, 16), CAP)] = made[g * CAP : (g + 1) * CAP]
            grad_hidden = jnp.dot(gs[e], weights[2, e], preferred_element_type=F32)
            slope = sigmoid * (1.0 + gate_pre * (1.0 - sigmoid))
            grad_gate = (grad_hidden * up_pre * slope).astype(BF16)
            grad_up = (grad_hidden * activated).astype(BF16)
            dgate[e] = grad_gate
            dup[e] = grad_up
            made = lax.dot_general(
                grad_gate, weights[0, e], (((1,), (1,)), ((), ())), preferred_element_type=F32
            )
            made = made + lax.dot_general(
                grad_up, weights[1, e], (((1,), (1,)), ((), ())), preferred_element_type=F32
            )
            made = made.astype(BF16)
            for g in range(GROUPS):
                gi[pl.ds(pl.multiple_of(g * OWN * CAP + at, 16), CAP)] = made[g * CAP : (g + 1) * CAP]
            return carry

        lax.fori_loop(0, OWN, expert, 0)

        @pl.when(k > 0)
        def _():
            for s in range(2):
                store_mix(k - 1, s).wait()

        @pl.when(k > 1)
        def _():
            to_sibling(k - 2).wait_send()

        parity = lax.rem(k, 2)
        for g in range(GROUPS):
            s, at = g // 2, (g % 2) * BLOCK
            slots = pl.ds(g * OWN * CAP, OWN * CAP)
            made = eo[slots]
            mix_now[s, at : at + BLOCK] = jnp.dot(
                comb[g][:, : OWN * CAP], made, preferred_element_type=F32
            ).astype(BF16)
            table = disp[g][:, : OWN * CAP]
            grad_mid = jnp.dot(table, gi[slots], preferred_element_type=F32).astype(BF16)
            met = lax.dot_general(
                cot_now[s, at : at + BLOCK], made, (((1,), (1,)), ((), ())), preferred_element_type=F32
            ) * table.astype(F32)
            values = jnp.zeros((BLOCK, 128), F32)
            for e in range(OWN):
                inside = (both >= e * CAP) & (both < (e + 1) * CAP)
                value = jnp.sum(jnp.where(inside, met, 0.0), axis=1, keepdims=True)
                values = jnp.where(lane == rank * OWN + e, value, values)
            target = own if s == 0 else out
            target[parity, at : at + BLOCK, :D] = grad_mid
            target[parity, at : at + BLOCK, D:] = values.astype(BF16)
        to_sibling(k).start()
        for s in range(2):
            store_mix(k, s).start()

        def weight_grads(e, carry):
            for m, (left, right) in enumerate(((dgate, xs), (dup, xs), (hid, gs))):
                total[m, e] += lax.dot_general(
                    left[e], right[e], (((0,), (0,)), ((), ())), preferred_element_type=F32
                )
            return carry

        lax.fori_loop(0, OWN, weight_grads, 0)
        to_sibling(k).wait_recv()
        sib[k] = (sib[k].astype(F32) + own[parity].astype(F32)).astype(BF16)

        @pl.when(k > 0)
        def _():
            to_chip(k).start()

        return carry

    lax.fori_loop(0, 4, chunk, 0)
    for s in range(2):
        store_mix(3, s).wait()
    stages = (eo, gi)
    pending = []
    for i in range(3 * OWN):
        m, e = i // OWN, i % OWN
        if i >= 2:
            for copy in pending[i - 2]:
                copy.wait()
        stages[i % 2][:FF] = total[m, e].astype(BF16)
        pending.append([])
        if len(grads.shape) == 4:
            pending[i].append(
                pltpu.make_async_copy(stages[i % 2].at[:FF], grads.at[m, e], piece_sem.at[i % 2, 0])
            )
        else:
            width = D // replicas
            for at, plane in enumerate(plane_order(replicas)):
                pending[i].append(
                    pltpu.make_async_copy(
                        stages[i % 2].at[:FF, plane * width : (plane + 1) * width],
                        grads.at[m, at, e],
                        piece_sem.at[i % 2, at],
                    )
                )
        for copy in pending[i]:
            copy.start()
    for copy in pending[-2] + pending[-1]:
        copy.wait()
    for k in (2, 3):
        to_sibling(k).wait_send()
    for k in range(4):
        for a in range(2):
            push(k, a).wait_send()
            if k:
                forward(k, a).wait_send()
    for k in range(1, 4):
        to_chip(k).wait_recv()
    back[...] = (sib[0].astype(F32) + ret[0].astype(F32)) + (ret[1].astype(F32) + ret[2].astype(F32))
    for k in range(1, 4):
        to_chip(k).wait_send()


def run_experts(cid, replicas, pay, cot, owns, after):
    width = D // replicas
    apart = width % 128 == 0
    tokens = SEQS * BLOCK
    anywhere = pl.BlockSpec(memory_space=pl.ANY)
    inside = pl.BlockSpec(memory_space=pltpu.VMEM)
    dma = pltpu.SemaphoreType.DMA
    back, mix, grads, _, _ = pl.pallas_call(
        functools.partial(experts_kernel, replicas),
        name="experts",
        out_shape=[
            jax.ShapeDtypeStruct((tokens, PAY), F32),
            jax.ShapeDtypeStruct((RANKS, tokens, D), BF16),
            jax.ShapeDtypeStruct((3, replicas, OWN, FF, width) if apart else (3, OWN, FF, D), BF16),
            jax.ShapeDtypeStruct((RANKS - 1, tokens, PAY), BF16),
            jax.ShapeDtypeStruct((RANKS - 1, tokens, D), BF16),
        ],
        in_specs=[anywhere] * 6,
        out_specs=[inside] + [anywhere] * 4,
        scratch_shapes=[
            pltpu.VMEM((3, OWN, D, FF), BF16),
            pltpu.VMEM((3, OWN, FF, D), F32),
            pltpu.VMEM((2, tokens, PAY), BF16),
            pltpu.VMEM((2, tokens, D), BF16),
            pltpu.VMEM((OWN, ROWS, D), BF16),
            pltpu.VMEM((OWN, ROWS, D), BF16),
            pltpu.VMEM((OWN * ROWS, D), BF16),
            pltpu.VMEM((OWN * ROWS, D), BF16),
            pltpu.VMEM((OWN, ROWS, FF), BF16),
            pltpu.VMEM((OWN, ROWS, FF), BF16),
            pltpu.VMEM((OWN, ROWS, FF), BF16),
            pltpu.VMEM((GROUPS, BLOCK, 2 * BLOCK), BF16),
            pltpu.VMEM((GROUPS, BLOCK, 2 * BLOCK), BF16),
            pltpu.VMEM((2, tokens, PAY), BF16),
            pltpu.VMEM((2, tokens, PAY), BF16),
            pltpu.VMEM((4, tokens, PAY), BF16),
            pltpu.VMEM((3, tokens, PAY), BF16),
            pltpu.VMEM((2, tokens, D), BF16),
            dma((4, 2)), dma((4, 2)), dma((3, 2)), dma((3, 2)),
            dma((4,)), dma((4,)), dma((3,)), dma((3,)),
            dma((4,)), dma((2, 2)), dma((2,)), dma((2, replicas)),
        ],
        compiler_params=pltpu.CompilerParams(
            collective_id=cid, has_side_effects=True, vmem_limit_bytes=63 << 20
        ),
        cost_estimate=lasting(110),
    )(pay, cot, *owns, after)
    if not apart:
        grads = grads.reshape(3, OWN, FF, replicas, width).transpose(0, 3, 1, 2, 4)
        grads = grads[:, jnp.array(plane_order(replicas))]
    return back, mix, grads


def half_masks(dtype):
    lane = lax.broadcasted_iota(jnp.int32, (1, 2 * HEAD_SIZE), 1)
    low = (lane < HEAD_SIZE).astype(F32)
    return low.astype(dtype), (1.0 - low).astype(dtype)


def allowed_at(block, step, segq, keycode):
    token = block * BLOCK + lax.broadcasted_iota(jnp.int32, (BLOCK, KEYS), 0)
    key = step * KEYS + lax.broadcasted_iota(jnp.int32, (BLOCK, KEYS), 1)
    return ((segq == keycode) & (key < token)) | (key == token)


SMALL = 32


def turn(field, cosine, sine):
    half = HEAD_SIZE // 2
    lane = lax.broadcasted_iota(jnp.int32, field.shape, field.ndim - 1)
    up = pltpu.roll(field, 2 * HEAD_SIZE - half, field.ndim - 1)
    down = pltpu.roll(field, half, field.ndim - 1)
    return field * cosine + jnp.where(lax.rem(lane, HEAD_SIZE) < half, -up, down) * sine


def attention_forward_kernel(
    parts, n_ctx, tok, small, w_q, w_k, w_v, w_o, pack0, pack1, pack2, cos_ref, sin_ref, seg_ref, code_ref,
    normed, small_all, q_full, k_full, v_full, q_ref, kv_ref, full_ref, log_ref, o_back, o_full,
    gate_own, up_own, down_own,
    acc, q_pack, kv_pack, o_buf,
    send_w, recv_w, send_s, recv_s, send_e, recv_e, send_q, recv_q, send_kv, recv_kv, send_o, recv_o, here,
):
    c, f = lax.axis_index("ctx"), lax.axis_index("fsdp")
    head, part, pair = lax.div(c, parts), lax.rem(c, parts), lax.rem(c, 2)
    rows = D // 4
    half = rows // 2
    wide = 2 * HEAD_SIZE
    barrier = pltpu.get_barrier_semaphore()
    peers = [(i, 0) for i in range(1, n_ctx)] + [(0, k) for k in range(1, 4)]
    for dc, df in peers:
        pl.semaphore_signal(
            barrier, inc=1, device_id=(flip(c, dc), flip(f, df)), device_id_type=MESH
        )
    shards = (w_q, w_k, w_v, w_o)
    fulls = (q_full, k_full, v_full, o_full)
    packs, owns = (pack0, pack1, pack2), (gate_own, up_own, down_own)
    my_rows = pl.ds(pl.multiple_of(f * rows, rows), rows)
    local = [pltpu.make_async_copy(shards[a], fulls[a].at[f], here.at[a]) for a in range(4)]
    local += [pltpu.make_async_copy(small, small_all.at[f], here.at[4])]
    local += [pltpu.make_async_copy(packs[m].at[f], owns[m].at[:, my_rows], here.at[5 + m]) for m in range(3)]
    for copy in local:
        copy.start()
    pl.semaphore_wait(barrier, len(peers))
    near = pl.ds(pl.multiple_of(pair * half, half), half)
    far = pl.ds(pl.multiple_of((1 - pair) * half, half), half)
    sibling, over_x, over_pair = (c, flip(f, 1)), (c, flip(f, 2)), (flip(c, 1), f)

    def weight(a, kind):
        beyond = flip(f, 2)
        source, target, device = (
            (shards[a], fulls[a].at[f], sibling),
            (shards[a].at[near], fulls[a].at[f, near], over_x),
            (fulls[a].at[beyond, near], fulls[a].at[beyond, near], sibling),
            (fulls[a].at[beyond, near], fulls[a].at[beyond, near], over_pair),
            (fulls[a].at[beyond, far], fulls[a].at[beyond, far], sibling),
        )[kind]
        return pltpu.make_async_remote_copy(
            source, target, send_w.at[a, kind], recv_w.at[a, kind], device_id=device, device_id_type=MESH
        )

    smalls = [
        pltpu.make_async_remote_copy(
            small, small_all.at[f], send_s.at[i - 1], recv_s.at[i - 1],
            device_id=(c, flip(f, i)), device_id_type=MESH,
        )
        for i in range(1, 4)
    ]
    for copy in smalls:
        copy.start()
    for a in range(4):
        weight(a, 1).start()
        weight(a, 0).start()
    experts = [
        pltpu.make_async_remote_copy(
            packs[m].at[flip(f, i)], owns[m].at[:, my_rows], send_e.at[i - 1, m], recv_e.at[i - 1, m],
            device_id=(c, flip(f, i)), device_id_type=MESH,
        )
        for m in range(3)
        for i in range(1, 4)
    ]
    for copy in experts:
        copy.start()

    x = tok[...].astype(F32)
    scale = lax.rsqrt(jnp.mean(x * x, axis=1, keepdims=True) + EPS)
    for copy in smalls:
        copy.wait_recv()
    local[4].wait()
    for b in range(4):
        columns = slice(b * rows, (b + 1) * rows)
        normed[:, columns] = (x[:, columns] * scale * small_all[b, :1].astype(F32)).astype(BF16)

    def project(b, first):
        block = normed[:, pl.ds(pl.multiple_of(b * rows, rows), rows)]
        at = 0
        for a in range(3):
            width = fulls[a].shape[2]
            made = jnp.dot(block, fulls[a][b], preferred_element_type=F32)
            acc[:, at : at + width] = made if first else acc[:, at : at + width] + made
            at += width

    for a in range(3):
        local[a].wait()
    project(f, True)
    for a in range(3):
        weight(a, 0).wait_recv()
    project(flip(f, 1), False)
    for a in range(3):
        weight(a, 1).wait_recv()
        weight(a, 2).start()
        weight(a, 3).start()
    for a in range(3):
        weight(a, 3).wait_recv()
        weight(a, 4).start()
    project(flip(f, 2), False)
    for a in range(3):
        weight(a, 2).wait_recv()
        weight(a, 4).wait_recv()
    project(flip(f, 3), False)

    lane = lax.broadcasted_iota(jnp.int32, (BLOCK, wide), 1)
    low = lane < HEAD_SIZE
    cosine, sine = cos_ref[...], sin_ref[...]
    for m in range((QUERY_HEADS + 2 * KEY_VALUE_HEADS) // 2):
        pieces = []
        for s in range(SEQS):
            piece = acc[s * BLOCK : (s + 1) * BLOCK, m * wide : (m + 1) * wide]
            pieces.append(turn(piece, cosine, sine) if m < (QUERY_HEADS + KEY_VALUE_HEADS) // 2 else piece)
        even = jnp.where(low, pieces[0], pltpu.roll(pieces[1], HEAD_SIZE, 1)).astype(BF16)
        odd = jnp.where(low, pltpu.roll(pieces[0], HEAD_SIZE, 1), pieces[1]).astype(BF16)
        for h, value in ((2 * m, even), (2 * m + 1, odd)):
            if h < QUERY_HEADS:
                q_pack[h // REP, h % REP] = value
            else:
                h -= QUERY_HEADS
                kv_pack[h % KEY_VALUE_HEADS, h // KEY_VALUE_HEADS] = value

    q_stays = pltpu.make_async_copy(q_pack.at[head], q_ref.at[head], here.at[8])
    kv_stays = pltpu.make_async_copy(kv_pack.at[head], kv_ref.at[c], here.at[9])
    q_stays.start()
    kv_stays.start()
    to_heads = []
    for i in range(1, n_ctx):
        peer = flip(c, i)
        moves = [(kv_pack.at[lax.div(peer, parts)], kv_ref.at[c], send_kv.at[i - 1], recv_kv.at[i - 1])]
        if i % parts == 0:
            number = i // parts - 1
            moves.append(
                (q_pack.at[lax.div(peer, parts)], q_ref.at[head], send_q.at[number], recv_q.at[number])
            )
        for source, target, sent, came in moves:
            copy = pltpu.make_async_remote_copy(
                source, target, sent, came, device_id=(peer, f), device_id_type=MESH
            )
            copy.start()
            to_heads.append(copy)
    weight(3, 1).wait_recv()
    weight(3, 2).start()
    weight(3, 3).start()
    q_stays.wait()
    kv_stays.wait()
    for copy in to_heads:
        copy.wait_recv()

    count = REP * BLOCK
    halves = half_masks(BF16)
    across = lax.broadcasted_iota(jnp.int32, (count, wide), 1)

    def out_back(j):
        return pltpu.make_async_remote_copy(
            o_buf.at[j], o_back.at[head], send_o.at[j], recv_o.at[head],
            device_id=(j * parts + part, f), device_id_type=MESH,
        )

    def out_stays(j):
        return pltpu.make_async_copy(o_buf.at[j], o_back.at[head], here.at[10])

    def one_block(j, nothing):
        block = j * parts + part
        q = q_ref[j].reshape(count, wide)
        queries = [q * half for half in halves]

        def step(number, carry):
            k = kv_ref[pl.ds(2 * number, 2), 0].reshape(KEYS, wide)
            v = kv_ref[pl.ds(2 * number, 2), 1].reshape(KEYS, wide)
            codes = code_ref[number]
            after = []
            for s in range(SEQS):
                largest, total, out = carry[s]
                mask = allowed_at(block, number, seg_ref[j, s], codes[s : s + 1])
                scores = lax.dot_general(
                    queries[s], k, (((1,), (1,)), ((), ())), preferred_element_type=F32
                )
                scores = jnp.where(mask[None], scores.reshape(REP, BLOCK, KEYS) * SCALE, MASKED)
                scores = scores.reshape(count, KEYS)
                new = jnp.maximum(largest, jnp.max(scores, axis=1, keepdims=True))
                probs = jnp.exp(scores - new)
                shrink = jnp.exp(largest - new)
                total = total * shrink + jnp.sum(probs, axis=1, keepdims=True)
                out = out * shrink + jnp.dot(probs.astype(BF16), v, preferred_element_type=F32)
                after.append((new, total, out))
            return tuple(after)

        start = (
            jnp.full((count, 1), MASKED, F32),
            jnp.zeros((count, 1), F32),
            jnp.zeros((count, wide), F32),
        )
        done = lax.fori_loop(0, lax.div(block, 2) + 1, step, (start,) * SEQS)
        outs, logs = [], []
        for largest, total, out in done:
            outs.append(out / total)
            logs.append(jnp.broadcast_to(largest + jnp.log(total), (count, wide)))
        out = jnp.where(across < HEAD_SIZE, outs[0], outs[1])
        full_ref[j] = out.reshape(REP, BLOCK, wide)
        log_ref[j] = jnp.where(across < HEAD_SIZE, logs[0], logs[1]).reshape(REP, BLOCK, wide)
        o_buf[j] = out.astype(BF16).reshape(REP, BLOCK, wide)

        @pl.when(j != head)
        def _():
            out_back(j).start()

        @pl.when(j == head)
        def _():
            out_stays(j).start()

        return nothing

    lax.fori_loop(0, KEY_VALUE_HEADS, one_block, 0)
    weight(3, 3).wait_recv()
    weight(3, 4).start()

    def came_out(h, nothing):
        @pl.when(h != head)
        def _():
            pltpu.make_async_remote_copy(
                o_buf.at[h], o_back.at[h], send_o.at[h], recv_o.at[h],
                device_id=(h * parts + part, f), device_id_type=MESH,
            ).wait()

        @pl.when(h == head)
        def _():
            out_stays(h).wait()

        return nothing

    lax.fori_loop(0, KEY_VALUE_HEADS, came_out, 0)
    for kind in (0, 2, 4):
        weight(3, kind).wait_recv()
    local[3].wait()
    for copy in local[5:]:
        copy.wait()
    for copy in experts:
        copy.wait()
    for copy in smalls + to_heads:
        copy.wait_send()
    for a in range(4):
        for kind in range(5):
            weight(a, kind).wait_send()


def attention_forward(
    cid, parts, n_ctx, tok, small, w_q, w_k, w_v, w_o, packs, cosine, sine, segq, codes
):
    wide = 2 * HEAD_SIZE
    anywhere = pl.BlockSpec(memory_space=pl.ANY)
    inside = pl.BlockSpec(memory_space=pltpu.VMEM)
    dma = pltpu.SemaphoreType.DMA
    heads = (KEY_VALUE_HEADS, REP, BLOCK, wide)
    keys = (n_ctx, 2, BLOCK, wide)
    others = max(n_ctx // parts - 1, 1)
    columns = w_q.shape[1] + w_k.shape[1] + w_v.shape[1]
    own = jax.ShapeDtypeStruct((OWN, D, FF), BF16)

    def full(x):
        return jax.ShapeDtypeStruct((4,) + x.shape, BF16)

    return pl.pallas_call(
        functools.partial(attention_forward_kernel, parts, n_ctx),
        name="attention_forward",
        out_shape=[
            jax.ShapeDtypeStruct(tok.shape, BF16),
            full(small), full(w_q), full(w_k), full(w_v),
            jax.ShapeDtypeStruct(heads, BF16),
            jax.ShapeDtypeStruct(keys, BF16),
            jax.ShapeDtypeStruct(heads, F32),
            jax.ShapeDtypeStruct(heads, F32),
            jax.ShapeDtypeStruct(heads, BF16),
            full(w_o), own, own, own,
        ],
        in_specs=[inside] + [anywhere] * 8 + [inside] * 4,
        out_specs=[inside] * 9 + [anywhere] * 5,
        scratch_shapes=[
            pltpu.VMEM((SEQS * BLOCK, columns), F32),
            pltpu.VMEM(heads, BF16),
            pltpu.VMEM((KEY_VALUE_HEADS, 2, BLOCK, wide), BF16),
            pltpu.VMEM(heads, BF16),
            dma((4, 5)), dma((4, 5)), dma((3,)), dma((3,)), dma((3, 3)), dma((3, 3)),
            dma((others,)), dma((others,)), dma((n_ctx - 1,)), dma((n_ctx - 1,)),
            dma((KEY_VALUE_HEADS,)), dma((KEY_VALUE_HEADS,)), dma((11,)),
        ],
        compiler_params=pltpu.CompilerParams(
            collective_id=cid, has_side_effects=True, vmem_limit_bytes=56 << 20
        ),
        cost_estimate=lasting(130),
    )(tok, small, w_q, w_k, w_v, w_o, *packs, cosine, sine, segq, codes)


def turn_back(field, cosine, sine):
    half = HEAD_SIZE // 2
    lane = lax.broadcasted_iota(jnp.int32, field.shape, field.ndim - 1)
    up = pltpu.roll(field, 2 * HEAD_SIZE - half, field.ndim - 1)
    down = pltpu.roll(field, half, field.ndim - 1)
    turned = jnp.where(lax.rem(lane, HEAD_SIZE) < half, -up, down)
    return field * cosine - turned * sine


def attention_backward_kernel(
    parts, n_ctx, g_own, q_ref, kv_ref, seg_ref, code_ref, full_ref, log_ref, cos_ref, sin_ref,
    grads, mix, dq_ref, dkv_ref, dq_back, dkv_back, gate_came, down_keep, down_came, mix_in,
    g_ref, total, kept, came,
    send_g, recv_g, send_q, recv_q, send_kv, recv_kv, send_mix, recv_mix, send_half, recv_half, here,
):
    c, f = lax.axis_index("ctx"), lax.axis_index("fsdp")
    head, part = lax.div(c, parts), lax.rem(c, parts)
    rows = REP * BLOCK
    wide = 2 * HEAD_SIZE
    barrier = pltpu.get_barrier_semaphore()
    peers = [(i, 0) for i in range(1, n_ctx)]
    peers += [(i // 4, i % 4) for i in range(1, RANKS) if i % 4]
    for dc, df in peers:
        pl.semaphore_signal(
            barrier, inc=1, device_id=(flip(c, dc), flip(f, df)), device_id_type=MESH
        )
    first = pltpu.make_async_copy(g_own.at[head], g_ref.at[head], here.at[0])
    first.start()
    pl.semaphore_wait(barrier, len(peers))
    to_heads = []
    for number, i in enumerate(range(parts, n_ctx, parts)):
        to_heads.append(
            pltpu.make_async_remote_copy(
                g_own.at[lax.div(flip(c, i), parts)], g_ref.at[head],
                send_g.at[number], recv_g.at[number],
                device_id=(flip(c, i), f), device_id_type=MESH,
            )
        )
        to_heads[-1].start()
    half = grads.shape[1] // 2
    quarter = half // 2
    mine = lax.rem(lax.div(c, 2), 2)
    second = lax.rem(lax.div(c, 4), 2)

    def halving(matrix, target, number):
        return pltpu.make_async_remote_copy(
            grads.at[matrix, pl.ds((1 - mine) * half, half)], target,
            send_half.at[number], recv_half.at[number],
            device_id=(flip(c, 2), f), device_id_type=MESH,
        )

    down_halving, gate_halving = halving(2, came, 0), halving(0, gate_came, 1)
    down_halving.start()
    keeping = pltpu.make_async_copy(grads.at[2, pl.ds(mine * half, half)], kept, here.at[3])
    keeping.start()
    returns = []
    for i in range(1, RANKS):
        returns.append(
            pltpu.make_async_remote_copy(
                mix.at[i], mix_in.at[i - 1], send_mix.at[i - 1], recv_mix.at[i - 1],
                device_id=(flip(c, i // 4), flip(f, i % 4)), device_id_type=MESH,
            )
        )
        returns[-1].start()
    total[...] = jnp.zeros_like(total)
    first.wait()
    for copy in to_heads:
        copy.wait_recv()
    halves = half_masks(BF16)
    lane = lax.broadcasted_iota(jnp.int32, (rows, wide), 1)

    def query_back(j):
        return pltpu.make_async_remote_copy(
            dq_ref.at[j], dq_back.at[head], send_q.at[j], recv_q.at[head],
            device_id=(j * parts + part, f), device_id_type=MESH,
        )

    def key_back(b):
        return pltpu.make_async_remote_copy(
            dkv_ref.at[b], dkv_back.at[c], send_kv.at[b], recv_kv.at[c],
            device_id=(b, f), device_id_type=MESH,
        )

    def query_stays(j):
        return pltpu.make_async_copy(dq_ref.at[j], dq_back.at[head], here.at[1])

    def key_stays(b):
        return pltpu.make_async_copy(dkv_ref.at[b], dkv_back.at[c], here.at[2])

    def one_block(j, nothing):
        block = j * parts + part
        q = q_ref[j].reshape(rows, wide)
        g = g_ref[j].reshape(rows, wide)
        queries = [q * half for half in halves]
        partial = [g * half for half in halves]
        product = g.astype(F32) * full_ref[j].reshape(rows, wide)
        logs = log_ref[j].reshape(rows, wide)
        log_total = [logs[:, :1], logs[:, HEAD_SIZE : HEAD_SIZE + 1]]
        inner = [jnp.sum(product * half, axis=1, keepdims=True) for half in half_masks(F32)]

        def step(number, carry):
            k = kv_ref[pl.ds(2 * number, 2), 0].reshape(KEYS, wide)
            v = kv_ref[pl.ds(2 * number, 2), 1].reshape(KEYS, wide)
            codes = code_ref[number]
            after = []
            dk = jnp.zeros((KEYS, wide), F32)
            dv = jnp.zeros((KEYS, wide), F32)
            for s in range(SEQS):
                mask = allowed_at(block, number, seg_ref[j, s], codes[s : s + 1])
                scores = lax.dot_general(
                    queries[s], k, (((1,), (1,)), ((), ())), preferred_element_type=F32
                )
                scores = jnp.where(mask[None], scores.reshape(REP, BLOCK, KEYS) * SCALE, MASKED)
                probs = jnp.exp(scores.reshape(rows, KEYS) - log_total[s])
                grad_probs = lax.dot_general(
                    partial[s], v, (((1,), (1,)), ((), ())), preferred_element_type=F32
                )
                grad_scores = (probs * (grad_probs - inner[s])).astype(BF16)
                dv = dv + lax.dot_general(
                    probs.astype(BF16), partial[s], (((0,), (0,)), ((), ())), preferred_element_type=F32
                )
                dk = dk + lax.dot_general(
                    grad_scores, queries[s], (((0,), (0,)), ((), ())), preferred_element_type=F32
                )
                after.append(carry[s] + jnp.dot(grad_scores, k, preferred_element_type=F32))
            total[pl.ds(2 * number, 2), 0] += dk.reshape(2, BLOCK, wide)
            total[pl.ds(2 * number, 2), 1] += dv.reshape(2, BLOCK, wide)
            return tuple(after)

        start = jnp.zeros((rows, wide), F32)
        done = lax.fori_loop(0, lax.div(block, 2) + 1, step, (start,) * SEQS)
        dq = (jnp.where(lane < HEAD_SIZE, done[0], done[1]) * SCALE).reshape(REP, BLOCK, wide)
        dq_ref[j] = turn_back(dq, cos_ref[block][None], sin_ref[block][None]).astype(BF16)

        @pl.when(j != head)
        def _():
            query_back(j).start()

        @pl.when(j == head)
        def _():
            query_stays(j).start()

        return nothing

    lax.fori_loop(0, KEY_VALUE_HEADS, one_block, 0)

    def finish(b, nothing):
        dkv_ref[b, 0] = turn_back(total[b, 0] * SCALE, cos_ref[b], sin_ref[b]).astype(BF16)
        dkv_ref[b, 1] = total[b, 1].astype(BF16)

        @pl.when(b != c)
        def _():
            key_back(b).start()

        @pl.when(b == c)
        def _():
            key_stays(b).start()

        return nothing

    lax.fori_loop(0, n_ctx, finish, 0)
    gate_halving.start()
    keeping.wait()
    down_halving.wait_recv()

    def add(i, nothing):
        at, e = lax.div(i, OWN), lax.rem(i, OWN)
        kept[at, e] = (kept[at, e].astype(F32) + came[at, e].astype(F32)).astype(BF16)
        return nothing

    lax.fori_loop(0, half * OWN, add, 0)
    down_second = pltpu.make_async_remote_copy(
        kept.at[pl.ds((1 - second) * quarter, quarter)], down_came, send_half.at[2], recv_half.at[2],
        device_id=(flip(c, 4), f), device_id_type=MESH,
    )
    down_second.start()
    leaving = pltpu.make_async_copy(kept.at[pl.ds(second * quarter, quarter)], down_keep, here.at[4])
    leaving.start()

    def came_query(h, nothing):
        @pl.when(h != head)
        def _():
            pltpu.make_async_remote_copy(
                dq_ref.at[h], dq_back.at[h], send_q.at[h], recv_q.at[h],
                device_id=(h * parts + part, f), device_id_type=MESH,
            ).wait()

        @pl.when(h == head)
        def _():
            query_stays(h).wait()

        return nothing

    def came_key(b, nothing):
        @pl.when(b != c)
        def _():
            pltpu.make_async_remote_copy(
                dkv_ref.at[b], dkv_back.at[b], send_kv.at[b], recv_kv.at[b],
                device_id=(b, f), device_id_type=MESH,
            ).wait()

        @pl.when(b == c)
        def _():
            key_stays(b).wait()

        return nothing

    lax.fori_loop(0, KEY_VALUE_HEADS, came_query, 0)
    lax.fori_loop(0, n_ctx, came_key, 0)
    for copy in to_heads:
        copy.wait_send()
    for copy in returns + [gate_halving, down_second, leaving]:
        copy.wait()
    down_halving.wait_send()


def attention_backward(
    cid, parts, n_ctx, g_own, q, kv, segq, codes, full, logs, cosine, sine, grads, mix
):
    wide = 2 * HEAD_SIZE
    anywhere = pl.BlockSpec(memory_space=pl.ANY)
    inside = pl.BlockSpec(memory_space=pltpu.VMEM)
    dma = pltpu.SemaphoreType.DMA
    others = max(n_ctx // parts - 1, 1)
    return pl.pallas_call(
        functools.partial(attention_backward_kernel, parts, n_ctx),
        name="attention_backward",
        out_shape=[
            jax.ShapeDtypeStruct(q.shape, BF16),
            jax.ShapeDtypeStruct(kv.shape, BF16),
            jax.ShapeDtypeStruct(q.shape, BF16),
            jax.ShapeDtypeStruct(kv.shape, BF16),
            jax.ShapeDtypeStruct((grads.shape[1] // 2,) + grads.shape[2:], BF16),
            jax.ShapeDtypeStruct((grads.shape[1] // 4,) + grads.shape[2:], BF16),
            jax.ShapeDtypeStruct((grads.shape[1] // 4,) + grads.shape[2:], BF16),
            jax.ShapeDtypeStruct((RANKS - 1,) + mix.shape[1:], BF16),
        ],
        in_specs=[anywhere] + [inside] * 8 + [anywhere] * 2,
        out_specs=[inside] * 2 + [anywhere] * 6,
        scratch_shapes=[
            pltpu.VMEM(q.shape, BF16),
            pltpu.VMEM((n_ctx, 2, BLOCK, wide), F32),
            pltpu.VMEM((grads.shape[1] // 2,) + grads.shape[2:], BF16),
            pltpu.VMEM((grads.shape[1] // 2,) + grads.shape[2:], BF16),
            dma((others,)), dma((others,)), dma((KEY_VALUE_HEADS,)), dma((KEY_VALUE_HEADS,)),
            dma((n_ctx,)), dma((n_ctx,)), dma((RANKS - 1,)), dma((RANKS - 1,)), dma((3,)), dma((3,)), dma((5,)),
        ],
        compiler_params=pltpu.CompilerParams(
            collective_id=cid, has_side_effects=True, vmem_limit_bytes=48 << 20
        ),
        cost_estimate=lasting(90),
    )(g_own, q, kv, segq, codes, full, logs, cosine, sine, grads, mix)


def rope_tables(positions):
    half_dim = HEAD_SIZE // 2
    frequency = ROPE_BASE ** (-jnp.arange(half_dim, dtype=F32) * 2.0 / HEAD_SIZE)
    angle = positions.astype(F32)[:, None] * frequency[None, :]
    angle = jnp.concatenate([angle, angle], axis=1)
    return (jnp.cos(angle), jnp.sin(angle))


def heads_out(field, per):
    field = field.reshape(SEQS, BLOCK, KEY_VALUE_HEADS, per, HEAD_SIZE)
    return field.transpose(2, 3, 1, 0, 4).reshape(KEY_VALUE_HEADS, per, BLOCK, SEQS * HEAD_SIZE)


def heads_in(field):
    per = field.shape[1]
    field = field.reshape(KEY_VALUE_HEADS, per, BLOCK, SEQS, HEAD_SIZE)
    return field.transpose(3, 2, 0, 1, 4).reshape(SEQS, BLOCK, KEY_VALUE_HEADS * per * HEAD_SIZE)


def on_device(
    n_ctx,
    n_fsdp,
    tokens,
    segments,
    valid,
    expert_ids,
    slot_order,
    cotangent,
    norm1_gain,
    w_query,
    key_weight,
    value_weight,
    w_output,
    norm2_gain,
    w_router,
    w_gate,
    w_up,
    w_down,
):
    parts = n_ctx // KEY_VALUE_HEADS
    replicas = n_ctx // 2
    full_len = segments.shape[1]
    c_index, f_index = lax.axis_index("ctx"), lax.axis_index("fsdp")
    pair = lax.rem(c_index, 2)
    rank = pair * n_fsdp + f_index
    part = lax.rem(c_index, parts)
    head = lax.div(c_index, parts)
    positions = c_index * BLOCK + jnp.arange(BLOCK, dtype=jnp.int32)

    def tie(x, after):
        return lax.optimization_barrier((x, after))[0]

    tokens_all = lax.all_gather(tokens, "ctx", axis=0, tiled=False)
    small = jnp.concatenate(
        [
            norm1_gain[None],
            norm2_gain[None],
            w_router.T,
            jnp.zeros((SMALL - EXPERTS - 2, D // n_fsdp), BF16),
        ],
        axis=0,
    )
    packs = [
        lax.dynamic_slice_in_dim(w, pair * (EXPERTS // 2), EXPERTS // 2, 1)
        .reshape(D // n_fsdp, n_fsdp, OWN, FF)
        .transpose(1, 2, 0, 3)
        for w in (w_gate, w_up, w_down)
    ]
    inputs_f = tokens.astype(F32)
    scale_one = lax.rsqrt(jnp.mean(inputs_f * inputs_f, axis=-1, keepdims=True) + EPS)
    segq = segments.reshape(SEQS, KEY_VALUE_HEADS, parts, BLOCK)
    segq = lax.dynamic_index_in_dim(segq, part, 2, keepdims=False).transpose(1, 0, 2)[..., None]
    codes = jnp.where(valid > 0, segments, -1)
    codes = codes.reshape(SEQS, full_len // KEYS, KEYS).transpose(1, 0, 2)
    all_cosine, all_sine = rope_tables(jnp.arange(full_len, dtype=jnp.int32))
    all_cosine = jnp.tile(all_cosine, (1, 2)).reshape(n_ctx, BLOCK, 2 * HEAD_SIZE)
    all_sine = jnp.tile(all_sine, (1, 2)).reshape(n_ctx, BLOCK, 2 * HEAD_SIZE)
    (
        normed_in, small_all, full_query, full_key, full_value, q_all, kv_all, head_full, head_logs,
        attn_heads, full_output, own_gate, own_up, own_down,
    ) = attention_forward(
        0, parts, n_ctx, tokens.reshape(SEQS * BLOCK, D), small, w_query, key_weight, value_weight,
        w_output, packs,
        lax.dynamic_index_in_dim(all_cosine, c_index, 0, keepdims=False),
        lax.dynamic_index_in_dim(all_sine, c_index, 0, keepdims=False),
        segq, codes,
    )
    gain_first = small_all[:, 0].reshape(D).astype(F32)
    gain_second = small_all[:, 1].reshape(D).astype(F32)
    full_router = small_all[:, 2 : 2 + EXPERTS].transpose(1, 0, 2).reshape(EXPERTS, D)
    full_output = full_output.reshape(D, D)
    attn_out = heads_in(attn_heads)
    attn_proj = jnp.einsum("sgq,dq->sgd", attn_out, full_output, preferred_element_type=F32)
    residual = inputs_f + attn_proj
    scale_two = lax.rsqrt(jnp.mean(residual * residual, axis=-1, keepdims=True) + EPS)
    normed_mid = (residual * scale_two * gain_second).astype(BF16)

    logits = jnp.einsum("sgd,ed->sge", normed_mid, full_router, preferred_element_type=F32)
    picked = jnp.any(expert_ids[..., None] == jnp.arange(EXPERTS, dtype=jnp.int32), axis=2)
    before = (slot_order[:, None, :] < slot_order[:, :, None]).astype(BF16)
    place = jnp.matmul(before, picked.astype(BF16), preferred_element_type=F32)
    is_kept = picked & (place < CAP)
    chosen = jnp.where(picked, logits, MASKED)
    raised = jnp.where(picked, jnp.exp(chosen - jnp.max(chosen, axis=-1, keepdims=True)), 0.0)
    gates = raised / jnp.sum(raised, axis=-1, keepdims=True)
    payload = jnp.concatenate(
        [
            normed_mid,
            jnp.where(is_kept, place, -1.0).astype(BF16),
            gates.astype(BF16),
            jnp.zeros((SEQS, BLOCK, 128 - 2 * EXPERTS), BF16),
        ],
        axis=2,
    )
    back, mix_part, own_grads = run_experts(
        2, replicas, payload.reshape(SEQS * BLOCK, PAY), cotangent.reshape(SEQS * BLOCK, D),
        (own_gate, own_up, own_down), tokens_all
    )

    replica = lax.div(c_index, 2)

    def halve(grad, bit):
        grad = grad.reshape((2, -1) + grad.shape[1:])
        mine = lax.rem(lax.div(replica, bit), 2)
        send = lax.dynamic_index_in_dim(grad, 1 - mine, 0, keepdims=False)
        keep = lax.dynamic_index_in_dim(grad, mine, 0, keepdims=False)
        return keep, lax.ppermute(send, "ctx", [(a, a ^ (2 * bit)) for a in range(n_ctx)])

    def joined(halves, after):
        keep, came = halves
        return (keep.astype(F32) + tie(came, after).astype(F32)).astype(BF16)

    back = back.reshape(SEQS, BLOCK, D + 128)
    grad_gates = jnp.where(is_kept, back[..., D : D + EXPERTS], 0.0)
    grad_chosen = gates * (grad_gates - jnp.sum(gates * grad_gates, axis=-1, keepdims=True))
    grad_logits = grad_chosen.astype(BF16)
    grad_mid = back[..., :D] + jnp.einsum(
        "sge,ed->sgd", grad_logits, full_router, preferred_element_type=F32
    )
    grad_router = jnp.einsum("sgd,sge->de", normed_mid, grad_logits, preferred_element_type=F32)

    grad_f = cotangent.astype(F32)
    weighted_two = gain_second * grad_mid
    grad_gain_second = jnp.sum(grad_mid * residual * scale_two, axis=(0, 1))
    cube_two = scale_two * scale_two * scale_two
    grad_resid = (
        grad_f
        + scale_two * weighted_two
        - residual * cube_two * jnp.mean(weighted_two * residual, axis=-1, keepdims=True)
    )
    grad_resid_low = grad_resid.astype(BF16)
    grad_attn = jnp.einsum("sgd,dq->sgq", grad_resid_low, full_output, preferred_element_type=F32)
    grad_attn = grad_attn.astype(BF16)
    grad_output_w = jnp.einsum("sgd,sgq->dq", grad_resid_low, attn_out, preferred_element_type=F32)
    rows = D // (n_ctx * n_fsdp)
    x_bit, core_bit = lax.div(f_index, 2), lax.rem(f_index, 2)

    def two(field, axis, bit):
        return (
            lax.dynamic_index_in_dim(field, 1 - bit, axis, keepdims=False),
            lax.dynamic_index_in_dim(field, bit, axis, keepdims=False),
        )

    def summed(mine, came):
        return (mine.astype(F32) + came.astype(F32)).astype(BF16)

    output_part = grad_output_w.astype(BF16).reshape(replicas, 2, 2, 2, rows, D)
    send, output_mine = two(output_part, 3, core_bit)
    output_came = lax.ppermute(send, "fsdp", [(a, a ^ 1) for a in range(n_fsdp)])

    dq_heads, dkv_heads, dq_back, dkv_back, gate_came, down_keep, down_came, mix_in = attention_backward(
        6, parts, n_ctx, heads_out(grad_attn, REP), q_all, kv_all, segq, codes, head_full, head_logs,
        all_cosine, all_sine, own_grads, mix_part,
    )
    layer_out = (
        residual.reshape(SEQS * BLOCK, D) + mix_part[0].astype(F32) + jnp.sum(mix_in.astype(F32), axis=0)
    ).astype(BF16).reshape(SEQS, BLOCK, D)
    gate_keep = own_grads[0].reshape((2, replicas // 2, OWN, FF, D // replicas))
    gate_half = (lax.dynamic_index_in_dim(gate_keep, lax.rem(replica, 2), 0, keepdims=False), gate_came)
    up_half = halve(tie(own_grads[1], dq_back), 1)
    gate_half = halve(joined(gate_half, dq_back), 2)
    send, output_mine = two(summed(output_mine, output_came), 2, x_bit)
    output_came = lax.ppermute(send, "fsdp", [(a, a ^ 2) for a in range(n_fsdp)])
    send, output_mine = two(summed(output_mine, output_came), 1, pair)
    output_came = lax.ppermute(send, "ctx", [(a, a ^ 1) for a in range(n_ctx)])
    down_half, bit = (down_keep, down_came), 4
    while bit < replicas:
        down_half = halve(joined(down_half, dq_back), bit)
        gate_half = halve(joined(gate_half, dq_back), bit)
        bit *= 2

    tokens_f = tokens_all.astype(F32)
    scale_all = lax.rsqrt(jnp.mean(tokens_f * tokens_f, axis=-1) + EPS)

    def head_weights(field, inputs, scales):
        blocks, per = field.shape[:2]
        field = field.reshape(blocks, per, BLOCK, SEQS, HEAD_SIZE).transpose(0, 3, 2, 1, 4)
        field = (field.astype(F32) * scales[..., None, None]).astype(BF16)
        made = jnp.dot(
            inputs.reshape(blocks * SEQS * BLOCK, D).T,
            field.reshape(blocks * SEQS * BLOCK, per * HEAD_SIZE),
            preferred_element_type=F32,
        )
        return made * gain_first[:, None]

    if parts == 1:
        head_grad = head_weights(jnp.concatenate([dq_heads, dkv_heads], axis=1), tokens_all, scale_all)
    else:
        tokens_part, scale_part = (
            lax.dynamic_index_in_dim(
                x.reshape((KEY_VALUE_HEADS, parts) + x.shape[1:]), part, 1, keepdims=False
            )
            for x in (tokens_all, scale_all)
        )
        head_grad = jnp.concatenate(
            [
                head_weights(dq_heads, tokens_part, scale_part),
                head_weights(dkv_heads, tokens_all, scale_all),
            ],
            axis=1,
        )
    head_width = (REP + 2) * HEAD_SIZE
    head_grad = head_grad.astype(BF16).reshape(n_ctx * n_fsdp, rows, head_width)
    dkv_back = dkv_back.reshape(KEY_VALUE_HEADS, parts, 2, BLOCK, SEQS * HEAD_SIZE)
    if parts == 1:
        dkv_back = dkv_back[:, 0]
    else:
        dkv_back = jnp.sum(dkv_back.astype(F32), axis=1).astype(BF16)
    grad_in = sum(
        jnp.einsum("sgq,dq->sgd", heads_in(grad), weight.reshape(D, -1), preferred_element_type=F32)
        for grad, weight in (
            (dq_back, full_query), (dkv_back[:, :1], full_key), (dkv_back[:, 1:], full_value)
        )
    )
    weighted_one = gain_first * grad_in
    grad_gain_first = jnp.sum(grad_in * inputs_f * scale_one, axis=(0, 1))
    cube_one = scale_one * scale_one * scale_one
    input_grad = (
        grad_resid
        + scale_one * weighted_one
        - inputs_f * cube_one * jnp.mean(weighted_one * inputs_f, axis=-1, keepdims=True)
    ).astype(BF16)
    small_grads = jnp.concatenate(
        [
            grad_router,
            grad_gain_first[:, None],
            grad_gain_second[:, None],
            jnp.zeros((D, 128 - EXPERTS - 2), F32),
        ],
        axis=1,
    ).reshape(n_ctx * n_fsdp, rows, 128)

    def device(c, f):
        return c * n_fsdp + f

    def ranked(c, f):
        return lax.rem(c, 2) * n_fsdp + f

    def by_rank(sums):
        field = jnp.stack(sums).reshape(len(sums), OWN, FF, RANKS, rows)
        return field.transpose(3, 0, 1, 4, 2)

    output_sum = summed(output_mine, output_came)
    gate_down = by_rank([joined(gate_half, head_grad), joined(down_half, head_grad)])
    up_other, up_mine = two(
        joined(up_half, head_grad).reshape(2, replicas // 4, OWN, FF, D // replicas),
        0,
        lax.rem(lax.div(replica, 2), 2),
    )
    routes = []
    for i in range(n_ctx):
        for k in range(n_fsdp):
            moves = [
                (a, lambda c, f, i=i, k=k: device(flip(c, i), flip(f, k)), a, device)
                for a in range(2)
            ]
            if k == 0 and i % 2 == 0:
                moves.append(
                    (2, lambda c, f, i=i: lax.div(flip(c, i), 2), 2, lambda c, f: lax.div(c, 2))
                )
            if i < 2:
                moves.append((4, lambda c, f, j=4 * i + k: flip(ranked(c, f), j), 4, ranked))
            if k == 0 and i == 4:
                moves.append((3, lambda c, f: slice(None), 3, lambda c, f: slice(None)))
            routes.append((i, k, moves))
    operands = [head_grad, small_grads, output_sum, up_other, gate_down]
    head_grads, small_all, output_all, up_came, gate_down = exchange(
        9, "sum_grads", routes, operands, [(x.shape, x.dtype) for x in operands], 60
    )
    output_grad = jnp.sum(output_all.astype(F32), axis=0)
    up_half, bit = (up_mine, up_came), 4
    while bit < replicas:
        up_half = halve(joined(up_half, up_came), bit)
        bit *= 2
    head_grads = head_grads.reshape(KEY_VALUE_HEADS, parts * n_fsdp, rows, head_width)
    head_grads = jnp.sum(head_grads.astype(F32), axis=1).transpose(1, 0, 2)
    query_grad = head_grads[..., : REP * HEAD_SIZE].reshape(rows, D)
    key_grad = head_grads[..., REP * HEAD_SIZE : (REP + 1) * HEAD_SIZE].reshape(rows, -1)
    value_grad = head_grads[..., (REP + 1) * HEAD_SIZE :].reshape(rows, -1)
    small_sum = jnp.sum(small_all, axis=0)

    up_sum = by_rank([joined(up_half, up_came)])
    (up_sum,) = exchange(
        8,
        "swap_up",
        [
            (i // 4, i % 4, [(0, lambda c, f, i=i: flip(ranked(c, f), i), 0, ranked)])
            for i in range(RANKS)
        ],
        [up_sum],
        [(up_sum.shape, BF16)],
    )

    def by_row(swapped, matrix):
        return swapped[:, matrix].transpose(2, 0, 1, 3).reshape(rows, EXPERTS, FF).astype(F32)

    return (
        layer_out,
        input_grad,
        small_sum[:, EXPERTS],
        query_grad,
        key_grad,
        value_grad,
        output_grad,
        small_sum[:, EXPERTS + 1],
        small_sum[:, :EXPERTS],
        by_row(gate_down, 0),
        by_row(up_sum, 0),
        by_row(gate_down, 1),
    )


def solution(mesh):
    placed = (
        P("fsdp", "ctx", None),
        P("fsdp", None),
        P("fsdp", None),
        P("fsdp", "ctx", None),
        P("fsdp", "ctx"),
        P("fsdp", "ctx", None),
        P("fsdp"),
        P("fsdp", None),
        P("fsdp", None),
        P("fsdp", None),
        P("fsdp", None),
        P("fsdp"),
        P("fsdp", None),
        P("fsdp", None, None),
        P("fsdp", None, None),
        P("fsdp", None, None),
    )
    return jax.shard_map(
        functools.partial(on_device, mesh.shape["ctx"], mesh.shape["fsdp"]),
        mesh=mesh,
        in_specs=placed,
        out_specs=(
            P("fsdp", "ctx", None),
            P("fsdp", "ctx", None),
            P(("ctx", "fsdp")),
            P(("ctx", "fsdp"), None),
            P(("ctx", "fsdp"), None),
            P(("ctx", "fsdp"), None),
            P(("ctx", "fsdp"), None),
            P(("ctx", "fsdp")),
            P(("ctx", "fsdp"), None),
            P(("ctx", "fsdp"), None, None),
            P(("ctx", "fsdp"), None, None),
            P(("ctx", "fsdp"), None, None),
        ),
        check_vma=False,
    )
```

time: 3110 us -> 706 us (0.23)
  the two profiles are of different devices: /device:TPU:0 before, /device:TPU:9 now
where the time goes in v1:
time: 706 us; the launch traced here: 701 us
  Pallas kernels  506 us (72%)
  local copies, waits for them, and re-layouts  79.1 us (11%)
  other arithmetic  37.9 us (5%)
  matrix products  28.4 us (4%)
  waiting for transfers between devices  27.5 us (4%)
  between operations  15.5 us (2%)
    pallas_call x1, Pallas kernels, attention_forward(): pl.pallas_call(functools.partial(attention_forward_kernel, parts, n_ctx),...  149 us
    pallas_call x1, Pallas kernels, attention_backward(): pl.pallas_call(functools.partial(attention_backward_kernel, parts, n_ctx)...  126 us
    pallas_call x1, Pallas kernels, run_experts(): pl.pallas_call(functools.partial(experts_kernel, replicas), name='experts...  123 us
    pallas_call x2, Pallas kernels, exchange(): pl.pallas_call(kernel, name=name, out_shape=[jax.ShapeDtypeStruct(shape,...  109 us
    ppermute x1, waiting for transfers between devices, on_device(): lax.ppermute(send, 'fsdp', [(a, a ^ 2) for a in range(n_fsdp)])  20.8 us
    unnamed x96, local copies, waits for them, and re-layouts  15.3 us
  transfers between devices with their start and end apart: 6, of which 2 were waited for; matrix products, arithmetic and copies ran while one was open for 13% of the time, Pallas kernels for 21%

profile of v1, /device:TPU:9, one launch (start us, length us, event | category | flops | bytes accessed | tf_op | source)
XLA Modules:
  0.0 700.8 jit_solution(12062679072731958229)
XLA Ops:
  8.0 3.4 constant_dynamic-slice_fusion.6
  11.4 2.7 copy.264
  14.2 2.8 copy.265
  17.3 2.7 copy.263
  27.3 148.9 %attention_forward.1 = (bf16[256,1536]{1,0:T(8,128)(2,1)}, bf16[4,32,384]{2,1,0:T(8,128)(2,1)}, bf16[4,384,1536]{2,1,0:T(8,128)(2,1)}, bf16[4,384,512]{2,1,0:T(8...) custom-call(bf16[256,1536]{1,0:T(8,128)(2,1)} %bitcast.177, ...), custom_call_target="tpu_custom_call" | custom-call | bytes 429000000 | tf_op jit(solution)/shard_map/attention_forward/pallas_call | solution.py:714
  178.1 5.0 multiply_reduce_fusion.3
  187.2 4.1 multiply_reduce_fusion
  191.2 122.6 %experts.1 = (f32[256,1664]{1,0:T(8,128)}, bf16[8,256,1536]{2,1,0:T(8,128)(2,1)}, bf16[3,4,2,512,384]{4,3,2,1,0:T(8,128)(2,1)}, bf16[7,256,1664]{2,1,0:T(8,128)(2,1)}, bf16[7,256,1536]{2,1,0:T(8,128)(2,1)}) custom-call(bf16[256,1664]{1,0:T(8,128)(2,1)} %bitcast.192, bf16[256,1536]{1,0:T(8,128)(2,1)} %bitcast.195, ...), custom_call_target="tpu_custom_call" | custom-call | bytes 363000000 | tf_op jit(solution)/shard_map/experts/pallas_call | solution.py:383
  314.9 2.6 multiply_reduce_fusion.1
  319.4 4.3 convolution_convert_fusion
  323.7 3.7 bitcast_convert_fusion
  329.0 6.3 fusion.32
  335.3 2.1 slice.56
  337.5 125.8 %attention_backward.1 = (bf16[8,3,128,128]{3,2,1,0:T(8,128)(2,1)S(1)}, bf16[8,2,128,128]{3,2,1,0:T(8,128)(2,1)S(1)}, bf16[8,3,128,128]{3,2,1,0:T(8,128)(2,1)S(1)...) custom-call(bf16[8,3,128,128]{3,2,1,0:T(8,128)(2,1)} %copy.278.g_own, ...), custom_call_target="tpu_custom_call" | custom-call | bytes 297000000 | tf_op jit(solution)/shard_map/attention_backward/pallas_call | solution.py:969
  466.2 2.3 fusion.2
  472.8 3.2 copy.291
  476.1 2.1 multiply_convert_fusion
  478.2 2.4 copy.292
  480.6 4.3 reshape.339
  484.8 6.3 fusion.5
  491.2 2.5 copy.293
  493.7 2.7 dynamic-slice_bitcast_fusion
  498.4 4.3 constant_dynamic-slice_fusion.3
  507.8 3.9 fusion.36
  517.8 2.4 fusion.1
  521.9 2.7 fusion.15
  528.1 20.8 %collective-permute-done.1 = bf16[4,2,48,1536]{3,2,0,1:T(8,128)(2,1)} collective-permute-done((bf16[4,2,48,1536]{3,2,0,1:T(8,128)(2,1)}, bf16[4,2,48,1536]{3,2,0,1:T(8,128)(2,1)}, u32[]{:S(2)}, u32[]{:S(2)}) %collective-permute-start.1) | collective-permute-done | bytes 1179680 | tf_op jit(solution)/shard_map/ppermute | solution.py:1181
  560.3 6.0 collective-permute-done.2
  568.3 96.5 %sum_grads.1 = (bf16[32,48,320]{2,1,0:T(8,128)(2,1)}, f32[32,48,128]{2,1,0:T(8,128)}, bf16[4,48,1536]{2,1,0:T(8,128)(2,1)}, bf16[1,2,512,384]{3,2,1,0:T(8,128)(2,1)}, bf16[8,2,2,48,512]{4,3,2,1,0:T(8,128)(2,1)}) custom-call(bf16[32,48,320]{2,1,0:T(8,128)(2,1)} %bitcast.191, f32[32,48,128]{2,1,0:T(8,128)} %maximum_maximum_fusion.refs_1_, ...), custom_call_target="tpu_custom_call" | custom-call | bytes 198000000 | tf_op jit(solution)/shard_map/sum_grads/pallas_call | solution.py:89
  668.3 12.3 %swap_up.1 = bf16[8,1,2,48,512]{4,3,2,1,0:T(8,128)(2,1)} custom-call(bf16[8,1,2,48,512]{4,3,2,1,0:T(8,128)(2,1)} %bitcast.202), custom_call_target="tpu_custom_call" | custom-call | bytes 99000000 | tf_op jit(solution)/shard_map/swap_up/pallas_call | solution.py:89
  681.9 2.1 copy.312
  684.4 2.1 copy.311
  (205 shorter events, 69.5 us)
Async XLA Ops:
  7.2 180.0 %all-gather.3.cloned.1.call-start = ((), (), s32[]{:S(2)}) async-start(), calls=%async_computation | async-start | bytes 7077888 | tf_op jit(solution)/shard_map/all_gather | solution.py:1051
  8.0 9.0 %slice-start.2 = ((s8[6291456]{0:T(1024)(128)(4,1)}), s8[4194304]{0:T(1024)(128)(4,1)S(1)}, s32[]{:S(2)}) async-start(s8[6291456]{0:T(1024)(128)(4,1)} %bitcast.217), calls=%async_computation.3 | async-start | bytes 8388608
  11.4 5.5 slice-start.3
  21.6 2.9 copy-start.33
  21.9 4.0 copy-start.37
  21.9 4.0 copy-start.38
  21.9 4.1 copy-start.35
  21.9 4.7 copy-start.34
  177.9 5.2 copy-start.23
  183.1 2.1 copy-start.39
  184.8 2.4 copy-start.13
  314.8 2.6 copy-start.21
  319.4 4.3 copy-start.9
  319.4 4.3 copy-start.24
  335.3 2.2 copy-start
  335.3 2.2 copy-start.7
  335.3 2.2 copy-start.8
  470.5 57.6 %collective-permute-start.4 = (bf16[1,2,512,384]{3,2,1,0:T(8,128)(2,1)}, bf16[1,2,512,384]{3,2,1,0:T(8,128)(2,1)}, u32[]{:S(2)}, u32[]{:S(2)}) collective-permute-start(bf16[1,2,512,384]{3,2,1,0:T(8,128)(2,1)} %constant_dynamic-slice_fusion), channel_id=1, source_target_pairs={{0,16},{4,20},{8,24},{12,28},{16,0},{20,4},{24,8},{28,12},{1,17},{... | collective-permute-start | bytes 2359304 | tf_op jit(solution)/shard_map/ppermute | solution.py:1125
  496.4 59.9 %collective-permute-start.3 = (bf16[2,2,512,384]{3,2,1,0:T(8,128)(2,1)}, bf16[2,2,512,384]{3,2,1,0:T(8,128)(2,1)}, u32[]{:S(2)}, u32[]{:S(2)}) collective-permute-start(bf16[2,2,512,384]{3,2,1,0:T(8,128)(2,1)} %dynamic-slice_bitcast_fusion), channel_id=1, source_target_pairs={{0,8},{4,12},{8,0},{12,4},{16,24},{20,28},{24,16},{28,20},{1,9},{5... | collective-permute-start | bytes 4718600 | tf_op jit(solution)/shard_map/ppermute | solution.py:1125
  504.3 2.4 copy-start.6
  504.3 12.9 %collective-permute-start = (bf16[4,2,2,48,1536]{4,3,0,1,2:T(8,128)(2,1)}, bf16[4,2,2,48,1536]{4,3,0,1,2:T(8,128)(2,1)}, u32[]{:S(2)}, u32[]{:S(2)}) collective-permute-start(bf16[4,2,2,48,1536]{4,3,0,1,2:T(8,128)(2,1)} %bitcast.166), channel_id=1, source_target_pairs={{0,1},{1,0},{2,3},{3,2},{4,5},{5,4},{6,7},{7,6},{8,9},{9,8},{10,11... | collective-permute-start | bytes 7077896 | tf_op jit(solution)/shard_map/ppermute | solution.py:1167
  507.8 3.9 copy-start.25
  507.8 6.6 slice-start
  511.8 2.7 slice-start.1
  520.2 4.4 copy-start.17
  521.3 27.6 %collective-permute-start.1 = (bf16[4,2,48,1536]{3,2,0,1:T(8,128)(2,1)}, bf16[4,2,48,1536]{3,2,0,1:T(8,128)(2,1)}, u32[]{:S(2)}, u32[]{:S(2)}) collective-permute-start(bf16[4,2,48,1536]{3,2,0,1:T(8,128)(2,1)} %dynamic-slice_bitcast_fusion.1), channel_id=1, source_target_pairs={{0,2},{1,3},{2,0},{3,1},{4,6},{5,7},{6,4},{7,5},{8,10},{9,11},{10,... | collective-permute-start | bytes 3538952 | tf_op jit(solution)/shard_map/ppermute | solution.py:1181
  526.7 22.2 %copy-start.18 = (bf16[4,2,2,48,1536]{4,3,0,1,2:T(8,128)(2,1)S(1)}, bf16[4,2,2,48,1536]{4,3,0,1,2:T(8,128)(2,1)}, u32[]{:S(2)}) copy-start(bf16[4,2,2,48,1536]{4,3,0,1,2:T(8,128)(2,1)} %copy-done.17) | copy-start | bytes 7077892
  528.1 25.3 %copy-start.20 = (bf16[2,2,512,384]{3,2,1,0:T(8,128)(2,1)S(1)}, bf16[2,2,512,384]{3,2,1,0:T(8,128)(2,1)}, u32[]{:S(2)}) copy-start(bf16[2,2,512,384]{3,2,1,0:T(8,128)(2,1)} %copy-done.19) | copy-start | bytes 4718596
  551.4 14.9 %collective-permute-start.2 = (bf16[4,48,1536]{2,1,0:T(8,128)(2,1)}, bf16[4,48,1536]{2,1,0:T(8,128)(2,1)}, u32[]{:S(2)}, u32[]{:S(2)}) collective-permute-start(bf16[4,48,1536]{2,1,0:T(8,128)(2,1)} %dynamic-slice_bitcast_fusion.2), channel_id=1, source_target_pairs={{0,4},{4,0},{8,12},{12,8},{16,20},{20,16},{24,28},{28,24},{1,5},{5... | collective-permute-start | bytes 1769480 | tf_op jit(solution)/shard_map/ppermute | solution.py:1183
  555.1 2.5 copy-start.15
  688.6 2.7 copy-start.31
  688.8 3.3 copy-start.30
  (18 other events, 26.3 us)
Sparse Core Ops, SparseCore 0:
  10.2 145.2 all-gather.2

commit v2 on v1

--- a/solution.py
+++ b/solution.py
@@ -753,21 +753,41 @@
 
 def attention_backward_kernel(
     parts, n_ctx, g_own, q_ref, kv_ref, seg_ref, code_ref, full_ref, log_ref, cos_ref, sin_ref,
-    grads, mix, dq_ref, dkv_ref, dq_back, dkv_back, gate_came, down_keep, down_came, mix_in,
-    g_ref, total, kept, came,
+    tok, gain, resid_grad, grads, mix, output_part, tokens_all, q_full, k_full, v_full,
+    input_grad, gain_grad, output_sum, gate_came, down_keep, down_came, mix_in, head_in,
+    g_ref, total, kept, came, dq_ref, dkv_ref, dq_back, dkv_back, w_q, w_k, w_v, grad_qkv, grad_in,
+    token_buf, field, head_acc, head_out, output_keep, output_came, output_x, output_pair,
     send_g, recv_g, send_q, recv_q, send_kv, recv_kv, send_mix, recv_mix, send_half, recv_half, here,
+    send_out, recv_out, send_head, recv_head, load_t,
 ):
     c, f = lax.axis_index("ctx"), lax.axis_index("fsdp")
     head, part = lax.div(c, parts), lax.rem(c, parts)
     rows = REP * BLOCK
     wide = 2 * HEAD_SIZE
     barrier = pltpu.get_barrier_semaphore()
-    peers = [(i, 0) for i in range(1, n_ctx)]
-    peers += [(i // 4, i % 4) for i in range(1, RANKS) if i % 4]
+    peers = [(i, k) for i in range(n_ctx) for k in range(4) if i or k]
     for dc, df in peers:
         pl.semaphore_signal(
             barrier, inc=1, device_id=(flip(c, dc), flip(f, df)), device_id_type=MESH
         )
+    pair, x_bit, core_bit = lax.rem(c, 2), lax.div(f, 2), lax.rem(f, 2)
+    loads = [
+        pltpu.make_async_copy(source, target, here.at[5 + i])
+        for i, (source, target) in enumerate(
+            (
+                (q_full, w_q), (k_full, w_k), (v_full, w_v),
+                (output_part.at[:, :, :, core_bit], output_keep),
+            )
+        )
+    ]
+
+    def bring(b):
+        return pltpu.make_async_copy(
+            tokens_all.at[b], token_buf.at[lax.rem(b, 2)], load_t.at[lax.rem(b, 2)]
+        )
+
+    for copy in loads + [bring(0), bring(1)]:
+        copy.start()
     first = pltpu.make_async_copy(g_own.at[head], g_ref.at[head], here.at[0])
     first.start()
     pl.semaphore_wait(barrier, len(peers))
@@ -797,6 +817,19 @@
     down_halving.start()
     keeping = pltpu.make_async_copy(grads.at[2, pl.ds(mine * half, half)], kept, here.at[3])
     keeping.start()
+    output_stages = [
+        pltpu.make_async_remote_copy(
+            source, target, send_out.at[i], recv_out.at[i], device_id=device, device_id_type=MESH
+        )
+        for i, (source, target, device) in enumerate(
+            (
+                (output_part.at[:, :, :, 1 - core_bit], output_came, (c, flip(f, 1))),
+                (output_keep.at[:, :, 1 - x_bit], output_x, (c, flip(f, 2))),
+                (output_x.at[:, 1 - pair], output_pair, (flip(c, 1), f)),
+            )
+        )
+    ]
+    output_stages[0].start()
     returns = []
     for i in range(1, RANKS):
         returns.append(
@@ -921,6 +954,75 @@
     leaving = pltpu.make_async_copy(kept.at[pl.ds(second * quarter, quarter)], down_keep, here.at[4])
     leaving.start()
 
+    planes = output_keep.shape[0]
+
+    def plus(mine, came):
+        return (mine.astype(F32) + came.astype(F32)).astype(BF16)
+
+    loads[3].wait()
+    output_stages[0].wait_recv()
+
+    def cores(i, nothing):
+        r, p, x = lax.div(i, 4), lax.rem(lax.div(i, 2), 2), lax.rem(i, 2)
+        output_keep[r, p, x] = plus(output_keep[r, p, x], output_came[r, p, x])
+        return nothing
+
+    lax.fori_loop(0, planes * 4, cores, 0)
+    output_stages[1].start()
+
+    low = lax.broadcasted_iota(jnp.int32, (BLOCK, wide), 1) < HEAD_SIZE
+
+    def side_by_side(even, odd):
+        even, odd = even.astype(F32), odd.astype(F32)
+        return (
+            jnp.where(low, even, pltpu.roll(odd, HEAD_SIZE, 1)),
+            jnp.where(low, pltpu.roll(even, HEAD_SIZE, 1), odd),
+        )
+
+    head_acc[...] = jnp.zeros_like(head_acc)
+
+    def head_weights(b, nothing):
+        bring(b).wait()
+        block = token_buf[lax.rem(b, 2)].reshape(SEQS * BLOCK, D)
+        wide_block = block.astype(F32)
+        scales = lax.rsqrt(jnp.mean(wide_block * wide_block, axis=1, keepdims=True) + EPS)
+        j = lax.div(b, parts)
+        have = jnp.where(lax.rem(b, parts) == part, 1.0, 0.0)
+        heads = [dq_ref[j, r].astype(F32) * have for r in range(REP)] + [dkv_ref[b, 0], dkv_ref[b, 1]]
+        heads.append(jnp.zeros((BLOCK, wide), F32))
+        for m in range((REP + 3) // 2):
+            for s, value in enumerate(side_by_side(heads[2 * m], heads[2 * m + 1])):
+                at = slice(s * BLOCK, (s + 1) * BLOCK)
+                field[at, m * wide : (m + 1) * wide] = (value * scales[at]).astype(BF16)
+        head_acc[...] += lax.dot_general(
+            block, field[...], (((0,), (0,)), ((), ())), preferred_element_type=F32
+        )
+
+        @pl.when(b + 2 < n_ctx)
+        def _():
+            bring(b + 2).start()
+
+        return nothing
+
+    lax.fori_loop(0, n_ctx, head_weights, 0)
+    slab = D // (n_ctx * 4)
+    for d in range(n_ctx * 4):
+        head_out[d] = head_acc[d * slab : (d + 1) * slab, : head_out.shape[2]].astype(BF16)
+    me = c * 4 + f
+    head_stays = pltpu.make_async_copy(head_out.at[me], head_in.at[me], here.at[9])
+    head_stays.start()
+    to_all = []
+    for number, (i, k) in enumerate(peers):
+        peer_c, peer_f = flip(c, i), flip(f, k)
+        to_all.append(
+            pltpu.make_async_remote_copy(
+                head_out.at[peer_c * 4 + peer_f], head_in.at[me],
+                send_head.at[number], recv_head.at[number],
+                device_id=(peer_c, peer_f), device_id_type=MESH,
+            )
+        )
+        to_all[-1].start()
+
     def came_query(h, nothing):
         @pl.when(h != head)
         def _():
@@ -951,49 +1053,132 @@
 
     lax.fori_loop(0, KEY_VALUE_HEADS, came_query, 0)
     lax.fori_loop(0, n_ctx, came_key, 0)
+
+    def head_of(h):
+        if h < QUERY_HEADS:
+            return dq_back[h // REP, h % REP]
+        kind, h = (h - QUERY_HEADS) // KEY_VALUE_HEADS, (h - QUERY_HEADS) % KEY_VALUE_HEADS
+        value = dkv_back[h * parts, kind]
+        if parts > 1:
+            value = value.astype(F32)
+            for p in range(1, parts):
+                value = value + dkv_back[h * parts + p, kind].astype(F32)
+        return value
+
+    for m in range((QUERY_HEADS + 2 * KEY_VALUE_HEADS) // 2):
+        for s, value in enumerate(side_by_side(head_of(2 * m), head_of(2 * m + 1))):
+            grad_qkv[s * BLOCK : (s + 1) * BLOCK, m * wide : (m + 1) * wide] = value.astype(BF16)
+    for copy in loads[:3]:
+        copy.wait()
+    depth = D // 4
+    for b in range(4):
+        made, at = 0.0, 0
+        for weight in (w_q, w_k, w_v):
+            width = weight.shape[2]
+            made = made + lax.dot_general(
+                grad_qkv[:, at : at + width], weight[b], (((1,), (1,)), ((), ())),
+                preferred_element_type=F32,
+            )
+            at += width
+        grad_in[:, b * depth : (b + 1) * depth] = made
+    x = tok[...].astype(F32)
+    scale = lax.rsqrt(jnp.mean(x * x, axis=1, keepdims=True) + EPS)
+    gain_grad[...] = jnp.sum(grad_in[...] * x * scale, axis=0, keepdims=True)
+    weighted = grad_in[...] * gain[...]
+    input_grad[...] = (
+        resid_grad[...]
+        + scale * weighted
+        - x * (scale * scale * scale) * jnp.mean(weighted * x, axis=1, keepdims=True)
+    ).astype(BF16)
+
+    output_stages[1].wait_recv()
+
+    def over_x(i, nothing):
+        r, p = lax.div(i, 2), lax.rem(i, 2)
+        output_x[r, p] = plus(output_keep[r, p, x_bit], output_x[r, p])
+        return nothing
+
+    lax.fori_loop(0, planes * 2, over_x, 0)
+    output_stages[2].start()
+    output_stages[2].wait_recv()
+
+    def over_pair(r, nothing):
+        output_sum[r] = plus(output_x[r, pair], output_pair[r])
+        return nothing
+
+    lax.fori_loop(0, planes, over_pair, 0)
     for copy in to_heads:
         copy.wait_send()
-    for copy in returns + [gate_halving, down_second, leaving]:
+    for copy in returns + to_all + [gate_halving, down_second, leaving, head_stays]:
         copy.wait()
+    for copy in output_stages:
+        copy.wait_send()
     down_halving.wait_send()
 
 
 def attention_backward(
-    cid, parts, n_ctx, g_own, q, kv, segq, codes, full, logs, cosine, sine, grads, mix
+    cid, parts, n_ctx, g_own, q, kv, segq, codes, full, logs, cosine, sine,
+    tok, gain, resid_grad, grads, mix, output_part, tokens_all, q_full, k_full, v_full,
 ):
     wide = 2 * HEAD_SIZE
     anywhere = pl.BlockSpec(memory_space=pl.ANY)
     inside = pl.BlockSpec(memory_space=pltpu.VMEM)
     dma = pltpu.SemaphoreType.DMA
     others = max(n_ctx // parts - 1, 1)
+    devices, planes = n_ctx * 4, n_ctx // 2
+    slab, head_width = D // devices, (REP + 2) * HEAD_SIZE
+    half = (grads.shape[1] // 2,) + grads.shape[2:]
+    quarter = (grads.shape[1] // 4,) + grads.shape[2:]
+    columns = q_full.shape[2] + k_full.shape[2] + v_full.shape[2]
     return pl.pallas_call(
         functools.partial(attention_backward_kernel, parts, n_ctx),
         name="attention_backward",
         out_shape=[
-            jax.ShapeDtypeStruct(q.shape, BF16),
-            jax.ShapeDtypeStruct(kv.shape, BF16),
-            jax.ShapeDtypeStruct(q.shape, BF16),
-            jax.ShapeDtypeStruct(kv.shape, BF16),
-            jax.ShapeDtypeStruct((grads.shape[1] // 2,) + grads.shape[2:], BF16),
-            jax.ShapeDtypeStruct((grads.shape[1] // 4,) + grads.shape[2:], BF16),
-            jax.ShapeDtypeStruct((grads.shape[1] // 4,) + grads.shape[2:], BF16),
+            jax.ShapeDtypeStruct(tok.shape, BF16),
+            jax.ShapeDtypeStruct((1, D), F32),
+            jax.ShapeDtypeStruct((planes, slab, D), BF16),
+            jax.ShapeDtypeStruct(half, BF16),
+            jax.ShapeDtypeStruct(quarter, BF16),
+            jax.ShapeDtypeStruct(quarter, BF16),
             jax.ShapeDtypeStruct((RANKS - 1,) + mix.shape[1:], BF16),
+            jax.ShapeDtypeStruct((devices, slab, head_width), BF16),
         ],
-        in_specs=[anywhere] + [inside] * 8 + [anywhere] * 2,
-        out_specs=[inside] * 2 + [anywhere] * 6,
+        in_specs=[anywhere] + [inside] * 11 + [anywhere] * 7,
+        out_specs=[inside] * 3 + [anywhere] * 5,
         scratch_shapes=[
             pltpu.VMEM(q.shape, BF16),
             pltpu.VMEM((n_ctx, 2, BLOCK, wide), F32),
-            pltpu.VMEM((grads.shape[1] // 2,) + grads.shape[2:], BF16),
-            pltpu.VMEM((grads.shape[1] // 2,) + grads.shape[2:], BF16),
+            pltpu.VMEM(half, BF16),
+            pltpu.VMEM(half, BF16),
+            pltpu.VMEM(q.shape, BF16),
+            pltpu.VMEM(kv.shape, BF16),
+            pltpu.VMEM(q.shape, BF16),
+            pltpu.VMEM(kv.shape, BF16),
+            pltpu.VMEM(q_full.shape, BF16),
+            pltpu.VMEM(k_full.shape, BF16),
+            pltpu.VMEM(v_full.shape, BF16),
+            pltpu.VMEM((SEQS * BLOCK, columns), BF16),
+            pltpu.VMEM((SEQS * BLOCK, D), F32),
+            pltpu.VMEM((2, SEQS, BLOCK, D), BF16),
+            pltpu.VMEM((SEQS * BLOCK, 3 * wide), BF16),
+            pltpu.VMEM((D, 3 * wide), F32),
+            pltpu.VMEM((devices, slab, head_width), BF16),
+            pltpu.VMEM((planes, 2, 2, slab, D), BF16),
+            pltpu.VMEM((planes, 2, 2, slab, D), BF16),
+            pltpu.VMEM((planes, 2, slab, D), BF16),
+            pltpu.VMEM((planes, slab, D), BF16),
             dma((others,)), dma((others,)), dma((KEY_VALUE_HEADS,)), dma((KEY_VALUE_HEADS,)),
-            dma((n_ctx,)), dma((n_ctx,)), dma((RANKS - 1,)), dma((RANKS - 1,)), dma((3,)), dma((3,)), dma((5,)),
+            dma((n_ctx,)), dma((n_ctx,)), dma((RANKS - 1,)), dma((RANKS - 1,)), dma((3,)), dma((3,)),
+            dma((10,)), dma((3,)), dma((3,)), dma((devices - 1,)), dma((devices - 1,)), dma((2,)),
         ],
         compiler_params=pltpu.CompilerParams(
-            collective_id=cid, has_side_effects=True, vmem_limit_bytes=48 << 20
+            collective_id=cid, has_side_effects=True, vmem_limit_bytes=60 << 20
         ),
-        cost_estimate=lasting(90),
-    )(g_own, q, kv, segq, codes, full, logs, cosine, sine, grads, mix)
+        cost_estimate=lasting(125),
+    )(
+        g_own, q, kv, segq, codes, full, logs, cosine, sine, tok, gain, resid_grad,
+        grads, mix, output_part, tokens_all, q_full, k_full, v_full,
+    )
 
 
 def rope_tables(positions):
@@ -1151,8 +1336,6 @@
     grad_attn = grad_attn.astype(BF16)
     grad_output_w = jnp.einsum("sgd,sgq->dq", grad_resid_low, attn_out, preferred_element_type=F32)
     rows = D // (n_ctx * n_fsdp)
-    x_bit, core_bit = lax.div(f_index, 2), lax.rem(f_index, 2)
-
     def two(field, axis, bit):
         return (
             lax.dynamic_index_in_dim(field, 1 - bit, axis, keepdims=False),
@@ -1163,88 +1346,21 @@
         return (mine.astype(F32) + came.astype(F32)).astype(BF16)
 
     output_part = grad_output_w.astype(BF16).reshape(replicas, 2, 2, 2, rows, D)
-    send, output_mine = two(output_part, 3, core_bit)
-    output_came = lax.ppermute(send, "fsdp", [(a, a ^ 1) for a in range(n_fsdp)])
-
-    dq_heads, dkv_heads, dq_back, dkv_back, gate_came, down_keep, down_came, mix_in = attention_backward(
+
+    input_grad, gain_grad, output_sum, gate_came, down_keep, down_came, mix_in, head_grads = attention_backward(
         6, parts, n_ctx, heads_out(grad_attn, REP), q_all, kv_all, segq, codes, head_full, head_logs,
-        all_cosine, all_sine, own_grads, mix_part,
+        all_cosine, all_sine, tokens.reshape(SEQS * BLOCK, D), gain_first[None],
+        grad_resid.reshape(SEQS * BLOCK, D), own_grads, mix_part, output_part, tokens_all,
+        full_query, full_key, full_value,
     )
+    input_grad = input_grad.reshape(SEQS, BLOCK, D)
     layer_out = (
         residual.reshape(SEQS * BLOCK, D) + mix_part[0].astype(F32) + jnp.sum(mix_in.astype(F32), axis=0)
     ).astype(BF16).reshape(SEQS, BLOCK, D)
     gate_keep = own_grads[0].reshape((2, replicas // 2, OWN, FF, D // replicas))
     gate_half = (lax.dynamic_index_in_dim(gate_keep, lax.rem(replica, 2), 0, keepdims=False), gate_came)
-    up_half = halve(tie(own_grads[1], dq_back), 1)
-    gate_half = halve(joined(gate_half, dq_back), 2)
-    send, output_mine = two(summed(output_mine, output_came), 2, x_bit)
-    output_came = lax.ppermute(send, "fsdp", [(a, a ^ 2) for a in range(n_fsdp)])
-    send, output_mine = two(summed(output_mine, output_came), 1, pair)
-    output_came = lax.ppermute(send, "ctx", [(a, a ^ 1) for a in range(n_ctx)])
-    down_half, bit = (down_keep, down_came), 4
-    while bit < replicas:
-        down_half = halve(joined(down_half, dq_back), bit)
-        gate_half = halve(joined(gate_half, dq_back), bit)
-        bit *= 2
-
-    tokens_f = tokens_all.astype(F32)
-    scale_all = lax.rsqrt(jnp.mean(tokens_f * tokens_f, axis=-1) + EPS)
-
-    def head_weights(field, inputs, scales):
-        blocks, per = field.shape[:2]
-        field = field.reshape(blocks, per, BLOCK, SEQS, HEAD_SIZE).transpose(0, 3, 2, 1, 4)
-        field = (field.astype(F32) * scales[..., None, None]).astype(BF16)
-        made = jnp.dot(
-            inputs.reshape(blocks * SEQS * BLOCK, D).T,
-            field.reshape(blocks * SEQS * BLOCK, per * HEAD_SIZE),
-            preferred_element_type=F32,
-        )
-        return made * gain_first[:, None]
-
-    if parts == 1:
-        head_grad = head_weights(jnp.concatenate([dq_heads, dkv_heads], axis=1), tokens_all, scale_all)
-    else:
-        tokens_part, scale_part = (
-            lax.dynamic_index_in_dim(
-                x.reshape((KEY_VALUE_HEADS, parts) + x.shape[1:]), part, 1, keepdims=False
-            )
-            for x in (tokens_all, scale_all)
-        )
-        head_grad = jnp.concatenate(
-            [
-                head_weights(dq_heads, tokens_part, scale_part),
-                head_weights(dkv_heads, tokens_all, scale_all),
-            ],
-            axis=1,
-        )
-    head_width = (REP + 2) * HEAD_SIZE
-    head_grad = head_grad.astype(BF16).reshape(n_ctx * n_fsdp, rows, head_width)
-    dkv_back = dkv_back.reshape(KEY_VALUE_HEADS, parts, 2, BLOCK, SEQS * HEAD_SIZE)
-    if parts == 1:
-        dkv_back = dkv_back[:, 0]
-    else:
-        dkv_back = jnp.sum(dkv_back.astype(F32), axis=1).astype(BF16)
-    grad_in = sum(
-        jnp.einsum("sgq,dq->sgd", heads_in(grad), weight.reshape(D, -1), preferred_element_type=F32)
-        for grad, weight in (
-            (dq_back, full_query), (dkv_back[:, :1], full_key), (dkv_back[:, 1:], full_value)
-        )
-    )
-    weighted_one = gain_first * grad_in
-    grad_gain_first = jnp.sum(grad_in * inputs_f * scale_one, axis=(0, 1))
-    cube_one = scale_one * scale_one * scale_one
-    input_grad = (
-        grad_resid
-        + scale_one * weighted_one
-        - inputs_f * cube_one * jnp.mean(weighted_one * inputs_f, axis=-1, keepdims=True)
-    ).astype(BF16)
     small_grads = jnp.concatenate(
-        [
-            grad_router,
-            grad_gain_first[:, None],
-            grad_gain_second[:, None],
-            jnp.zeros((D, 128 - EXPERTS - 2), F32),
-        ],
+        [grad_router, gain_grad.T, grad_gain_second[:, None], jnp.zeros((D, 128 - EXPERTS - 2), F32)],
         axis=1,
     ).reshape(n_ctx * n_fsdp, rows, 128)
 
@@ -1258,53 +1374,84 @@
         field = jnp.stack(sums).reshape(len(sums), OWN, FF, RANKS, rows)
         return field.transpose(3, 0, 1, 4, 2)
 
-    output_sum = summed(output_mine, output_came)
-    gate_down = by_rank([joined(gate_half, head_grad), joined(down_half, head_grad)])
-    up_other, up_mine = two(
-        joined(up_half, head_grad).reshape(2, replicas // 4, OWN, FF, D // replicas),
-        0,
-        lax.rem(lax.div(replica, 2), 2),
-    )
+    def quarters(halves):
+        return two(
+            summed(*halves).reshape(2, replicas // 4, OWN, FF, D // replicas),
+            0,
+            lax.rem(lax.div(replica, 2), 2),
+        )
+
+    def whole(keep, came):
+        bit = 4
+        while bit < replicas:
+            keep, came = halve(summed(keep, came), bit)
+            bit *= 2
+        return summed(keep, came)
+
+    everything = lambda c, f: slice(None)
+
+    def kept_half(grad):
+        grad = grad.reshape((2, replicas // 2) + grad.shape[1:])
+        return lax.dynamic_index_in_dim(grad, lax.rem(replica, 2), 0, keepdims=False)
+
+    gate_other, gate_mine = quarters((kept_half(own_grads[0]), gate_came))
     routes = []
     for i in range(n_ctx):
         for k in range(n_fsdp):
-            moves = [
-                (a, lambda c, f, i=i, k=k: device(flip(c, i), flip(f, k)), a, device)
-                for a in range(2)
-            ]
+            moves = []
+            if k == 0 and i == 4:
+                moves.append((2, everything, 2, everything))
+            if k == 0 and i == 2:
+                moves.append(
+                    (
+                        3,
+                        lambda c, f: (
+                            1,
+                            pl.ds((1 - lax.rem(lax.div(c, 2), 2)) * (replicas // 2), replicas // 2),
+                        ),
+                        3,
+                        everything,
+                    )
+                )
+            moves.append(
+                (0, lambda c, f, i=i, k=k: device(flip(c, i), flip(f, k)), 0, device)
+            )
             if k == 0 and i % 2 == 0:
                 moves.append(
-                    (2, lambda c, f, i=i: lax.div(flip(c, i), 2), 2, lambda c, f: lax.div(c, 2))
+                    (1, lambda c, f, i=i: lax.div(flip(c, i), 2), 1, lambda c, f: lax.div(c, 2))
                 )
-            if i < 2:
-                moves.append((4, lambda c, f, j=4 * i + k: flip(ranked(c, f), j), 4, ranked))
-            if k == 0 and i == 4:
-                moves.append((3, lambda c, f: slice(None), 3, lambda c, f: slice(None)))
             routes.append((i, k, moves))
-    operands = [head_grad, small_grads, output_sum, up_other, gate_down]
-    head_grads, small_all, output_all, up_came, gate_down = exchange(
-        9, "sum_grads", routes, operands, [(x.shape, x.dtype) for x in operands], 60
+    routes.sort(key=lambda r: not (r[1] == 0 and r[0] in (2, 4)))
+    operands = [small_grads, output_sum, gate_other, own_grads]
+    outs = [(x.shape, x.dtype) for x in operands[:3]] + [(gate_came.shape, BF16)]
+    small_all, output_all, gate_came, up_came = exchange(9, "sum_grads", routes, operands, outs, 60)
+    output_grad = jnp.sum(output_all.astype(F32), axis=0)
+    up_other, up_mine = quarters((kept_half(own_grads[1]), up_came))
+    gate_down = by_rank([whole(gate_mine, gate_came), whole(down_keep, down_came)])
+    routes = [
+        (i // 4, i % 4, [(0, lambda c, f, i=i: flip(ranked(c, f), i), 0, ranked)]) for i in range(RANKS)
+    ]
+    gate_down, up_came = exchange(
+        10,
+        "swap_gate_down",
+        [(4, 0, [(1, everything, 1, everything)])] + routes,
+        [gate_down, up_other],
+        [(gate_down.shape, BF16), (up_other.shape, BF16)],
+        40,
     )
-    output_grad = jnp.sum(output_all.astype(F32), axis=0)
-    up_half, bit = (up_mine, up_came), 4
-    while bit < replicas:
-        up_half = halve(joined(up_half, up_came), bit)
-        bit *= 2
-    head_grads = head_grads.reshape(KEY_VALUE_HEADS, parts * n_fsdp, rows, head_width)
-    head_grads = jnp.sum(head_grads.astype(F32), axis=1).transpose(1, 0, 2)
+    head_grads = head_grads.reshape(KEY_VALUE_HEADS, parts * n_fsdp, rows, (REP + 2) * HEAD_SIZE)
+    own_gain = lax.dynamic_slice_in_dim(gain_first, device(c_index, f_index) * rows, rows, 0)
+    head_grads = jnp.sum(head_grads.astype(F32), axis=1).transpose(1, 0, 2) * own_gain[:, None, None]
     query_grad = head_grads[..., : REP * HEAD_SIZE].reshape(rows, D)
     key_grad = head_grads[..., REP * HEAD_SIZE : (REP + 1) * HEAD_SIZE].reshape(rows, -1)
     value_grad = head_grads[..., (REP + 1) * HEAD_SIZE :].reshape(rows, -1)
     small_sum = jnp.sum(small_all, axis=0)
 
-    up_sum = by_rank([joined(up_half, up_came)])
+    up_sum = by_rank([whole(up_mine, up_came)])
     (up_sum,) = exchange(
         8,
         "swap_up",
-        [
-            (i // 4, i % 4, [(0, lambda c, f, i=i: flip(ranked(c, f), i), 0, ranked)])
-            for i in range(RANKS)
-        ],
+        routes,
         [up_sum],
         [(up_sum.shape, BF16)],
     )

time: 706 us -> 695 us (0.984)
  the two profiles are of different devices: /device:TPU:9 before, /device:TPU:0 now
where the time goes in v2:
time: 695 us; the launch traced here: 686 us
  Pallas kernels  565 us (81%)
  local copies, waits for them, and re-layouts  59.7 us (9%)
  other arithmetic  28.3 us (4%)
  matrix products  17.2 us (2%)
  between operations  14.8 us (2%)
    pallas_call x1, Pallas kernels, attention_backward(): pl.pallas_call(functools.partial(attention_backward_kernel, parts, n_ctx)...  161 us
    pallas_call x1, Pallas kernels, attention_forward(): pl.pallas_call(functools.partial(attention_forward_kernel, parts, n_ctx),...  150 us
    pallas_call x3, Pallas kernels, exchange(): pl.pallas_call(kernel, name=name, out_shape=[jax.ShapeDtypeStruct(shape,...  130 us
    pallas_call x1, Pallas kernels, run_experts(): pl.pallas_call(functools.partial(experts_kernel, replicas), name='experts...  123 us
  transfers between devices with their start and end apart: 1, of which 0 were waited for; matrix products, arithmetic and copies ran while one was open for 5% of the time, Pallas kernels for 22%

profile of v2, /device:TPU:0, one launch (start us, length us, event | category | flops | bytes accessed | tf_op | source)
XLA Modules:
  0.0 685.8 jit_solution(12515140079951885143)
XLA Ops:
  18.2 2.4 constant_dynamic-slice_fusion.6
  20.6 2.7 copy.203
  23.3 1.8 copy-done.15
  25.9 2.8 copy.205
  28.7 2.7 copy.204
  32.8 150.5 %attention_forward.1 = (bf16[256,1536]{1,0:T(8,128)(2,1)}, bf16[4,32,384]{2,1,0:T(8,128)(2,1)}, bf16[4,384,1536]{2,1,0:T(8,128)(2,1)}, bf16[4,384,512]{2,1,0:T(8...) custom-call(bf16[256,1536]{1,0:T(8,128)(2,1)} %bitcast.122, ...), custom_call_target="tpu_custom_call" | custom-call | bytes 429000000 | tf_op jit(solution)/shard_map/attention_forward/pallas_call | solution.py:714
  183.3 1.6 copy.209
  185.2 4.0 multiply_reduce_fusion.2
  193.6 123.3 %experts.1 = (f32[256,1664]{1,0:T(8,128)}, bf16[8,256,1536]{2,1,0:T(8,128)(2,1)}, bf16[3,4,2,512,384]{4,3,2,1,0:T(8,128)(2,1)}, bf16[7,256,1664]{2,1,0:T(8,128)(2,1)}, bf16[7,256,1536]{2,1,0:T(8,128)(2,1)}) custom-call(bf16[256,1664]{1,0:T(8,128)(2,1)} %bitcast.130, bf16[256,1536]{1,0:T(8,128)(2,1)} %bitcast.131, ...), custom_call_target="tpu_custom_call" | custom-call | bytes 363000000 | tf_op jit(solution)/shard_map/experts/pallas_call | solution.py:383
  317.9 2.6 multiply_reduce_fusion
  322.5 4.3 convolution_convert_fusion
  326.9 3.7 bitcast_convert_fusion
  332.2 2.1 slice.50
  334.2 161.3 %attention_backward.1 = (bf16[256,1536]{1,0:T(8,128)(2,1)}, f32[1,1536]{1,0:T(1,128)}, bf16[4,48,1536]{2,1,0:T(8,128)(2,1)}, bf16[2,2,512,384]{3,2,1,0:T(8,128)(...) custom-call(bf16[8,3,128,128]{3,2,1,0:T(8,128)(2,1)} %copy.220.g_own, ...), custom_call_target="tpu_custom_call" | custom-call | bytes 412500000 | tf_op jit(solution)/shard_map/attention_backward/pallas_call | solution.py:1133
  495.5 1.5 convert_reduce_fusion.1
  497.3 6.5 fusion.21
  503.8 1.5 concatenate.36
  505.3 4.6 convert_reduce_fusion
  512.7 1.5 concatenate.35
  516.7 2.3 fusion.2
  520.7 1.4 maximum_maximum_fusion.refs_0_
  522.0 80.1 %sum_grads.1 = (f32[32,48,128]{2,1,0:T(8,128)}, bf16[4,48,1536]{2,1,0:T(8,128)(2,1)}, bf16[1,2,512,384]{3,2,1,0:T(8,128)(2,1)}, bf16[2,2,512,384]{3,2,1,0:T(8,128)(2,1)}) custom-call(f32[32,48,128]{2,1,0:T(8,128)} %maximum_maximum_fusion.refs_0_, bf16[4,48,1536]{2,1,0:T(8,128)(2,1)} %get-tuple-element.61.refs_1_, ...), custom_call_target="tpu_custom_call" | custom-call | bytes 198000000 | tf_op jit(solution)/shard_map/sum_grads/pallas_call | solution.py:89
  602.1 2.2 add_convert_fusion.2
  604.3 2.4 copy.230
  609.0 2.3 fusion.1
  614.1 37.6 %swap_gate_down.1 = (bf16[8,2,2,48,512]{4,3,2,1,0:T(8,128)(2,1)}, bf16[1,2,512,384]{3,2,1,0:T(8,128)(2,1)}) custom-call(bf16[8,2,2,48,512]{4,3,2,1,0:T(8,128)(2,1)} %copy_bitcast_fusion.refs_0_, bf16[1,2,512,384]{3,2,1,0:T(8,128)(2,1)} %constant_dynamic-slice_fusion.refs_1_), custom_call_target="tpu_custom_call" | custom-call | bytes 132000000 | tf_op jit(solution)/shard_map/swap_gate_down/pallas_call | solution.py:89
  651.7 2.2 add_convert_fusion
  654.0 1.4 copy.234
  656.3 12.3 %swap_up.1 = bf16[8,1,2,48,512]{4,3,2,1,0:T(8,128)(2,1)} custom-call(bf16[8,1,2,48,512]{4,3,2,1,0:T(8,128)(2,1)} %bitcast.137), custom_call_target="tpu_custom_call" | custom-call | bytes 99000000 | tf_op jit(solution)/shard_map/swap_up/pallas_call | solution.py:89
  670.0 2.1 copy.238
  672.5 2.1 copy.239
  674.5 2.1 copy.237
  (138 shorter events, 39.4 us)
Async XLA Ops:
  7.2 186.4 %all-gather.3.cloned.1.call-start = ((), (), s32[]{:S(2)}) async-start(), calls=%async_computation | async-start | bytes 7077888 | tf_op jit(solution)/shard_map/all_gather | solution.py:1236
  16.9 6.5 slice-start.1
  18.2 5.1 slice-start.2
  20.6 4.5 copy-start.15
  28.7 2.8 copy-start.22
  28.7 2.8 copy-start.24
  28.7 3.4 copy-start.23
  183.3 1.7 copy-start.21
  183.3 1.8 copy-start.3
  185.0 4.2 copy-start.13
  189.1 1.1 copy-start
  317.9 3.9 copy-start.6
  320.6 1.5 copy-start.1
  322.5 4.3 copy-start.2
  322.5 4.3 copy-start.14
  497.2 6.6 copy-start.5
  505.3 5.5 slice-start
  509.9 2.7 copy-start.25
  510.0 4.2 copy-start.19
  516.7 3.3 copy-start.12
  519.0 1.4 copy-start.10
  519.0 1.6 copy-start.11
  604.3 2.4 copy-start.18
  604.3 3.8 copy-start.20
  611.2 1.4 copy-start.8
  611.2 1.6 copy-start.9
  670.0 2.1 copy-start.16
  674.5 2.1 copy-start.4
  674.5 2.1 copy-start.7
  676.6 1.3 copy-start.17
Sparse Core Ops, SparseCore 0:
  10.2 152.2 all-gather.2

commit v3 on v2

--- a/solution.py
+++ b/solution.py
@@ -41,65 +41,6 @@
 
 def lasting(microseconds):
     return pl.CostEstimate(flops=0, bytes_accessed=int(microseconds * 3.3e6), transcendentals=0)
-
-
-def exchange(cid, name, routes, operands, outs, microseconds=30):
-    remote = [r for r in routes if r[0] or r[1]]
-    local = [r for r in routes if not (r[0] or r[1])]
-    amount = sum(len(r[2]) for r in remote)
-    local_amount = sum(len(r[2]) for r in local)
-
-    def kernel(*refs):
-        ins = refs[: len(operands)]
-        out = refs[len(operands) : len(operands) + len(outs)]
-        send, recv, own = refs[len(operands) + len(outs) :]
-        c, f = lax.axis_index("ctx"), lax.axis_index("fsdp")
-        barrier = pltpu.get_barrier_semaphore()
-        for dc, df, _ in remote:
-            pl.semaphore_signal(
-                barrier, inc=1, device_id=(flip(c, dc), flip(f, df)), device_id_type=MESH
-            )
-        copies = []
-        for dc, df, moves in local:
-            for a, src, b, dst in moves:
-                copy = pltpu.make_async_copy(
-                    ins[a].at[src(c, f)], out[b].at[dst(c, f)], own.at[len(copies)]
-                )
-                copy.start()
-                copies.append(copy)
-        pl.semaphore_wait(barrier, len(remote))
-        number = 0
-        for dc, df, moves in remote:
-            for a, src, b, dst in moves:
-                copy = pltpu.make_async_remote_copy(
-                    ins[a].at[src(c, f)],
-                    out[b].at[dst(c, f)],
-                    send.at[number],
-                    recv.at[number],
-                    device_id=(flip(c, dc), flip(f, df)),
-                    device_id_type=MESH,
-                )
-                copy.start()
-                copies.append(copy)
-                number += 1
-        for copy in copies:
-            copy.wait()
-
-    anywhere = pl.BlockSpec(memory_space=pl.ANY)
-    return pl.pallas_call(
-        kernel,
-        name=name,
-        out_shape=[jax.ShapeDtypeStruct(shape, dtype) for shape, dtype in outs],
-        in_specs=[anywhere] * len(operands),
-        out_specs=[anywhere] * len(outs),
-        scratch_shapes=[
-            pltpu.SemaphoreType.DMA((amount,)),
-            pltpu.SemaphoreType.DMA((amount,)),
-            pltpu.SemaphoreType.DMA((max(local_amount, 1),)),
-        ],
-        compiler_params=pltpu.CompilerParams(collective_id=cid, has_side_effects=True),
-        cost_estimate=lasting(microseconds),
-    )(*operands)
 
 
 PAY = D + 128
@@ -753,8 +694,8 @@
 
 def attention_backward_kernel(
     parts, n_ctx, g_own, q_ref, kv_ref, seg_ref, code_ref, full_ref, log_ref, cos_ref, sin_ref,
-    tok, gain, resid_grad, grads, mix, output_part, tokens_all, q_full, k_full, v_full,
-    input_grad, gain_grad, output_sum, gate_came, down_keep, down_came, mix_in, head_in,
+    tok, gain, resid_grad, residual, grads, mix, output_part, tokens_all, q_full, k_full, v_full,
+    input_grad, layer_out, gain_grad, output_sum, gate_came, down_keep, down_came, mix_in, head_in,
     g_ref, total, kept, came, dq_ref, dkv_ref, dq_back, dkv_back, w_q, w_k, w_v, grad_qkv, grad_in,
     token_buf, field, head_acc, head_out, output_keep, output_came, output_x, output_pair,
     send_g, recv_g, send_q, recv_q, send_kv, recv_kv, send_mix, recv_mix, send_half, recv_half, here,
@@ -983,7 +924,7 @@
 
     def head_weights(b, nothing):
         bring(b).wait()
-        block = token_buf[lax.rem(b, 2)].reshape(SEQS * BLOCK, D)
+        block = token_buf[lax.rem(b, 2)]
         wide_block = block.astype(F32)
         scales = lax.rsqrt(jnp.mean(wide_block * wide_block, axis=1, keepdims=True) + EPS)
         j = lax.div(b, parts)
@@ -1091,6 +1032,24 @@
         - x * (scale * scale * scale) * jnp.mean(weighted * x, axis=1, keepdims=True)
     ).astype(BF16)
 
+    staying = pltpu.make_async_copy(residual, grad_in, here.at[8])
+    staying.start()
+    staying.wait()
+
+    def share(i):
+        return pltpu.make_async_copy(
+            mix_in.at[i - 1] if i else mix.at[0], token_buf.at[i % 2], load_t.at[i % 2]
+        )
+
+    share(0).start()
+    for i in range(RANKS):
+        if i + 1 < RANKS:
+            returns[i].wait_recv()
+            share(i + 1).start()
+        share(i).wait()
+        grad_in[...] += token_buf[i % 2].astype(F32)
+    layer_out[...] = grad_in[...].astype(BF16)
+
     output_stages[1].wait_recv()
 
     def over_x(i, nothing):
@@ -1109,16 +1068,16 @@
     lax.fori_loop(0, planes, over_pair, 0)
     for copy in to_heads:
         copy.wait_send()
-    for copy in returns + to_all + [gate_halving, down_second, leaving, head_stays]:
+    for copy in to_all + [gate_halving, down_second, leaving, head_stays]:
         copy.wait()
-    for copy in output_stages:
+    for copy in returns + output_stages:
         copy.wait_send()
     down_halving.wait_send()
 
 
 def attention_backward(
     cid, parts, n_ctx, g_own, q, kv, segq, codes, full, logs, cosine, sine,
-    tok, gain, resid_grad, grads, mix, output_part, tokens_all, q_full, k_full, v_full,
+    tok, gain, resid_grad, residual, grads, mix, output_part, tokens_all, q_full, k_full, v_full,
 ):
     wide = 2 * HEAD_SIZE
     anywhere = pl.BlockSpec(memory_space=pl.ANY)
@@ -1135,6 +1094,7 @@
         name="attention_backward",
         out_shape=[
             jax.ShapeDtypeStruct(tok.shape, BF16),
+            jax.ShapeDtypeStruct(tok.shape, BF16),
             jax.ShapeDtypeStruct((1, D), F32),
             jax.ShapeDtypeStruct((planes, slab, D), BF16),
             jax.ShapeDtypeStruct(half, BF16),
@@ -1143,8 +1103,8 @@
             jax.ShapeDtypeStruct((RANKS - 1,) + mix.shape[1:], BF16),
             jax.ShapeDtypeStruct((devices, slab, head_width), BF16),
         ],
-        in_specs=[anywhere] + [inside] * 11 + [anywhere] * 7,
-        out_specs=[inside] * 3 + [anywhere] * 5,
+        in_specs=[anywhere] + [inside] * 11 + [anywhere] * 8,
+        out_specs=[inside] * 4 + [anywhere] * 5,
         scratch_shapes=[
             pltpu.VMEM(q.shape, BF16),
             pltpu.VMEM((n_ctx, 2, BLOCK, wide), F32),
@@ -1159,7 +1119,7 @@
             pltpu.VMEM(v_full.shape, BF16),
             pltpu.VMEM((SEQS * BLOCK, columns), BF16),
             pltpu.VMEM((SEQS * BLOCK, D), F32),
-            pltpu.VMEM((2, SEQS, BLOCK, D), BF16),
+            pltpu.VMEM((2, SEQS * BLOCK, D), BF16),
             pltpu.VMEM((SEQS * BLOCK, 3 * wide), BF16),
             pltpu.VMEM((D, 3 * wide), F32),
             pltpu.VMEM((devices, slab, head_width), BF16),
@@ -1176,9 +1136,200 @@
         ),
         cost_estimate=lasting(125),
     )(
-        g_own, q, kv, segq, codes, full, logs, cosine, sine, tok, gain, resid_grad,
+        g_own, q, kv, segq, codes, full, logs, cosine, sine, tok, gain, resid_grad, residual,
         grads, mix, output_part, tokens_all, q_full, k_full, v_full,
     )
+
+
+def final_kernel(
+    n_ctx, small, output_part, grads, gate_came, down_keep, down_came,
+    swapped, output_grad, small_sum,
+    halves, landed, rest, rest_landed, last, last_landed, turned, output_in, small_in,
+    send_half, recv_half, send_out, recv_out, send_small, recv_small, send_swap, recv_swap, load,
+):
+    c, f = lax.axis_index("ctx"), lax.axis_index("fsdp")
+    me, plane, rank = c * 4 + f, lax.div(c, 2), lax.rem(c, 2) * 4 + f
+    planes = n_ctx // 2
+    half, quarter = planes // 2, planes // 4
+    barrier = pltpu.get_barrier_semaphore()
+    peers = [(i, k) for i in range(n_ctx) for k in range(4) if i or k]
+    for dc, df in peers:
+        pl.semaphore_signal(
+            barrier, inc=1, device_id=(flip(c, dc), flip(f, df)), device_id_type=MESH
+        )
+    first, second = lax.rem(plane, 2), lax.rem(lax.div(plane, 2), 2)
+    loads = [
+        pltpu.make_async_copy(source, target, load.at[i])
+        for i, (source, target) in enumerate(
+            (
+                (grads.at[0, pl.ds(first * half, half)], halves.at[0]),
+                (gate_came, landed.at[0]),
+                (grads.at[1, pl.ds(first * half, half)], halves.at[1]),
+                (down_keep, rest.at[2]),
+                (down_came, rest_landed.at[2]),
+                (output_part.at[plane], output_in.at[plane]),
+                (small.at[me], small_in.at[me]),
+            )
+        )
+    ]
+    for copy in loads:
+        copy.start()
+    pl.semaphore_wait(barrier, len(peers))
+
+    def over(source, target, number, bit):
+        return pltpu.make_async_remote_copy(
+            source, target, send_half.at[number], recv_half.at[number],
+            device_id=(flip(c, 2 * bit), f), device_id_type=MESH,
+        )
+
+    up_first = over(grads.at[1, pl.ds((1 - first) * half, half)], landed.at[1], 0, 1)
+    up_first.start()
+
+    def plus(mine, came):
+        return (mine.astype(F32) + came.astype(F32)).astype(BF16)
+
+    def join(mine, came, amount):
+        def one(i, nothing):
+            at, e = lax.div(i, OWN), lax.rem(i, OWN)
+            mine[at, e] = plus(mine[at, e], came[at, e])
+            return nothing
+
+        lax.fori_loop(0, amount * OWN, one, 0)
+
+    def second_halving(m):
+        copy = over(halves.at[m, pl.ds((1 - second) * quarter, quarter)], rest_landed.at[m], 1 + m, 2)
+        copy.start()
+        return copy
+
+    loads[0].wait()
+    loads[1].wait()
+    join(halves.at[0], landed.at[0], half)
+    gate_second = second_halving(0)
+    smalls = []
+    for number, (i, k) in enumerate(peers):
+        peer_c, peer_f = flip(c, i), flip(f, k)
+        smalls.append(
+            pltpu.make_async_remote_copy(
+                small.at[peer_c * 4 + peer_f], small_in.at[me], send_small.at[number], recv_small.at[number],
+                device_id=(peer_c, peer_f), device_id_type=MESH,
+            )
+        )
+    outputs = []
+    for i in range(1, planes):
+        outputs.append(
+            pltpu.make_async_remote_copy(
+                output_part.at[flip(plane, i)], output_in.at[plane], send_out.at[i - 1], recv_out.at[i - 1],
+                device_id=(flip(c, 2 * i), f), device_id_type=MESH,
+            )
+        )
+    for copy in smalls + outputs:
+        copy.start()
+
+    def more_halvings(m):
+        count, bit, number = quarter, 4, 0
+        mine, sent = rest.at[m], []
+        join(mine, rest_landed.at[m], quarter)
+        while count > 1:
+            count //= 2
+            chosen = lax.rem(lax.div(plane, bit), 2)
+            came = last_landed.at[m, number, pl.ds(0, count)]
+            copy = over(mine.at[pl.ds((1 - chosen) * count, count)], came, 4 + 2 * m + number, bit)
+            copy.start()
+            copy.wait_recv()
+            sent.append(copy)
+            kept = last.at[m, number, pl.ds(0, count)]
+            for at in range(count):
+                for e in range(OWN):
+                    kept[at, e] = plus(mine[chosen * count + at, e], came[at, e])
+            mine, bit, number = kept, bit * 2, number + 1
+        rows = turned.shape[3]
+        for e in range(OWN):
+            across = mine[0, e].astype(F32).T
+            for r in range(RANKS):
+                turned[m, r, e] = across[r * rows : (r + 1) * rows].astype(BF16)
+        for i in range(RANKS):
+            source, target = turned.at[m, flip(rank, i)], swapped.at[rank, m]
+            if i:
+                copy = pltpu.make_async_remote_copy(
+                    source, target, send_swap.at[m, i], recv_swap.at[m, i],
+                    device_id=(flip(c, i // 4), flip(f, i % 4)), device_id_type=MESH,
+                )
+            else:
+                copy = pltpu.make_async_copy(source, target, load.at[7 + m])
+            copy.start()
+            swaps.append(copy)
+        return sent
+
+    swaps = []
+    loads[3].wait()
+    loads[4].wait()
+    sent = more_halvings(2)
+    loads[2].wait()
+    up_first.wait_recv()
+    join(halves.at[1], landed.at[1], half)
+    up_second = second_halving(1)
+
+    def quarter_sum(m, copy):
+        for at in range(quarter):
+            for e in range(OWN):
+                rest[m, at, e] = halves[m, second * quarter + at, e]
+        copy.wait_recv()
+
+    quarter_sum(0, gate_second)
+    sent += more_halvings(0)
+    loads[5].wait()
+    loads[6].wait()
+    for copy in outputs + smalls:
+        copy.wait_recv()
+    made = output_in[0].astype(F32)
+    for i in range(1, planes):
+        made = made + output_in[i].astype(F32)
+    output_grad[...] = made
+    small_sum[...] = jnp.sum(small_in[...], axis=0)
+    quarter_sum(1, up_second)
+    sent += more_halvings(1)
+    for copy in swaps:
+        copy.wait()
+    for copy in smalls + outputs + sent + [up_first, gate_second, up_second]:
+        copy.wait_send()
+
+
+def final_sums(cid, n_ctx, small, output_part, grads, gate_came, down_keep, down_came):
+    anywhere = pl.BlockSpec(memory_space=pl.ANY)
+    inside = pl.BlockSpec(memory_space=pltpu.VMEM)
+    dma = pltpu.SemaphoreType.DMA
+    devices, planes = n_ctx * 4, n_ctx // 2
+    slab, piece = D // devices, grads.shape[2:]
+    half, quarter = (planes // 2,) + piece, (planes // 4,) + piece
+    deep = (3, 2, max(planes // 8, 1)) + piece
+    return pl.pallas_call(
+        functools.partial(final_kernel, n_ctx),
+        name="final_sums",
+        out_shape=[
+            jax.ShapeDtypeStruct((RANKS, 3, OWN, slab, FF), BF16),
+            jax.ShapeDtypeStruct((slab, D), F32),
+            jax.ShapeDtypeStruct(small.shape[1:], F32),
+        ],
+        in_specs=[anywhere] * 6,
+        out_specs=[anywhere] + [inside] * 2,
+        scratch_shapes=[
+            pltpu.VMEM((2,) + half, BF16),
+            pltpu.VMEM((2,) + half, BF16),
+            pltpu.VMEM((3,) + quarter, BF16),
+            pltpu.VMEM((3,) + quarter, BF16),
+            pltpu.VMEM(deep if planes > 4 else (1, 1, 1, 1, 8, 128), BF16),
+            pltpu.VMEM(deep if planes > 4 else (1, 1, 1, 1, 8, 128), BF16),
+            pltpu.VMEM((3, RANKS, OWN, slab, FF), BF16),
+            pltpu.VMEM((planes, slab, D), BF16),
+            pltpu.VMEM(small.shape, F32),
+            dma((10,)), dma((10,)), dma((planes - 1,)), dma((planes - 1,)),
+            dma((devices - 1,)), dma((devices - 1,)), dma((3, RANKS)), dma((3, RANKS)), dma((10,)),
+        ],
+        compiler_params=pltpu.CompilerParams(
+            collective_id=cid, has_side_effects=True, vmem_limit_bytes=56 << 20
+        ),
+        cost_estimate=lasting(100),
+    )(small, output_part, grads, gate_came, down_keep, down_came)
 
 
 def rope_tables(positions):
@@ -1229,9 +1380,6 @@
     part = lax.rem(c_index, parts)
     head = lax.div(c_index, parts)
     positions = c_index * BLOCK + jnp.arange(BLOCK, dtype=jnp.int32)
-
-    def tie(x, after):
-        return lax.optimization_barrier((x, after))[0]
 
     tokens_all = lax.all_gather(tokens, "ctx", axis=0, tiled=False)
     small = jnp.concatenate(
@@ -1300,19 +1448,6 @@
         (own_gate, own_up, own_down), tokens_all
     )
 
-    replica = lax.div(c_index, 2)
-
-    def halve(grad, bit):
-        grad = grad.reshape((2, -1) + grad.shape[1:])
-        mine = lax.rem(lax.div(replica, bit), 2)
-        send = lax.dynamic_index_in_dim(grad, 1 - mine, 0, keepdims=False)
-        keep = lax.dynamic_index_in_dim(grad, mine, 0, keepdims=False)
-        return keep, lax.ppermute(send, "ctx", [(a, a ^ (2 * bit)) for a in range(n_ctx)])
-
-    def joined(halves, after):
-        keep, came = halves
-        return (keep.astype(F32) + tie(came, after).astype(F32)).astype(BF16)
-
     back = back.reshape(SEQS, BLOCK, D + 128)
     grad_gates = jnp.where(is_kept, back[..., D : D + EXPERTS], 0.0)
     grad_chosen = gates * (grad_gates - jnp.sum(gates * grad_gates, axis=-1, keepdims=True))
@@ -1336,127 +1471,34 @@
     grad_attn = grad_attn.astype(BF16)
     grad_output_w = jnp.einsum("sgd,sgq->dq", grad_resid_low, attn_out, preferred_element_type=F32)
     rows = D // (n_ctx * n_fsdp)
-    def two(field, axis, bit):
-        return (
-            lax.dynamic_index_in_dim(field, 1 - bit, axis, keepdims=False),
-            lax.dynamic_index_in_dim(field, bit, axis, keepdims=False),
-        )
-
-    def summed(mine, came):
-        return (mine.astype(F32) + came.astype(F32)).astype(BF16)
-
     output_part = grad_output_w.astype(BF16).reshape(replicas, 2, 2, 2, rows, D)
 
-    input_grad, gain_grad, output_sum, gate_came, down_keep, down_came, mix_in, head_grads = attention_backward(
+    input_grad, layer_out, gain_grad, output_sum, gate_came, down_keep, down_came, _, head_grads = attention_backward(
         6, parts, n_ctx, heads_out(grad_attn, REP), q_all, kv_all, segq, codes, head_full, head_logs,
         all_cosine, all_sine, tokens.reshape(SEQS * BLOCK, D), gain_first[None],
-        grad_resid.reshape(SEQS * BLOCK, D), own_grads, mix_part, output_part, tokens_all,
-        full_query, full_key, full_value,
+        grad_resid.reshape(SEQS * BLOCK, D), residual.reshape(SEQS * BLOCK, D), own_grads, mix_part, output_part,
+        tokens_all.reshape(n_ctx, SEQS * BLOCK, D), full_query, full_key, full_value,
     )
     input_grad = input_grad.reshape(SEQS, BLOCK, D)
-    layer_out = (
-        residual.reshape(SEQS * BLOCK, D) + mix_part[0].astype(F32) + jnp.sum(mix_in.astype(F32), axis=0)
-    ).astype(BF16).reshape(SEQS, BLOCK, D)
-    gate_keep = own_grads[0].reshape((2, replicas // 2, OWN, FF, D // replicas))
-    gate_half = (lax.dynamic_index_in_dim(gate_keep, lax.rem(replica, 2), 0, keepdims=False), gate_came)
-    small_grads = jnp.concatenate(
-        [grad_router, gain_grad.T, grad_gain_second[:, None], jnp.zeros((D, 128 - EXPERTS - 2), F32)],
-        axis=1,
-    ).reshape(n_ctx * n_fsdp, rows, 128)
-
-    def device(c, f):
-        return c * n_fsdp + f
-
-    def ranked(c, f):
-        return lax.rem(c, 2) * n_fsdp + f
-
-    def by_rank(sums):
-        field = jnp.stack(sums).reshape(len(sums), OWN, FF, RANKS, rows)
-        return field.transpose(3, 0, 1, 4, 2)
-
-    def quarters(halves):
-        return two(
-            summed(*halves).reshape(2, replicas // 4, OWN, FF, D // replicas),
-            0,
-            lax.rem(lax.div(replica, 2), 2),
-        )
-
-    def whole(keep, came):
-        bit = 4
-        while bit < replicas:
-            keep, came = halve(summed(keep, came), bit)
-            bit *= 2
-        return summed(keep, came)
-
-    everything = lambda c, f: slice(None)
-
-    def kept_half(grad):
-        grad = grad.reshape((2, replicas // 2) + grad.shape[1:])
-        return lax.dynamic_index_in_dim(grad, lax.rem(replica, 2), 0, keepdims=False)
-
-    gate_other, gate_mine = quarters((kept_half(own_grads[0]), gate_came))
-    routes = []
-    for i in range(n_ctx):
-        for k in range(n_fsdp):
-            moves = []
-            if k == 0 and i == 4:
-                moves.append((2, everything, 2, everything))
-            if k == 0 and i == 2:
-                moves.append(
-                    (
-                        3,
-                        lambda c, f: (
-                            1,
-                            pl.ds((1 - lax.rem(lax.div(c, 2), 2)) * (replicas // 2), replicas // 2),
-                        ),
-                        3,
-                        everything,
-                    )
-                )
-            moves.append(
-                (0, lambda c, f, i=i, k=k: device(flip(c, i), flip(f, k)), 0, device)
-            )
-            if k == 0 and i % 2 == 0:
-                moves.append(
-                    (1, lambda c, f, i=i: lax.div(flip(c, i), 2), 1, lambda c, f: lax.div(c, 2))
-                )
-            routes.append((i, k, moves))
-    routes.sort(key=lambda r: not (r[1] == 0 and r[0] in (2, 4)))
-    operands = [small_grads, output_sum, gate_other, own_grads]
-    outs = [(x.shape, x.dtype) for x in operands[:3]] + [(gate_came.shape, BF16)]
-    small_all, output_all, gate_came, up_came = exchange(9, "sum_grads", routes, operands, outs, 60)
-    output_grad = jnp.sum(output_all.astype(F32), axis=0)
-    up_other, up_mine = quarters((kept_half(own_grads[1]), up_came))
-    gate_down = by_rank([whole(gate_mine, gate_came), whole(down_keep, down_came)])
-    routes = [
-        (i // 4, i % 4, [(0, lambda c, f, i=i: flip(ranked(c, f), i), 0, ranked)]) for i in range(RANKS)
-    ]
-    gate_down, up_came = exchange(
-        10,
-        "swap_gate_down",
-        [(4, 0, [(1, everything, 1, everything)])] + routes,
-        [gate_down, up_other],
-        [(gate_down.shape, BF16), (up_other.shape, BF16)],
-        40,
+    layer_out = layer_out.reshape(SEQS, BLOCK, D)
+    amount = rows * (EXPERTS + 2)
+    tiles = -(-amount // 1024) * 8
+    small_grads = jnp.concatenate([grad_router, gain_grad.T, grad_gain_second[:, None]], axis=1)
+    small_grads = jnp.pad(
+        small_grads.reshape(n_ctx * n_fsdp, amount), ((0, 0), (0, tiles * 128 - amount))
+    ).reshape(n_ctx * n_fsdp, tiles, 128)
+    swapped, output_grad, small_sum = final_sums(
+        9, n_ctx, small_grads, output_sum, own_grads, gate_came, down_keep, down_came
     )
+    small_sum = small_sum.reshape(tiles * 128)[:amount].reshape(rows, EXPERTS + 2)
     head_grads = head_grads.reshape(KEY_VALUE_HEADS, parts * n_fsdp, rows, (REP + 2) * HEAD_SIZE)
-    own_gain = lax.dynamic_slice_in_dim(gain_first, device(c_index, f_index) * rows, rows, 0)
+    own_gain = lax.dynamic_slice_in_dim(gain_first, (c_index * n_fsdp + f_index) * rows, rows, 0)
     head_grads = jnp.sum(head_grads.astype(F32), axis=1).transpose(1, 0, 2) * own_gain[:, None, None]
     query_grad = head_grads[..., : REP * HEAD_SIZE].reshape(rows, D)
     key_grad = head_grads[..., REP * HEAD_SIZE : (REP + 1) * HEAD_SIZE].reshape(rows, -1)
     value_grad = head_grads[..., (REP + 1) * HEAD_SIZE :].reshape(rows, -1)
-    small_sum = jnp.sum(small_all, axis=0)
-
-    up_sum = by_rank([whole(up_mine, up_came)])
-    (up_sum,) = exchange(
-        8,
-        "swap_up",
-        routes,
-        [up_sum],
-        [(up_sum.shape, BF16)],
-    )
-
-    def by_row(swapped, matrix):
+
+    def by_row(matrix):
         return swapped[:, matrix].transpose(2, 0, 1, 3).reshape(rows, EXPERTS, FF).astype(F32)
 
     return (
@@ -1469,9 +1511,9 @@
         output_grad,
         small_sum[:, EXPERTS + 1],
         small_sum[:, :EXPERTS],
-        by_row(gate_down, 0),
-        by_row(up_sum, 0),
-        by_row(gate_down, 1),
+        by_row(0),
+        by_row(1),
+        by_row(2),
     )
 
 

time: 695 us -> 637 us (0.917)
  other arithmetic: 28.3 us -> 8.36 us
  Pallas kernels: 565 us -> 546 us
  local copies, waits for them, and re-layouts: 59.7 us -> 43.9 us
    pallas_call x3 -> x1, Pallas kernels: 130 us -> 111 us  [final_sums(): pl.pallas_call(functools.partial(final_kernel, n_ctx), name='final_sums',...]
    convert_element_type x6 -> x0, other arithmetic: 11.6 us -> none  [the longest x5 10.3 us: summed(): return (mine.astype(F32) + came.astype(F32)).astype(BF16)]
    slice x2 -> x0, local copies, waits for them, and re-layouts: 8.52 us -> none  [the longest x1 6.45 us: on_device(): up_other, up_mine = quarters((kept_half(own_grads[1]), up_came))]
    unnamed x65 -> x53, local copies, waits for them, and re-layouts: 13.2 us -> 15.4 us
  transfers between devices with their start and end apart: 1 -> 1, of which waited for: 0 -> 0; matrix products, arithmetic and copies ran while one was open for 5% -> 5% of each run, Pallas kernels for 22% -> 24%
where the time goes in v3:
time: 637 us; the launch traced here: 628 us
  Pallas kernels  546 us (86%)
  local copies, waits for them, and re-layouts  43.9 us (7%)
  between operations  15 us (2%)
  matrix products  13.2 us (2%)
  other arithmetic  8.36 us (1%)
    pallas_call x1, Pallas kernels, attention_backward(): pl.pallas_call(functools.partial(attention_backward_kernel, parts, n_ctx)...  161 us
    pallas_call x1, Pallas kernels, attention_forward(): pl.pallas_call(functools.partial(attention_forward_kernel, parts, n_ctx),...  150 us
    pallas_call x1, Pallas kernels, run_experts(): pl.pallas_call(functools.partial(experts_kernel, replicas), name='experts...  123 us
    pallas_call x1, Pallas kernels, final_sums(): pl.pallas_call(functools.partial(final_kernel, n_ctx), name='final_sums',...  111 us
    unnamed x53, local copies, waits for them, and re-layouts  15.4 us
  transfers between devices with their start and end apart: 1, of which 0 were waited for; matrix products, arithmetic and copies ran while one was open for 5% of the time, Pallas kernels for 24%

profile of v3, /device:TPU:0, one launch (start us, length us, event | category | flops | bytes accessed | tf_op | source)
XLA Modules:
  0.0 627.6 jit_solution(8204043119411557688)
XLA Ops:
  10.7 1.0 fusion.14
  11.9 1.0 fusion.6
  13.1 1.0 copy.221.sin_ref
  14.2 1.0 copy.220.cos_ref
  16.8 1.3 copy.206.seg_ref
  18.2 2.4 constant_dynamic-slice_fusion.4
  20.6 2.7 copy.201
  23.3 1.8 copy-done.7
  25.9 2.8 copy.203
  28.6 2.7 copy.202
  32.7 150.5 %attention_forward.1 = (bf16[256,1536]{1,0:T(8,128)(2,1)}, bf16[4,32,384]{2,1,0:T(8,128)(2,1)}, bf16[4,384,1536]{2,1,0:T(8,128)(2,1)}, bf16[4,384,512]{2,1,0:T(8...) custom-call(bf16[256,1536]{1,0:T(8,128)(2,1)} %bitcast.112, ...), custom_call_target="tpu_custom_call" | custom-call | bytes 429000000 | tf_op jit(solution)/shard_map/attention_forward/pallas_call | solution.py:655
  183.2 1.6 copy.207
  185.1 4.0 multiply_reduce_fusion.2
  189.1 1.1 copy-done
  191.0 1.1 concatenate.22
  192.7 123.3 %experts.1 = (f32[256,1664]{1,0:T(8,128)}, bf16[8,256,1536]{2,1,0:T(8,128)(2,1)}, bf16[3,4,2,512,384]{4,3,2,1,0:T(8,128)(2,1)}, bf16[7,256,1664]{2,1,0:T(8,128)(2,1)}, bf16[7,256,1536]{2,1,0:T(8,128)(2,1)}) custom-call(bf16[256,1664]{1,0:T(8,128)(2,1)} %bitcast.117, bf16[256,1536]{1,0:T(8,128)(2,1)} %bitcast.118, ...), custom_call_target="tpu_custom_call" | custom-call | bytes 363000000 | tf_op jit(solution)/shard_map/experts/pallas_call | solution.py:324
  316.0 1.0 slice.61
  317.3 2.7 multiply_reduce_fusion
  321.1 1.4 convolution_convert_fusion
  322.8 3.7 bitcast_convert_fusion
  326.9 1.2 copy.218.g_own
  328.1 161.5 %attention_backward.1 = (bf16[256,1536]{1,0:T(8,128)(2,1)}, bf16[256,1536]{1,0:T(8,128)(2,1)}, f32[1,1536]{1,0:T(1,128)}, bf16[4,48,1536]{2,1,0:T(8,128)(2,1)}, ...) custom-call(bf16[8,3,128,128]{3,2,1,0:T(8,128)(2,1)} %copy.218.g_own, ...), custom_call_target="tpu_custom_call" | custom-call | bytes 412500000 | tf_op jit(solution)/shard_map/attention_backward/pallas_call | solution.py:1092
  489.6 1.5 convert_reduce_fusion
  492.5 0.9 reshape.264
  495.5 111.1 %final_sums.1 = (bf16[8,3,2,48,512]{4,3,2,1,0:T(8,128)(2,1)}, f32[48,1536]{1,0:T(8,128)}, f32[8,128]{1,0:T(8,128)}) custom-call(f32[32,8,128]{2,1,0:T(8,128)} %bitcast.136, bf16[4,48,1536]{2,1,0:T(8,128)(2,1)} %get-tuple-element.58.output_part, bf16[3,4,2,512,384]{4,3,2,1,0:T(8,128)(2,1)} %get-tuple-element.50.grads, ...), custom_call_target="tpu_custom_call" | custom-call | bytes 330000000 | tf_op jit(solution)/shard_map/final_sums/pallas_call | solution.py:1305
  606.6 0.8 reshape.263
  608.8 2.3 bitcast_convert_fusion.1
  611.0 2.1 copy.229
  613.1 2.1 copy.228
  615.2 2.1 copy.227
  617.2 0.9 copy.243
  618.6 0.9 copy.244
  (104 shorter events, 17.5 us)
Async XLA Ops:
  7.2 185.5 %all-gather.3.cloned.1.call-start = ((), (), s32[]{:S(2)}) async-start(), calls=%async_computation | async-start | bytes 7077888 | tf_op jit(solution)/shard_map/all_gather | solution.py:1384
  16.8 6.4 %slice-start = ((s8[6291456]{0:T(1024)(128)(4,1)}), s8[2097152]{0:T(1024)(128)(4,1)S(1)}, s32[]{:S(2)}) async-start(s8[6291456]{0:T(1024)(128)(4,1)} %bitcast.132), calls=%async_computation.1 | async-start | bytes 4194304
  18.2 5.1 slice-start.1
  20.5 4.5 copy-start.7
  28.6 2.8 copy-start.12
  28.6 2.8 copy-start.14
  28.6 3.4 copy-start.13
  183.2 1.7 copy-start.11
  183.2 1.8 copy-start.3
  184.9 4.2 copy-start.5
  189.1 1.1 copy-start
  316.0 4.5 slice-start.2
  317.3 2.7 copy-start.1
  317.3 2.7 copy-start.4
  317.3 3.8 slice-start.3
  321.1 1.4 copy-start.2
  321.1 1.7 copy-start.6
  491.4 2.7 copy-start.15
  615.2 2.1 copy-start.9
  617.2 1.4 copy-start.8
  617.2 2.3 copy-start.10
Sparse Core Ops, SparseCore 0:
  10.2 152.2 all-gather.2

commit v4 on v3

--- a/solution.py
+++ b/solution.py
@@ -65,11 +65,11 @@
 
 def experts_kernel(
     replicas, pay, cot, gate_own, up_own, down_own, after,
-    back, mix, grads, pay_in, cot_in,
+    back, mix, grads, down_came, pay_in, cot_in,
     weights, total, pay_now, cot_now, xs, gs, eo, gi, hid, dgate, dup, disp, comb,
     own, out, sib, ret, mix_now,
     send_first, recv_first, send_fwd, recv_fwd, send_sib, recv_sib, send_chip, recv_chip,
-    load_w, load, store, piece_sem,
+    load_w, load, store, piece_sem, send_down, recv_down,
 ):
     c, f = lax.axis_index("ctx"), lax.axis_index("fsdp")
     rank = lax.rem(c, 2) * 4 + f
@@ -78,11 +78,14 @@
     pl.semaphore_signal(barrier, inc=1, device_id=sibling, device_id_type=MESH)
     for k in range(1, 4):
         pl.semaphore_signal(barrier, inc=1, device_id=other_chip(c, f, k), device_id_type=MESH)
+    apart = len(grads.shape) == 5
+    if apart:
+        pl.semaphore_signal(barrier, inc=1, device_id=(flip(c, 2), f), device_id_type=MESH)
     bring = []
     for m, own_weight in enumerate((gate_own, up_own, down_own)):
         bring.append(pltpu.make_async_copy(own_weight, weights.at[m], load_w.at[m]))
         bring[-1].start()
-    pl.semaphore_wait(barrier, 4)
+    pl.semaphore_wait(barrier, 5 if apart else 4)
     sources, landed = (pay, cot), (pay_in, cot_in)
 
     def push(k, a):
@@ -275,14 +278,22 @@
         store_mix(3, s).wait()
     stages = (eo, gi)
     pending = []
+    if apart:
+        half = replicas // 2
+        down_first = pltpu.make_async_remote_copy(
+            grads.at[2, pl.ds((1 - lax.rem(lax.div(c, 2), 2)) * half, half)], down_came,
+            send_down, recv_down, device_id=(flip(c, 2), f), device_id_type=MESH,
+        )
     for i in range(3 * OWN):
-        m, e = i // OWN, i % OWN
+        m, e = (2, 0, 1)[i // OWN], i % OWN
         if i >= 2:
             for copy in pending[i - 2]:
                 copy.wait()
+        if i == OWN + 1 and apart:
+            down_first.start()
         stages[i % 2][:FF] = total[m, e].astype(BF16)
         pending.append([])
-        if len(grads.shape) == 4:
+        if not apart:
             pending[i].append(
                 pltpu.make_async_copy(stages[i % 2].at[:FF], grads.at[m, e], piece_sem.at[i % 2, 0])
             )
@@ -312,6 +323,8 @@
     back[...] = (sib[0].astype(F32) + ret[0].astype(F32)) + (ret[1].astype(F32) + ret[2].astype(F32))
     for k in range(1, 4):
         to_chip(k).wait_send()
+    if apart:
+        down_first.wait()
 
 
 def run_experts(cid, replicas, pay, cot, owns, after):
@@ -321,18 +334,19 @@
     anywhere = pl.BlockSpec(memory_space=pl.ANY)
     inside = pl.BlockSpec(memory_space=pltpu.VMEM)
     dma = pltpu.SemaphoreType.DMA
-    back, mix, grads, _, _ = pl.pallas_call(
+    back, mix, grads, down_came, _, _ = pl.pallas_call(
         functools.partial(experts_kernel, replicas),
         name="experts",
         out_shape=[
             jax.ShapeDtypeStruct((tokens, PAY), F32),
             jax.ShapeDtypeStruct((RANKS, tokens, D), BF16),
             jax.ShapeDtypeStruct((3, replicas, OWN, FF, width) if apart else (3, OWN, FF, D), BF16),
+            jax.ShapeDtypeStruct((replicas // 2, OWN, FF, width) if apart else (8, 128), BF16),
             jax.ShapeDtypeStruct((RANKS - 1, tokens, PAY), BF16),
             jax.ShapeDtypeStruct((RANKS - 1, tokens, D), BF16),
         ],
         in_specs=[anywhere] * 6,
-        out_specs=[inside] + [anywhere] * 4,
+        out_specs=[inside] + [anywhere] * 5,
         scratch_shapes=[
             pltpu.VMEM((3, OWN, D, FF), BF16),
             pltpu.VMEM((3, OWN, FF, D), F32),
@@ -354,7 +368,7 @@
             pltpu.VMEM((2, tokens, D), BF16),
             dma((4, 2)), dma((4, 2)), dma((3, 2)), dma((3, 2)),
             dma((4,)), dma((4,)), dma((3,)), dma((3,)),
-            dma((4,)), dma((2, 2)), dma((2,)), dma((2, replicas)),
+            dma((4,)), dma((2, 2)), dma((2,)), dma((2, replicas)), dma, dma,
         ],
         compiler_params=pltpu.CompilerParams(
             collective_id=cid, has_side_effects=True, vmem_limit_bytes=63 << 20
@@ -364,7 +378,7 @@
     if not apart:
         grads = grads.reshape(3, OWN, FF, replicas, width).transpose(0, 3, 1, 2, 4)
         grads = grads[:, jnp.array(plane_order(replicas))]
-    return back, mix, grads
+    return back, mix, grads, down_came, apart
 
 
 def half_masks(dtype):
@@ -693,10 +707,10 @@
 
 
 def attention_backward_kernel(
-    parts, n_ctx, g_own, q_ref, kv_ref, seg_ref, code_ref, full_ref, log_ref, cos_ref, sin_ref,
-    tok, gain, resid_grad, residual, grads, mix, output_part, tokens_all, q_full, k_full, v_full,
-    input_grad, layer_out, gain_grad, output_sum, gate_came, down_keep, down_came, mix_in, head_in,
-    g_ref, total, kept, came, dq_ref, dkv_ref, dq_back, dkv_back, w_q, w_k, w_v, grad_qkv, grad_in,
+    parts, n_ctx, early, g_own, q_ref, kv_ref, seg_ref, code_ref, full_ref, log_ref, cos_ref, sin_ref,
+    tok, gain, resid_grad, residual, grads, down_in, mix, output_part, tokens_all, q_full, k_full, v_full,
+    input_grad, layer_out, gain_grad, output_sum, gate_first, gate_keep, gate_came, down_keep, down_came, mix_in,
+    head_in, g_ref, total, kept, came, dq_ref, dkv_ref, dq_back, dkv_back, w_q, w_k, w_v, grad_qkv, grad_in,
     token_buf, field, head_acc, head_out, output_keep, output_came, output_x, output_pair,
     send_g, recv_g, send_q, recv_q, send_kv, recv_kv, send_mix, recv_mix, send_half, recv_half, here,
     send_out, recv_out, send_head, recv_head, load_t,
@@ -754,8 +768,9 @@
             device_id=(flip(c, 2), f), device_id_type=MESH,
         )
 
-    down_halving, gate_halving = halving(2, came, 0), halving(0, gate_came, 1)
-    down_halving.start()
+    down_halving, gate_halving = halving(2, came, 0), halving(0, gate_first, 1)
+    arriving = pltpu.make_async_copy(down_in, came, here.at[10]) if early else down_halving
+    arriving.start()
     keeping = pltpu.make_async_copy(grads.at[2, pl.ds(mine * half, half)], kept, here.at[3])
     keeping.start()
     output_stages = [
@@ -780,6 +795,30 @@
             )
         )
         returns[-1].start()
+    def plus(mine, came):
+        return (mine.astype(F32) + came.astype(F32)).astype(BF16)
+
+    def second_halving(keep, target, number):
+        def add(i, nothing):
+            at, e = lax.div(i, OWN), lax.rem(i, OWN)
+            kept[at, e] = plus(kept[at, e], came[at, e])
+            return nothing
+
+        lax.fori_loop(0, half * OWN, add, 0)
+        going = pltpu.make_async_remote_copy(
+            kept.at[pl.ds((1 - second) * quarter, quarter)], target, send_half.at[number], recv_half.at[number],
+            device_id=(flip(c, 4), f), device_id_type=MESH,
+        )
+        going.start()
+        staying = pltpu.make_async_copy(kept.at[pl.ds(second * quarter, quarter)], keep, here.at[4])
+        staying.start()
+        return going, staying
+
+    if early:
+        keeping.wait()
+        arriving.wait()
+        down_second, leaving = second_halving(down_keep, down_came, 2)
+    gate_halving.start()
     total[...] = jnp.zeros_like(total)
     first.wait()
     for copy in to_heads:
@@ -877,28 +916,12 @@
         return nothing
 
     lax.fori_loop(0, n_ctx, finish, 0)
-    gate_halving.start()
-    keeping.wait()
-    down_halving.wait_recv()
-
-    def add(i, nothing):
-        at, e = lax.div(i, OWN), lax.rem(i, OWN)
-        kept[at, e] = (kept[at, e].astype(F32) + came[at, e].astype(F32)).astype(BF16)
-        return nothing
-
-    lax.fori_loop(0, half * OWN, add, 0)
-    down_second = pltpu.make_async_remote_copy(
-        kept.at[pl.ds((1 - second) * quarter, quarter)], down_came, send_half.at[2], recv_half.at[2],
-        device_id=(flip(c, 4), f), device_id_type=MESH,
-    )
-    down_second.start()
-    leaving = pltpu.make_async_copy(kept.at[pl.ds(second * quarter, quarter)], down_keep, here.at[4])
-    leaving.start()
+    if not early:
+        keeping.wait()
+        down_halving.wait_recv()
+        down_second, leaving = second_halving(down_keep, down_came, 2)
 
     planes = output_keep.shape[0]
-
-    def plus(mine, came):
-        return (mine.astype(F32) + came.astype(F32)).astype(BF16)
 
     loads[3].wait()
     output_stages[0].wait_recv()
@@ -963,6 +986,19 @@
             )
         )
         to_all[-1].start()
+
+    down_second.wait_send()
+    leaving.wait()
+    gate_halving.wait_recv()
+    refill = [
+        pltpu.make_async_copy(grads.at[0, pl.ds(mine * half, half)], kept, here.at[3]),
+        pltpu.make_async_copy(gate_first, came, here.at[10]),
+    ]
+    for copy in refill:
+        copy.start()
+    for copy in refill:
+        copy.wait()
+    gate_second, leaving = second_halving(gate_keep, gate_came, 3)
 
     def came_query(h, nothing):
         @pl.when(h != head)
@@ -1068,16 +1104,16 @@
     lax.fori_loop(0, planes, over_pair, 0)
     for copy in to_heads:
         copy.wait_send()
-    for copy in to_all + [gate_halving, down_second, leaving, head_stays]:
+    for copy in to_all + [gate_second, leaving, head_stays]:
         copy.wait()
-    for copy in returns + output_stages:
+    down_second.wait_recv()
+    for copy in returns + output_stages + [gate_halving] + ([] if early else [down_halving]):
         copy.wait_send()
-    down_halving.wait_send()
 
 
 def attention_backward(
-    cid, parts, n_ctx, g_own, q, kv, segq, codes, full, logs, cosine, sine,
-    tok, gain, resid_grad, residual, grads, mix, output_part, tokens_all, q_full, k_full, v_full,
+    cid, parts, n_ctx, early, g_own, q, kv, segq, codes, full, logs, cosine, sine,
+    tok, gain, resid_grad, residual, grads, down_in, mix, output_part, tokens_all, q_full, k_full, v_full,
 ):
     wide = 2 * HEAD_SIZE
     anywhere = pl.BlockSpec(memory_space=pl.ANY)
@@ -1090,7 +1126,7 @@
     quarter = (grads.shape[1] // 4,) + grads.shape[2:]
     columns = q_full.shape[2] + k_full.shape[2] + v_full.shape[2]
     return pl.pallas_call(
-        functools.partial(attention_backward_kernel, parts, n_ctx),
+        functools.partial(attention_backward_kernel, parts, n_ctx, early),
         name="attention_backward",
         out_shape=[
             jax.ShapeDtypeStruct(tok.shape, BF16),
@@ -1100,11 +1136,13 @@
             jax.ShapeDtypeStruct(half, BF16),
             jax.ShapeDtypeStruct(quarter, BF16),
             jax.ShapeDtypeStruct(quarter, BF16),
+            jax.ShapeDtypeStruct(quarter, BF16),
+            jax.ShapeDtypeStruct(quarter, BF16),
             jax.ShapeDtypeStruct((RANKS - 1,) + mix.shape[1:], BF16),
             jax.ShapeDtypeStruct((devices, slab, head_width), BF16),
         ],
-        in_specs=[anywhere] + [inside] * 11 + [anywhere] * 8,
-        out_specs=[inside] * 4 + [anywhere] * 5,
+        in_specs=[anywhere] + [inside] * 11 + [anywhere] * 9,
+        out_specs=[inside] * 4 + [anywhere] * 7,
         scratch_shapes=[
             pltpu.VMEM(q.shape, BF16),
             pltpu.VMEM((n_ctx, 2, BLOCK, wide), F32),
@@ -1128,8 +1166,8 @@
             pltpu.VMEM((planes, 2, slab, D), BF16),
             pltpu.VMEM((planes, slab, D), BF16),
             dma((others,)), dma((others,)), dma((KEY_VALUE_HEADS,)), dma((KEY_VALUE_HEADS,)),
-            dma((n_ctx,)), dma((n_ctx,)), dma((RANKS - 1,)), dma((RANKS - 1,)), dma((3,)), dma((3,)),
-            dma((10,)), dma((3,)), dma((3,)), dma((devices - 1,)), dma((devices - 1,)), dma((2,)),
+            dma((n_ctx,)), dma((n_ctx,)), dma((RANKS - 1,)), dma((RANKS - 1,)), dma((4,)), dma((4,)),
+            dma((11,)), dma((3,)), dma((3,)), dma((devices - 1,)), dma((devices - 1,)), dma((2,)),
         ],
         compiler_params=pltpu.CompilerParams(
             collective_id=cid, has_side_effects=True, vmem_limit_bytes=60 << 20
@@ -1137,15 +1175,16 @@
         cost_estimate=lasting(125),
     )(
         g_own, q, kv, segq, codes, full, logs, cosine, sine, tok, gain, resid_grad, residual,
-        grads, mix, output_part, tokens_all, q_full, k_full, v_full,
+        grads, down_in, mix, output_part, tokens_all, q_full, k_full, v_full,
     )
 
 
 def final_kernel(
-    n_ctx, small, output_part, grads, gate_came, down_keep, down_came,
+    n_ctx, small, output_part, grads, gate_keep, gate_came, down_keep, down_came,
     swapped, output_grad, small_sum,
     halves, landed, rest, rest_landed, last, last_landed, turned, output_in, small_in,
-    send_half, recv_half, send_out, recv_out, send_small, recv_small, send_swap, recv_swap, load,
+    send_half, recv_half, send_deep, recv_deep, send_out, recv_out, send_small, recv_small,
+    send_swap, recv_swap, load, stay,
 ):
     c, f = lax.axis_index("ctx"), lax.axis_index("fsdp")
     me, plane, rank = c * 4 + f, lax.div(c, 2), lax.rem(c, 2) * 4 + f
@@ -1162,11 +1201,11 @@
         pltpu.make_async_copy(source, target, load.at[i])
         for i, (source, target) in enumerate(
             (
-                (grads.at[0, pl.ds(first * half, half)], halves.at[0]),
-                (gate_came, landed.at[0]),
-                (grads.at[1, pl.ds(first * half, half)], halves.at[1]),
                 (down_keep, rest.at[2]),
                 (down_came, rest_landed.at[2]),
+                (gate_keep, rest.at[0]),
+                (gate_came, rest_landed.at[0]),
+                (grads.at[1, pl.ds(first * half, half)], halves),
                 (output_part.at[plane], output_in.at[plane]),
                 (small.at[me], small_in.at[me]),
             )
@@ -1176,35 +1215,28 @@
         copy.start()
     pl.semaphore_wait(barrier, len(peers))
 
-    def over(source, target, number, bit):
+    def over(source, target, sent, came, bit):
         return pltpu.make_async_remote_copy(
-            source, target, send_half.at[number], recv_half.at[number],
-            device_id=(flip(c, 2 * bit), f), device_id_type=MESH,
-        )
-
-    up_first = over(grads.at[1, pl.ds((1 - first) * half, half)], landed.at[1], 0, 1)
-    up_first.start()
-
-    def plus(mine, came):
-        return (mine.astype(F32) + came.astype(F32)).astype(BF16)
-
-    def join(mine, came, amount):
-        def one(i, nothing):
-            at, e = lax.div(i, OWN), lax.rem(i, OWN)
-            mine[at, e] = plus(mine[at, e], came[at, e])
-            return nothing
-
-        lax.fori_loop(0, amount * OWN, one, 0)
-
-    def second_halving(m):
-        copy = over(halves.at[m, pl.ds((1 - second) * quarter, quarter)], rest_landed.at[m], 1 + m, 2)
+            source, target, sent, came, device_id=(flip(c, 2 * bit), f), device_id_type=MESH
+        )
+
+    up_first = [
+        over(
+            grads.at[1, pl.ds((1 - first) * half, half), e], landed.at[:, e],
+            send_half.at[0, e], recv_half.at[0, e], 1,
+        )
+        for e in range(OWN)
+    ]
+    for copy in up_first:
         copy.start()
-        return copy
-
-    loads[0].wait()
-    loads[1].wait()
-    join(halves.at[0], landed.at[0], half)
-    gate_second = second_halving(0)
+    outputs = []
+    for i in range(1, planes):
+        outputs.append(
+            pltpu.make_async_remote_copy(
+                output_part.at[flip(plane, i)], output_in.at[plane], send_out.at[i - 1], recv_out.at[i - 1],
+                device_id=(flip(c, 2 * i), f), device_id_type=MESH,
+            )
+        )
     smalls = []
     for number, (i, k) in enumerate(peers):
         peer_c, peer_f = flip(c, i), flip(f, k)
@@ -1214,71 +1246,68 @@
                 device_id=(peer_c, peer_f), device_id_type=MESH,
             )
         )
-    outputs = []
-    for i in range(1, planes):
-        outputs.append(
-            pltpu.make_async_remote_copy(
-                output_part.at[flip(plane, i)], output_in.at[plane], send_out.at[i - 1], recv_out.at[i - 1],
-                device_id=(flip(c, 2 * i), f), device_id_type=MESH,
-            )
-        )
-    for copy in smalls + outputs:
+    for copy in outputs + smalls:
         copy.start()
 
-    def more_halvings(m):
+    def plus(mine, came):
+        return (mine.astype(F32) + came.astype(F32)).astype(BF16)
+
+    swaps, sent = [], []
+
+    def finish(m, e):
         count, bit, number = quarter, 4, 0
-        mine, sent = rest.at[m], []
-        join(mine, rest_landed.at[m], quarter)
+        for at in range(quarter):
+            rest[m, at, e] = plus(rest[m, at, e], rest_landed[m, at, e])
+        mine = rest.at[m, :, e]
         while count > 1:
             count //= 2
             chosen = lax.rem(lax.div(plane, bit), 2)
-            came = last_landed.at[m, number, pl.ds(0, count)]
-            copy = over(mine.at[pl.ds((1 - chosen) * count, count)], came, 4 + 2 * m + number, bit)
+            came = last_landed.at[m, number, pl.ds(0, count), e]
+            copy = over(
+                mine.at[pl.ds((1 - chosen) * count, count)], came,
+                send_deep.at[2 * m + number, e], recv_deep.at[2 * m + number, e], bit,
+            )
             copy.start()
             copy.wait_recv()
             sent.append(copy)
-            kept = last.at[m, number, pl.ds(0, count)]
             for at in range(count):
-                for e in range(OWN):
-                    kept[at, e] = plus(mine[chosen * count + at, e], came[at, e])
-            mine, bit, number = kept, bit * 2, number + 1
+                last[m, number, at, e] = plus(mine[chosen * count + at], came[at])
+            mine, bit, number = last.at[m, number, :, e], bit * 2, number + 1
         rows = turned.shape[3]
-        for e in range(OWN):
-            across = mine[0, e].astype(F32).T
-            for r in range(RANKS):
-                turned[m, r, e] = across[r * rows : (r + 1) * rows].astype(BF16)
+        across = mine[0].astype(F32).T
+        for r in range(RANKS):
+            turned[m, r, e] = across[r * rows : (r + 1) * rows].astype(BF16)
         for i in range(RANKS):
-            source, target = turned.at[m, flip(rank, i)], swapped.at[rank, m]
+            source, target = turned.at[m, flip(rank, i), e], swapped.at[rank, m, e]
             if i:
                 copy = pltpu.make_async_remote_copy(
-                    source, target, send_swap.at[m, i], recv_swap.at[m, i],
+                    source, target, send_swap.at[m * OWN + e, i], recv_swap.at[m * OWN + e, i],
                     device_id=(flip(c, i // 4), flip(f, i % 4)), device_id_type=MESH,
                 )
             else:
-                copy = pltpu.make_async_copy(source, target, load.at[7 + m])
+                copy = pltpu.make_async_copy(source, target, stay.at[m * OWN + e])
             copy.start()
             swaps.append(copy)
-        return sent
-
-    swaps = []
-    loads[3].wait()
-    loads[4].wait()
-    sent = more_halvings(2)
-    loads[2].wait()
-    up_first.wait_recv()
-    join(halves.at[1], landed.at[1], half)
-    up_second = second_halving(1)
-
-    def quarter_sum(m, copy):
+
+    for copy in loads:
+        copy.wait()
+    for e in range(OWN):
+        finish(2, e)
+    up_second = []
+    for e in range(OWN):
+        up_first[e].wait_recv()
+        for at in range(half):
+            halves[at, e] = plus(halves[at, e], landed[at, e])
+        up_second.append(
+            over(
+                halves.at[pl.ds((1 - second) * quarter, quarter), e], rest_landed.at[1, :, e],
+                send_half.at[1, e], recv_half.at[1, e], 2,
+            )
+        )
+        up_second[e].start()
         for at in range(quarter):
-            for e in range(OWN):
-                rest[m, at, e] = halves[m, second * quarter + at, e]
-        copy.wait_recv()
-
-    quarter_sum(0, gate_second)
-    sent += more_halvings(0)
-    loads[5].wait()
-    loads[6].wait()
+            rest[1, at, e] = halves[second * quarter + at, e]
+        finish(0, e)
     for copy in outputs + smalls:
         copy.wait_recv()
     made = output_in[0].astype(F32)
@@ -1286,15 +1315,16 @@
         made = made + output_in[i].astype(F32)
     output_grad[...] = made
     small_sum[...] = jnp.sum(small_in[...], axis=0)
-    quarter_sum(1, up_second)
-    sent += more_halvings(1)
+    for e in range(OWN):
+        up_second[e].wait_recv()
+        finish(1, e)
     for copy in swaps:
         copy.wait()
-    for copy in smalls + outputs + sent + [up_first, gate_second, up_second]:
+    for copy in smalls + outputs + sent + up_first + up_second:
         copy.wait_send()
 
 
-def final_sums(cid, n_ctx, small, output_part, grads, gate_came, down_keep, down_came):
+def final_sums(cid, n_ctx, small, output_part, grads, gate_keep, gate_came, down_keep, down_came):
     anywhere = pl.BlockSpec(memory_space=pl.ANY)
     inside = pl.BlockSpec(memory_space=pltpu.VMEM)
     dma = pltpu.SemaphoreType.DMA
@@ -1310,11 +1340,11 @@
             jax.ShapeDtypeStruct((slab, D), F32),
             jax.ShapeDtypeStruct(small.shape[1:], F32),
         ],
-        in_specs=[anywhere] * 6,
+        in_specs=[anywhere] * 7,
         out_specs=[anywhere] + [inside] * 2,
         scratch_shapes=[
-            pltpu.VMEM((2,) + half, BF16),
-            pltpu.VMEM((2,) + half, BF16),
+            pltpu.VMEM(half, BF16),
+            pltpu.VMEM(half, BF16),
             pltpu.VMEM((3,) + quarter, BF16),
             pltpu.VMEM((3,) + quarter, BF16),
             pltpu.VMEM(deep if planes > 4 else (1, 1, 1, 1, 8, 128), BF16),
@@ -1322,14 +1352,15 @@
             pltpu.VMEM((3, RANKS, OWN, slab, FF), BF16),
             pltpu.VMEM((planes, slab, D), BF16),
             pltpu.VMEM(small.shape, F32),
-            dma((10,)), dma((10,)), dma((planes - 1,)), dma((planes - 1,)),
-            dma((devices - 1,)), dma((devices - 1,)), dma((3, RANKS)), dma((3, RANKS)), dma((10,)),
+            dma((2, OWN)), dma((2, OWN)), dma((6, OWN)), dma((6, OWN)),
+            dma((planes - 1,)), dma((planes - 1,)), dma((devices - 1,)), dma((devices - 1,)),
+            dma((3 * OWN, RANKS)), dma((3 * OWN, RANKS)), dma((7,)), dma((3 * OWN,)),
         ],
         compiler_params=pltpu.CompilerParams(
             collective_id=cid, has_side_effects=True, vmem_limit_bytes=56 << 20
         ),
-        cost_estimate=lasting(100),
-    )(small, output_part, grads, gate_came, down_keep, down_came)
+        cost_estimate=lasting(80),
+    )(small, output_part, grads, gate_keep, gate_came, down_keep, down_came)
 
 
 def rope_tables(positions):
@@ -1443,7 +1474,7 @@
         ],
         axis=2,
     )
-    back, mix_part, own_grads = run_experts(
+    back, mix_part, own_grads, down_first, down_early = run_experts(
         2, replicas, payload.reshape(SEQS * BLOCK, PAY), cotangent.reshape(SEQS * BLOCK, D),
         (own_gate, own_up, own_down), tokens_all
     )
@@ -1473,10 +1504,13 @@
     rows = D // (n_ctx * n_fsdp)
     output_part = grad_output_w.astype(BF16).reshape(replicas, 2, 2, 2, rows, D)
 
-    input_grad, layer_out, gain_grad, output_sum, gate_came, down_keep, down_came, _, head_grads = attention_backward(
-        6, parts, n_ctx, heads_out(grad_attn, REP), q_all, kv_all, segq, codes, head_full, head_logs,
+    (
+        input_grad, layer_out, gain_grad, output_sum, _, gate_keep, gate_came, down_keep, down_came, _,
+        head_grads,
+    ) = attention_backward(
+        6, parts, n_ctx, down_early, heads_out(grad_attn, REP), q_all, kv_all, segq, codes, head_full, head_logs,
         all_cosine, all_sine, tokens.reshape(SEQS * BLOCK, D), gain_first[None],
-        grad_resid.reshape(SEQS * BLOCK, D), residual.reshape(SEQS * BLOCK, D), own_grads, mix_part, output_part,
+        grad_resid.reshape(SEQS * BLOCK, D), residual.reshape(SEQS * BLOCK, D), own_grads, down_first, mix_part, output_part,
         tokens_all.reshape(n_ctx, SEQS * BLOCK, D), full_query, full_key, full_value,
     )
     input_grad = input_grad.reshape(SEQS, BLOCK, D)
@@ -1488,7 +1522,7 @@
         small_grads.reshape(n_ctx * n_fsdp, amount), ((0, 0), (0, tiles * 128 - amount))
     ).reshape(n_ctx * n_fsdp, tiles, 128)
     swapped, output_grad, small_sum = final_sums(
-        9, n_ctx, small_grads, output_sum, own_grads, gate_came, down_keep, down_came
+        9, n_ctx, small_grads, output_sum, own_grads, gate_keep, gate_came, down_keep, down_came
     )
     small_sum = small_sum.reshape(tiles * 128)[:amount].reshape(rows, EXPERTS + 2)
     head_grads = head_grads.reshape(KEY_VALUE_HEADS, parts * n_fsdp, rows, (REP + 2) * HEAD_SIZE)

time: 637 us -> 635 us (level)
    pallas_call x1, Pallas kernels: 123 us -> 153 us  [run_experts(): pl.pallas_call(functools.partial(experts_kernel, replicas), name='experts...]
    pallas_call x1, Pallas kernels: 111 us -> 82.3 us  [final_sums(): pl.pallas_call(functools.partial(final_kernel, n_ctx), name='final_sums',...]
where the time goes in v4:
time: 635 us; the launch traced here: 626 us
  Pallas kernels  544 us (86%)
  local copies, waits for them, and re-layouts  43.9 us (7%)
  between operations  14.9 us (2%)
  matrix products  13.2 us (2%)
  other arithmetic  8.36 us (1%)
    pallas_call x1, Pallas kernels, attention_backward(): pl.pallas_call(functools.partial(attention_backward_kernel, parts, n_ctx,...  159 us
    pallas_call x1, Pallas kernels, run_experts(): pl.pallas_call(functools.partial(experts_kernel, replicas), name='experts...  153 us
    pallas_call x1, Pallas kernels, attention_forward(): pl.pallas_call(functools.partial(attention_forward_kernel, parts, n_ctx),...  150 us
    pallas_call x1, Pallas kernels, final_sums(): pl.pallas_call(functools.partial(final_kernel, n_ctx), name='final_sums',...  82.3 us
    unnamed x53, local copies, waits for them, and re-layouts  15.4 us
  transfers between devices with their start and end apart: 1, of which 0 were waited for; matrix products, arithmetic and copies ran while one was open for 5% of the time, Pallas kernels for 24%

profile of v4, /device:TPU:0, one launch (start us, length us, event | category | flops | bytes accessed | tf_op | source)
XLA Modules:
  0.0 625.6 jit_solution(12476040005192245078)
XLA Ops:
  10.7 1.0 fusion.14
  11.9 1.0 fusion.6
  13.1 1.0 copy.221.sin_ref
  14.3 1.0 copy.220.cos_ref
  16.9 1.3 copy.206.seg_ref
  18.2 2.4 constant_dynamic-slice_fusion.4
  20.6 2.7 copy.201
  23.3 1.8 copy-done.7
  25.9 2.8 copy.203
  28.6 2.7 copy.202
  32.8 150.5 %attention_forward.1 = (bf16[256,1536]{1,0:T(8,128)(2,1)}, bf16[4,32,384]{2,1,0:T(8,128)(2,1)}, bf16[4,384,1536]{2,1,0:T(8,128)(2,1)}, bf16[4,384,512]{2,1,0:T(8...) custom-call(bf16[256,1536]{1,0:T(8,128)(2,1)} %bitcast.112, ...), custom_call_target="tpu_custom_call" | custom-call | bytes 429000000 | tf_op jit(solution)/shard_map/attention_forward/pallas_call | solution.py:669
  183.2 1.6 copy.207
  185.1 4.0 multiply_reduce_fusion.2
  189.1 1.1 copy-done
  191.0 1.1 concatenate.22
  192.7 152.7 %experts.1 = (f32[256,1664]{1,0:T(8,128)}, bf16[8,256,1536]{2,1,0:T(8,128)(2,1)}, bf16[3,4,2,512,384]{4,3,2,1,0:T(8,128)(2,1)}, bf16[2,2,512,384]{3,2,1,0:T(8,12...) custom-call(bf16[256,1664]{1,0:T(8,128)(2,1)} %bitcast.117, bf16[256,1536]{1,0:T(8,128)(2,1)} %bitcast.118, ...), custom_call_target="tpu_custom_call" | custom-call | bytes 363000000 | tf_op jit(solution)/shard_map/experts/pallas_call | solution.py:337
  345.4 1.0 slice.61
  346.7 2.7 multiply_reduce_fusion
  350.6 1.4 convolution_convert_fusion
  352.2 3.7 bitcast_convert_fusion
  356.4 1.2 copy.218.g_own
  357.5 158.9 %attention_backward.1 = (bf16[256,1536]{1,0:T(8,128)(2,1)}, bf16[256,1536]{1,0:T(8,128)(2,1)}, f32[1,1536]{1,0:T(1,128)}, bf16[4,48,1536]{2,1,0:T(8,128)(2,1)}, ...) custom-call(bf16[8,3,128,128]{3,2,1,0:T(8,128)(2,1)} %copy.218.g_own, ...), custom_call_target="tpu_custom_call" | custom-call | bytes 412500000 | tf_op jit(solution)/shard_map/attention_backward/pallas_call | solution.py:1128
  516.4 1.5 convert_reduce_fusion
  519.3 0.9 reshape.264
  522.3 82.3 %final_sums.1 = (bf16[8,3,2,48,512]{4,3,2,1,0:T(8,128)(2,1)}, f32[48,1536]{1,0:T(8,128)}, f32[8,128]{1,0:T(8,128)}) custom-call(f32[32,8,128]{2,1,0:T(8,128)} %bitcast.136, bf16[4,48,1536]{2,1,0:T(8,128)(2,1)} %get-tuple-element.61.output_part, bf16[3,4,2,512,384]{4,3,2,1,0:T(8,128)(2,1)} %get-tuple-element.52.grads, ...), custom_call_target="tpu_custom_call" | custom-call | bytes 264000000 | tf_op jit(solution)/shard_map/final_sums/pallas_call | solution.py:1335
  604.7 0.8 reshape.263
  606.8 2.3 bitcast_convert_fusion.1
  609.1 2.1 copy.229
  611.2 2.1 copy.228
  613.2 2.1 copy.227
  615.3 0.9 copy.243
  616.7 0.9 copy.244
  (104 shorter events, 17.5 us)
Async XLA Ops:
  7.2 185.5 %all-gather.3.cloned.1.call-start = ((), (), s32[]{:S(2)}) async-start(), calls=%async_computation | async-start | bytes 7077888 | tf_op jit(solution)/shard_map/all_gather | solution.py:1415
  16.9 6.4 %slice-start = ((s8[6291456]{0:T(1024)(128)(4,1)}), s8[2097152]{0:T(1024)(128)(4,1)S(1)}, s32[]{:S(2)}) async-start(s8[6291456]{0:T(1024)(128)(4,1)} %bitcast.132), calls=%async_computation.1 | async-start | bytes 4194304
  18.2 5.1 slice-start.1
  20.6 4.5 copy-start.7
  28.6 2.8 copy-start.12
  28.6 2.8 copy-start.14
  28.6 3.4 copy-start.13
  183.2 1.7 copy-start.11
  183.2 1.8 copy-start.3
  184.9 4.2 copy-start.5
  189.1 1.1 copy-start
  345.4 4.5 slice-start.2
  346.7 2.7 copy-start.1
  346.7 2.7 copy-start.4
  346.7 3.8 slice-start.3
  350.5 1.4 copy-start.2
  350.6 1.7 copy-start.6
  518.2 2.7 copy-start.15
  613.2 2.1 copy-start.9
  615.3 1.4 copy-start.8
  615.3 2.3 copy-start.10
Sparse Core Ops, SparseCore 0:
  10.2 152.2 all-gather.2

commit v5 on v4

--- a/solution.py
+++ b/solution.py
@@ -408,7 +408,7 @@
     parts, n_ctx, tok, small, w_q, w_k, w_v, w_o, pack0, pack1, pack2, cos_ref, sin_ref, seg_ref, code_ref,
     normed, small_all, q_full, k_full, v_full, q_ref, kv_ref, full_ref, log_ref, o_back, o_full,
     gate_own, up_own, down_own,
-    acc, q_pack, kv_pack, o_buf,
+    acc, q_pack, kv_pack, o_buf, own_buf,
     send_w, recv_w, send_s, recv_s, send_e, recv_e, send_q, recv_q, send_kv, recv_kv, send_o, recv_o, here,
 ):
     c, f = lax.axis_index("ctx"), lax.axis_index("fsdp")
@@ -428,7 +428,7 @@
     my_rows = pl.ds(pl.multiple_of(f * rows, rows), rows)
     local = [pltpu.make_async_copy(shards[a], fulls[a].at[f], here.at[a]) for a in range(4)]
     local += [pltpu.make_async_copy(small, small_all.at[f], here.at[4])]
-    local += [pltpu.make_async_copy(packs[m].at[f], owns[m].at[:, my_rows], here.at[5 + m]) for m in range(3)]
+    local += [pltpu.make_async_copy(packs[m].at[f], own_buf.at[m], here.at[5 + m]) for m in range(3)]
     for copy in local:
         copy.start()
     pl.semaphore_wait(barrier, len(peers))
@@ -492,6 +492,11 @@
 
     for a in range(3):
         local[a].wait()
+    stores = []
+    for m in range(3):
+        local[5 + m].wait()
+        stores.append(pltpu.make_async_copy(own_buf.at[m], owns[m].at[:, my_rows], here.at[5 + m]))
+        stores[m].start()
     project(f, True)
     for a in range(3):
         weight(a, 0).wait_recv()
@@ -639,7 +644,7 @@
     for kind in (0, 2, 4):
         weight(3, kind).wait_recv()
     local[3].wait()
-    for copy in local[5:]:
+    for copy in stores:
         copy.wait()
     for copy in experts:
         copy.wait()
@@ -680,12 +685,13 @@
             full(w_o), own, own, own,
         ],
         in_specs=[inside] + [anywhere] * 8 + [inside] * 4,
-        out_specs=[inside] * 9 + [anywhere] * 5,
+        out_specs=[inside] * 9 + [anywhere, inside] + [anywhere] * 3,
         scratch_shapes=[
             pltpu.VMEM((SEQS * BLOCK, columns), F32),
             pltpu.VMEM(heads, BF16),
             pltpu.VMEM((KEY_VALUE_HEADS, 2, BLOCK, wide), BF16),
             pltpu.VMEM(heads, BF16),
+            pltpu.VMEM((3,) + packs[0].shape[1:], BF16),
             dma((4, 5)), dma((4, 5)), dma((3,)), dma((3,)), dma((3, 3)), dma((3, 3)),
             dma((others,)), dma((others,)), dma((n_ctx - 1,)), dma((n_ctx - 1,)),
             dma((KEY_VALUE_HEADS,)), dma((KEY_VALUE_HEADS,)), dma((11,)),
@@ -709,9 +715,9 @@
 def attention_backward_kernel(
     parts, n_ctx, early, g_own, q_ref, kv_ref, seg_ref, code_ref, full_ref, log_ref, cos_ref, sin_ref,
     tok, gain, resid_grad, residual, grads, down_in, mix, output_part, tokens_all, q_full, k_full, v_full,
-    input_grad, layer_out, gain_grad, output_sum, gate_first, gate_keep, gate_came, down_keep, down_came, mix_in,
-    head_in, g_ref, total, kept, came, dq_ref, dkv_ref, dq_back, dkv_back, w_q, w_k, w_v, grad_qkv, grad_in,
-    token_buf, field, head_acc, head_out, output_keep, output_came, output_x, output_pair,
+    input_grad, layer_out, gain_grad, output_sum, gate_first, gate_keep, gate_came, gate_other, down_keep, down_came,
+    mix_in, head_in, g_ref, total, kept, came, dq_ref, dkv_ref, dq_back, dkv_back, w_q, w_k, w_v, grad_qkv, grad_in,
+    token_buf, field, head_acc, head_out, head_core, head_x, output_keep, output_came, output_x, output_pair,
     send_g, recv_g, send_q, recv_q, send_kv, recv_kv, send_mix, recv_mix, send_half, recv_half, here,
     send_out, recv_out, send_head, recv_head, load_t,
 ):
@@ -798,15 +804,23 @@
     def plus(mine, came):
         return (mine.astype(F32) + came.astype(F32)).astype(BF16)
 
-    def second_halving(keep, target, number):
+    def second_halving(keep, target, number, later=None):
         def add(i, nothing):
             at, e = lax.div(i, OWN), lax.rem(i, OWN)
             kept[at, e] = plus(kept[at, e], came[at, e])
             return nothing
 
         lax.fori_loop(0, half * OWN, add, 0)
+        source = kept.at[pl.ds((1 - second) * quarter, quarter)]
+        if later is not None:
+            source, target = source.at[:, 0], target.at[:, 0]
+            rest = pltpu.make_async_copy(
+                kept.at[pl.ds((1 - second) * quarter, quarter), 1], later, here.at[3]
+            )
+            rest.start()
+            rest.wait()
         going = pltpu.make_async_remote_copy(
-            kept.at[pl.ds((1 - second) * quarter, quarter)], target, send_half.at[number], recv_half.at[number],
+            source, target, send_half.at[number], recv_half.at[number],
             device_id=(flip(c, 4), f), device_id_type=MESH,
         )
         going.start()
@@ -971,22 +985,21 @@
     lax.fori_loop(0, n_ctx, head_weights, 0)
     slab = D // (n_ctx * 4)
     for d in range(n_ctx * 4):
-        head_out[d] = head_acc[d * slab : (d + 1) * slab, : head_out.shape[2]].astype(BF16)
-    me = c * 4 + f
-    head_stays = pltpu.make_async_copy(head_out.at[me], head_in.at[me], here.at[9])
-    head_stays.start()
-    to_all = []
-    for number, (i, k) in enumerate(peers):
-        peer_c, peer_f = flip(c, i), flip(f, k)
-        to_all.append(
-            pltpu.make_async_remote_copy(
-                head_out.at[peer_c * 4 + peer_f], head_in.at[me],
-                send_head.at[number], recv_head.at[number],
-                device_id=(peer_c, peer_f), device_id_type=MESH,
-            )
-        )
-        to_all[-1].start()
-
+        head_out[d // 4, d // 2 % 2, d % 2] = head_acc[
+            d * slab : (d + 1) * slab, : head_out.shape[4]
+        ].astype(BF16)
+    head_stages = [
+        pltpu.make_async_remote_copy(
+            source, target, send_head.at[i], recv_head.at[i], device_id=device, device_id_type=MESH
+        )
+        for i, (source, target, device) in enumerate(
+            (
+                (head_out.at[:, :, 1 - core_bit], head_core, (c, flip(f, 1))),
+                (head_core.at[:, 1 - x_bit], head_x, (c, flip(f, 2))),
+            )
+        )
+    ]
+    head_stages[0].start()
     down_second.wait_send()
     leaving.wait()
     gate_halving.wait_recv()
@@ -998,7 +1011,17 @@
         copy.start()
     for copy in refill:
         copy.wait()
-    gate_second, leaving = second_halving(gate_keep, gate_came, 3)
+    gate_second, leaving = second_halving(gate_keep, gate_came, 3, gate_other)
+
+    head_stages[0].wait_recv()
+
+    def head_cores(i, nothing):
+        d, x = lax.div(i, 2), lax.rem(i, 2)
+        head_core[d, x] = plus(head_out[d, x, core_bit], head_core[d, x])
+        return nothing
+
+    lax.fori_loop(0, n_ctx * 2, head_cores, 0)
+    head_stages[1].start()
 
     def came_query(h, nothing):
         @pl.when(h != head)
@@ -1042,6 +1065,24 @@
                 value = value + dkv_back[h * parts + p, kind].astype(F32)
         return value
 
+    head_stages[1].wait_recv()
+
+    def head_over_x(d, nothing):
+        head_x[d] = plus(head_core[d, x_bit], head_x[d])
+        return nothing
+
+    lax.fori_loop(0, n_ctx, head_over_x, 0)
+    head_stays = pltpu.make_async_copy(head_x.at[c], head_in.at[c], here.at[9])
+    head_stays.start()
+    to_all = []
+    for i in range(1, n_ctx):
+        to_all.append(
+            pltpu.make_async_remote_copy(
+                head_x.at[flip(c, i)], head_in.at[c], send_head.at[1 + i], recv_head.at[1 + i],
+                device_id=(flip(c, i), f), device_id_type=MESH,
+            )
+        )
+        to_all[-1].start()
     for m in range((QUERY_HEADS + 2 * KEY_VALUE_HEADS) // 2):
         for s, value in enumerate(side_by_side(head_of(2 * m), head_of(2 * m + 1))):
             grad_qkv[s * BLOCK : (s + 1) * BLOCK, m * wide : (m + 1) * wide] = value.astype(BF16)
@@ -1107,7 +1148,7 @@
     for copy in to_all + [gate_second, leaving, head_stays]:
         copy.wait()
     down_second.wait_recv()
-    for copy in returns + output_stages + [gate_halving] + ([] if early else [down_halving]):
+    for copy in returns + output_stages + head_stages + [gate_halving] + ([] if early else [down_halving]):
         copy.wait_send()
 
 
@@ -1136,13 +1177,14 @@
             jax.ShapeDtypeStruct(half, BF16),
             jax.ShapeDtypeStruct(quarter, BF16),
             jax.ShapeDtypeStruct(quarter, BF16),
+            jax.ShapeDtypeStruct(quarter[:1] + quarter[2:], BF16),
             jax.ShapeDtypeStruct(quarter, BF16),
             jax.ShapeDtypeStruct(quarter, BF16),
             jax.ShapeDtypeStruct((RANKS - 1,) + mix.shape[1:], BF16),
-            jax.ShapeDtypeStruct((devices, slab, head_width), BF16),
+            jax.ShapeDtypeStruct((n_ctx, slab, head_width), BF16),
         ],
         in_specs=[anywhere] + [inside] * 11 + [anywhere] * 9,
-        out_specs=[inside] * 4 + [anywhere] * 7,
+        out_specs=[inside] * 4 + [anywhere] * 8,
         scratch_shapes=[
             pltpu.VMEM(q.shape, BF16),
             pltpu.VMEM((n_ctx, 2, BLOCK, wide), F32),
@@ -1160,17 +1202,19 @@
             pltpu.VMEM((2, SEQS * BLOCK, D), BF16),
             pltpu.VMEM((SEQS * BLOCK, 3 * wide), BF16),
             pltpu.VMEM((D, 3 * wide), F32),
-            pltpu.VMEM((devices, slab, head_width), BF16),
+            pltpu.VMEM((n_ctx, 2, 2, slab, head_width), BF16),
+            pltpu.VMEM((n_ctx, 2, slab, head_width), BF16),
+            pltpu.VMEM((n_ctx, slab, head_width), BF16),
             pltpu.VMEM((planes, 2, 2, slab, D), BF16),
             pltpu.VMEM((planes, 2, 2, slab, D), BF16),
             pltpu.VMEM((planes, 2, slab, D), BF16),
             pltpu.VMEM((planes, slab, D), BF16),
             dma((others,)), dma((others,)), dma((KEY_VALUE_HEADS,)), dma((KEY_VALUE_HEADS,)),
             dma((n_ctx,)), dma((n_ctx,)), dma((RANKS - 1,)), dma((RANKS - 1,)), dma((4,)), dma((4,)),
-            dma((11,)), dma((3,)), dma((3,)), dma((devices - 1,)), dma((devices - 1,)), dma((2,)),
+            dma((11,)), dma((3,)), dma((3,)), dma((n_ctx + 1,)), dma((n_ctx + 1,)), dma((2,)),
         ],
         compiler_params=pltpu.CompilerParams(
-            collective_id=cid, has_side_effects=True, vmem_limit_bytes=60 << 20
+            collective_id=cid, has_side_effects=True, vmem_limit_bytes=62 << 20
         ),
         cost_estimate=lasting(125),
     )(
@@ -1180,7 +1224,7 @@
 
 
 def final_kernel(
-    n_ctx, small, output_part, grads, gate_keep, gate_came, down_keep, down_came,
+    n_ctx, small, output_part, grads, gate_keep, gate_came, gate_other, down_keep, down_came,
     swapped, output_grad, small_sum,
     halves, landed, rest, rest_landed, last, last_landed, turned, output_in, small_in,
     send_half, recv_half, send_deep, recv_deep, send_out, recv_out, send_small, recv_small,
@@ -1204,7 +1248,7 @@
                 (down_keep, rest.at[2]),
                 (down_came, rest_landed.at[2]),
                 (gate_keep, rest.at[0]),
-                (gate_came, rest_landed.at[0]),
+                (gate_came.at[:, 0], rest_landed.at[0, :, 0]),
                 (grads.at[1, pl.ds(first * half, half)], halves),
                 (output_part.at[plane], output_in.at[plane]),
                 (small.at[me], small_in.at[me]),
@@ -1227,7 +1271,8 @@
         )
         for e in range(OWN)
     ]
-    for copy in up_first:
+    gate_second = over(gate_other, rest_landed.at[0, :, 1], send_half.at[2, 1], recv_half.at[2, 1], 2)
+    for copy in [gate_second] + up_first:
         copy.start()
     outputs = []
     for i in range(1, planes):
@@ -1293,6 +1338,7 @@
         copy.wait()
     for e in range(OWN):
         finish(2, e)
+    finish(0, 0)
     up_second = []
     for e in range(OWN):
         up_first[e].wait_recv()
@@ -1307,7 +1353,8 @@
         up_second[e].start()
         for at in range(quarter):
             rest[1, at, e] = halves[second * quarter + at, e]
-        finish(0, e)
+    gate_second.wait_recv()
+    finish(0, 1)
     for copy in outputs + smalls:
         copy.wait_recv()
     made = output_in[0].astype(F32)
@@ -1320,11 +1367,13 @@
         finish(1, e)
     for copy in swaps:
         copy.wait()
-    for copy in smalls + outputs + sent + up_first + up_second:
+    for copy in smalls + outputs + sent + up_first + up_second + [gate_second]:
         copy.wait_send()
 
 
-def final_sums(cid, n_ctx, small, output_part, grads, gate_keep, gate_came, down_keep, down_came):
+def final_sums(
+    cid, n_ctx, small, output_part, grads, gate_keep, gate_came, gate_other, down_keep, down_came
+):
     anywhere = pl.BlockSpec(memory_space=pl.ANY)
     inside = pl.BlockSpec(memory_space=pltpu.VMEM)
     dma = pltpu.SemaphoreType.DMA
@@ -1340,7 +1389,7 @@
             jax.ShapeDtypeStruct((slab, D), F32),
             jax.ShapeDtypeStruct(small.shape[1:], F32),
         ],
-        in_specs=[anywhere] * 7,
+        in_specs=[anywhere] * 8,
         out_specs=[anywhere] + [inside] * 2,
         scratch_shapes=[
             pltpu.VMEM(half, BF16),
@@ -1352,7 +1401,7 @@
             pltpu.VMEM((3, RANKS, OWN, slab, FF), BF16),
             pltpu.VMEM((planes, slab, D), BF16),
             pltpu.VMEM(small.shape, F32),
-            dma((2, OWN)), dma((2, OWN)), dma((6, OWN)), dma((6, OWN)),
+            dma((3, OWN)), dma((3, OWN)), dma((6, OWN)), dma((6, OWN)),
             dma((planes - 1,)), dma((planes - 1,)), dma((devices - 1,)), dma((devices - 1,)),
             dma((3 * OWN, RANKS)), dma((3 * OWN, RANKS)), dma((7,)), dma((3 * OWN,)),
         ],
@@ -1360,7 +1409,7 @@
             collective_id=cid, has_side_effects=True, vmem_limit_bytes=56 << 20
         ),
         cost_estimate=lasting(80),
-    )(small, output_part, grads, gate_keep, gate_came, down_keep, down_came)
+    )(small, output_part, grads, gate_keep, gate_came, gate_other, down_keep, down_came)
 
 
 def rope_tables(positions):
@@ -1505,8 +1554,8 @@
     output_part = grad_output_w.astype(BF16).reshape(replicas, 2, 2, 2, rows, D)
 
     (
-        input_grad, layer_out, gain_grad, output_sum, _, gate_keep, gate_came, down_keep, down_came, _,
-        head_grads,
+        input_grad, layer_out, gain_grad, output_sum, _, gate_keep, gate_came, gate_other, down_keep, down_came,
+        _, head_grads,
     ) = attention_backward(
         6, parts, n_ctx, down_early, heads_out(grad_attn, REP), q_all, kv_all, segq, codes, head_full, head_logs,
         all_cosine, all_sine, tokens.reshape(SEQS * BLOCK, D), gain_first[None],
@@ -1522,10 +1571,10 @@
         small_grads.reshape(n_ctx * n_fsdp, amount), ((0, 0), (0, tiles * 128 - amount))
     ).reshape(n_ctx * n_fsdp, tiles, 128)
     swapped, output_grad, small_sum = final_sums(
-        9, n_ctx, small_grads, output_sum, own_grads, gate_keep, gate_came, down_keep, down_came
+        9, n_ctx, small_grads, output_sum, own_grads, gate_keep, gate_came, gate_other, down_keep, down_came
     )
     small_sum = small_sum.reshape(tiles * 128)[:amount].reshape(rows, EXPERTS + 2)
-    head_grads = head_grads.reshape(KEY_VALUE_HEADS, parts * n_fsdp, rows, (REP + 2) * HEAD_SIZE)
+    head_grads = head_grads.reshape(KEY_VALUE_HEADS, parts, rows, (REP + 2) * HEAD_SIZE)
     own_gain = lax.dynamic_slice_in_dim(gain_first, (c_index * n_fsdp + f_index) * rows, rows, 0)
     head_grads = jnp.sum(head_grads.astype(F32), axis=1).transpose(1, 0, 2) * own_gain[:, None, None]
     query_grad = head_grads[..., : REP * HEAD_SIZE].reshape(rows, D)

time: 635 us -> 634 us (level)
    pallas_call x1, Pallas kernels: 159 us -> 150 us  [attention_backward(): pl.pallas_call(functools.partial(attention_backward_kernel, parts, n_ctx,...]
    pallas_call x1, Pallas kernels: 82.3 us -> 90.5 us  [final_sums(): pl.pallas_call(functools.partial(final_kernel, n_ctx), name='final_sums',...]
where the time goes in v5:
time: 634 us; the launch traced here: 625 us
  Pallas kernels  545 us (86%)
  local copies, waits for them, and re-layouts  43.9 us (7%)
  between operations  14.9 us (2%)
  matrix products  13.2 us (2%)
  other arithmetic  7.8 us (1%)
    pallas_call x1, Pallas kernels, run_experts(): pl.pallas_call(functools.partial(experts_kernel, replicas), name='experts...  153 us
    pallas_call x1, Pallas kernels, attention_forward(): pl.pallas_call(functools.partial(attention_forward_kernel, parts, n_ctx),...  152 us
    pallas_call x1, Pallas kernels, attention_backward(): pl.pallas_call(functools.partial(attention_backward_kernel, parts, n_ctx,...  150 us
    pallas_call x1, Pallas kernels, final_sums(): pl.pallas_call(functools.partial(final_kernel, n_ctx), name='final_sums',...  90.5 us
    unnamed x53, local copies, waits for them, and re-layouts  15.4 us
  transfers between devices with their start and end apart: 1, of which 0 were waited for; matrix products, arithmetic and copies ran while one was open for 5% of the time, Pallas kernels for 24%

profile of v5, /device:TPU:0, one launch (start us, length us, event | category | flops | bytes accessed | tf_op | source)
XLA Modules:
  0.0 625.4 jit_solution(14640407127108653379)
XLA Ops:
  10.7 1.0 fusion.14
  11.9 1.0 fusion.6
  13.1 1.0 copy.197.sin_ref
  14.3 1.0 copy.196.cos_ref
  16.9 1.3 copy.182.seg_ref
  18.2 2.4 constant_dynamic-slice_fusion.4
  20.6 2.7 copy.177
  23.3 1.8 copy-done.7
  25.9 2.8 copy.179
  28.6 2.7 copy.178
  32.8 152.0 %attention_forward.1 = (bf16[256,1536]{1,0:T(8,128)(2,1)}, bf16[4,32,384]{2,1,0:T(8,128)(2,1)}, bf16[4,384,1536]{2,1,0:T(8,128)(2,1)}, bf16[4,384,512]{2,1,0:T(8...) custom-call(bf16[256,1536]{1,0:T(8,128)(2,1)} %bitcast.109, ...), custom_call_target="tpu_custom_call" | custom-call | bytes 429000000 | tf_op jit(solution)/shard_map/attention_forward/pallas_call | solution.py:674
  184.7 1.6 copy.183
  186.6 4.0 multiply_reduce_fusion.2
  190.6 1.1 copy-done
  192.5 1.1 concatenate.22
  194.2 152.7 %experts.1 = (f32[256,1664]{1,0:T(8,128)}, bf16[8,256,1536]{2,1,0:T(8,128)(2,1)}, bf16[3,4,2,512,384]{4,3,2,1,0:T(8,128)(2,1)}, bf16[2,2,512,384]{3,2,1,0:T(8,12...) custom-call(bf16[256,1664]{1,0:T(8,128)(2,1)} %bitcast.114, bf16[256,1536]{1,0:T(8,128)(2,1)} %bitcast.115, ...), custom_call_target="tpu_custom_call" | custom-call | bytes 363000000 | tf_op jit(solution)/shard_map/experts/pallas_call | solution.py:337
  346.9 1.0 slice.61
  348.2 2.7 multiply_reduce_fusion
  352.0 1.4 convolution_convert_fusion
  353.7 3.7 bitcast_convert_fusion
  357.8 1.2 copy.194.g_own
  359.0 149.7 %attention_backward.1 = (bf16[256,1536]{1,0:T(8,128)(2,1)}, bf16[256,1536]{1,0:T(8,128)(2,1)}, f32[1,1536]{1,0:T(1,128)}, bf16[4,48,1536]{2,1,0:T(8,128)(2,1)}, ...) custom-call(bf16[8,3,128,128]{3,2,1,0:T(8,128)(2,1)} %copy.194.g_own, ...), custom_call_target="tpu_custom_call" | custom-call | bytes 412500000 | tf_op jit(solution)/shard_map/attention_backward/pallas_call | solution.py:1169
  508.7 1.1 multiply_bitcast_fusion
  511.0 0.9 reshape.265
  514.0 90.5 %final_sums.1 = (bf16[8,3,2,48,512]{4,3,2,1,0:T(8,128)(2,1)}, f32[48,1536]{1,0:T(8,128)}, f32[8,128]{1,0:T(8,128)}) custom-call(f32[32,8,128]{2,1,0:T(8,128)} %bitcast.133, bf16[4,48,1536]{2,1,0:T(8,128)(2,1)} %get-tuple-element.62.output_part, bf16[3,4,2,512,384]{4,3,2,1,0:T(8,128)(2,1)} %get-tuple-element.53.grads, ...), custom_call_target="tpu_custom_call" | custom-call | bytes 264000000 | tf_op jit(solution)/shard_map/final_sums/pallas_call | solution.py:1384
  604.5 0.8 reshape.264
  606.6 2.3 bitcast_convert_fusion.1
  608.9 2.1 copy.205
  611.0 2.1 copy.204
  613.0 2.1 copy.203
  615.1 0.9 copy.219
  616.5 0.9 copy.220
  (103 shorter events, 17.4 us)
Async XLA Ops:
  7.2 187.0 %all-gather.3.cloned.1.call-start = ((), (), s32[]{:S(2)}) async-start(), calls=%async_computation | async-start | bytes 7077888 | tf_op jit(solution)/shard_map/all_gather | solution.py:1464
  16.9 6.4 %slice-start = ((s8[6291456]{0:T(1024)(128)(4,1)}), s8[2097152]{0:T(1024)(128)(4,1)S(1)}, s32[]{:S(2)}) async-start(s8[6291456]{0:T(1024)(128)(4,1)} %bitcast.129), calls=%async_computation.1 | async-start | bytes 4194304
  18.2 5.1 slice-start.1
  20.6 4.5 copy-start.7
  28.6 2.8 copy-start.12
  28.6 2.8 copy-start.14
  28.6 3.4 copy-start.13
  184.7 1.7 copy-start.11
  184.7 1.8 copy-start.3
  186.4 4.2 copy-start.5
  190.6 1.1 copy-start
  346.9 4.5 slice-start.2
  348.2 2.7 copy-start.1
  348.2 2.7 copy-start.4
  348.2 3.8 slice-start.3
  352.0 1.4 copy-start.2
  352.0 1.7 copy-start.6
  509.9 2.7 copy-start.15
  613.0 2.1 copy-start.9
  615.1 1.4 copy-start.8
  615.1 2.3 copy-start.10
Sparse Core Ops, SparseCore 0:
  10.2 152.2 all-gather.2

commit v6 on v5

--- a/solution.py
+++ b/solution.py
@@ -405,7 +405,7 @@
 
 
 def attention_forward_kernel(
-    parts, n_ctx, tok, small, w_q, w_k, w_v, w_o, pack0, pack1, pack2, cos_ref, sin_ref, seg_ref, code_ref,
+    parts, n_ctx, tok, small, w_q, w_k, w_v, w_o, near_q, near_k, near_v, pack0, pack1, pack2, cos_ref, sin_ref, seg_ref, code_ref,
     normed, small_all, q_full, k_full, v_full, q_ref, kv_ref, full_ref, log_ref, o_back, o_full,
     gate_own, up_own, down_own,
     acc, q_pack, kv_pack, o_buf, own_buf,
@@ -435,14 +435,21 @@
     near = pl.ds(pl.multiple_of(pair * half, half), half)
     far = pl.ds(pl.multiple_of((1 - pair) * half, half), half)
     sibling, over_x, over_pair = (c, flip(f, 1)), (c, flip(f, 2)), (flip(c, 1), f)
+    nears = (near_q, near_k, near_v)
+    crossed = [
+        pltpu.make_async_copy(nears[a], fulls[a].at[flip(f, 2), near], here.at[11 + a]) for a in range(3)
+    ]
+    for copy in crossed:
+        copy.start()
 
     def weight(a, kind):
         beyond = flip(f, 2)
+        brought = nears[a] if a < 3 else fulls[a].at[beyond, near]
         source, target, device = (
             (shards[a], fulls[a].at[f], sibling),
             (shards[a].at[near], fulls[a].at[f, near], over_x),
-            (fulls[a].at[beyond, near], fulls[a].at[beyond, near], sibling),
-            (fulls[a].at[beyond, near], fulls[a].at[beyond, near], over_pair),
+            (brought, fulls[a].at[beyond, near], sibling),
+            (brought, fulls[a].at[beyond, near], over_pair),
             (fulls[a].at[beyond, far], fulls[a].at[beyond, far], sibling),
         )[kind]
         return pltpu.make_async_remote_copy(
@@ -459,8 +466,8 @@
     for copy in smalls:
         copy.start()
     for a in range(4):
-        weight(a, 1).start()
-        weight(a, 0).start()
+        for kind in (3, 0, 2) if a < 3 else (1, 0):
+            weight(a, kind).start()
     experts = [
         pltpu.make_async_remote_copy(
             packs[m].at[flip(f, i)], owns[m].at[:, my_rows], send_e.at[i - 1, m], recv_e.at[i - 1, m],
@@ -502,12 +509,9 @@
         weight(a, 0).wait_recv()
     project(flip(f, 1), False)
     for a in range(3):
-        weight(a, 1).wait_recv()
-        weight(a, 2).start()
-        weight(a, 3).start()
-    for a in range(3):
         weight(a, 3).wait_recv()
         weight(a, 4).start()
+        crossed[a].wait()
     project(flip(f, 2), False)
     for a in range(3):
         weight(a, 2).wait_recv()
@@ -651,12 +655,12 @@
     for copy in smalls + to_heads:
         copy.wait_send()
     for a in range(4):
-        for kind in range(5):
+        for kind in (0, 2, 3, 4) if a < 3 else range(5):
             weight(a, kind).wait_send()
 
 
 def attention_forward(
-    cid, parts, n_ctx, tok, small, w_q, w_k, w_v, w_o, packs, cosine, sine, segq, codes
+    cid, parts, n_ctx, tok, small, w_q, w_k, w_v, w_o, nears, packs, cosine, sine, segq, codes
 ):
     wide = 2 * HEAD_SIZE
     anywhere = pl.BlockSpec(memory_space=pl.ANY)
@@ -684,7 +688,7 @@
             jax.ShapeDtypeStruct(heads, BF16),
             full(w_o), own, own, own,
         ],
-        in_specs=[inside] + [anywhere] * 8 + [inside] * 4,
+        in_specs=[inside] + [anywhere] * 11 + [inside] * 4,
         out_specs=[inside] * 9 + [anywhere, inside] + [anywhere] * 3,
         scratch_shapes=[
             pltpu.VMEM((SEQS * BLOCK, columns), F32),
@@ -694,13 +698,13 @@
             pltpu.VMEM((3,) + packs[0].shape[1:], BF16),
             dma((4, 5)), dma((4, 5)), dma((3,)), dma((3,)), dma((3, 3)), dma((3, 3)),
             dma((others,)), dma((others,)), dma((n_ctx - 1,)), dma((n_ctx - 1,)),
-            dma((KEY_VALUE_HEADS,)), dma((KEY_VALUE_HEADS,)), dma((11,)),
+            dma((KEY_VALUE_HEADS,)), dma((KEY_VALUE_HEADS,)), dma((14,)),
         ],
         compiler_params=pltpu.CompilerParams(
             collective_id=cid, has_side_effects=True, vmem_limit_bytes=56 << 20
         ),
         cost_estimate=lasting(130),
-    )(tok, small, w_q, w_k, w_v, w_o, *packs, cosine, sine, segq, codes)
+    )(tok, small, w_q, w_k, w_v, w_o, *nears, *packs, cosine, sine, segq, codes)
 
 
 def turn_back(field, cosine, sine):
@@ -716,7 +720,7 @@
     parts, n_ctx, early, g_own, q_ref, kv_ref, seg_ref, code_ref, full_ref, log_ref, cos_ref, sin_ref,
     tok, gain, resid_grad, residual, grads, down_in, mix, output_part, tokens_all, q_full, k_full, v_full,
     input_grad, layer_out, gain_grad, output_sum, gate_first, gate_keep, gate_came, gate_other, down_keep, down_came,
-    mix_in, head_in, g_ref, total, kept, came, dq_ref, dkv_ref, dq_back, dkv_back, w_q, w_k, w_v, grad_qkv, grad_in,
+    mix_core, mix_in, head_in, g_ref, total, kept, came, dq_ref, dkv_ref, dq_back, dkv_back, w_q, w_k, w_v, grad_qkv, grad_in,
     token_buf, field, head_acc, head_out, head_core, head_x, output_keep, output_came, output_x, output_pair,
     send_g, recv_g, send_q, recv_q, send_kv, recv_kv, send_mix, recv_mix, send_half, recv_half, here,
     send_out, recv_out, send_head, recv_head, load_t,
@@ -747,7 +751,7 @@
             tokens_all.at[b], token_buf.at[lax.rem(b, 2)], load_t.at[lax.rem(b, 2)]
         )
 
-    for copy in loads + [bring(0), bring(1)]:
+    for copy in loads[1:]:
         copy.start()
     first = pltpu.make_async_copy(g_own.at[head], g_ref.at[head], here.at[0])
     first.start()
@@ -792,15 +796,16 @@
         )
     ]
     output_stages[0].start()
-    returns = []
-    for i in range(1, RANKS):
-        returns.append(
-            pltpu.make_async_remote_copy(
-                mix.at[i], mix_in.at[i - 1], send_mix.at[i - 1], recv_mix.at[i - 1],
-                device_id=(flip(c, i // 4), flip(f, i % 4)), device_id_type=MESH,
-            )
-        )
-        returns[-1].start()
+    to_core = [
+        pltpu.make_async_remote_copy(
+            mix.at[2 * k + 1], mix_core.at[k], send_mix.at[k], recv_mix.at[k],
+            device_id=(c, flip(f, 1)), device_id_type=MESH,
+        )
+        for k in range(4)
+    ]
+    for copy in to_core:
+        copy.start()
+
     def plus(mine, came):
         return (mine.astype(F32) + came.astype(F32)).astype(BF16)
 
@@ -833,6 +838,31 @@
         arriving.wait()
         down_second, leaving = second_halving(down_keep, down_came, 2)
     gate_halving.start()
+    shares = w_q.at[:, pl.ds(0, SEQS * BLOCK)]
+    for k in range(4):
+        pair_in = [
+            pltpu.make_async_copy(mix.at[2 * k], token_buf.at[0], load_t.at[0]),
+            pltpu.make_async_copy(mix_core.at[k], token_buf.at[1], load_t.at[1]),
+        ]
+        pair_in[0].start()
+        to_core[k].wait_recv()
+        pair_in[1].start()
+        for copy in pair_in:
+            copy.wait()
+        shares[k] = plus(token_buf[0], token_buf[1])
+    own_share = pltpu.make_async_copy(shares.at[0], mix_in.at[0], here.at[5])
+    own_share.start()
+    returns = [
+        pltpu.make_async_remote_copy(
+            shares.at[k], mix_in.at[k], send_mix.at[3 + k], recv_mix.at[3 + k],
+            device_id=(flip(c, k // 2), flip(f, 2 * (k % 2))), device_id_type=MESH,
+        )
+        for k in range(1, 4)
+    ]
+    for copy in returns:
+        copy.start()
+    for b in range(2):
+        bring(b).start()
     total[...] = jnp.zeros_like(total)
     first.wait()
     for copy in to_heads:
@@ -1000,6 +1030,10 @@
         )
     ]
     head_stages[0].start()
+    for copy in returns:
+        copy.wait_send()
+    own_share.wait()
+    loads[0].start()
     down_second.wait_send()
     leaving.wait()
     gate_halving.wait_recv()
@@ -1113,18 +1147,16 @@
     staying.start()
     staying.wait()
 
-    def share(i):
-        return pltpu.make_async_copy(
-            mix_in.at[i - 1] if i else mix.at[0], token_buf.at[i % 2], load_t.at[i % 2]
-        )
+    def share(k):
+        return pltpu.make_async_copy(mix_in.at[k], token_buf.at[k % 2], load_t.at[k % 2])
 
     share(0).start()
-    for i in range(RANKS):
-        if i + 1 < RANKS:
-            returns[i].wait_recv()
-            share(i + 1).start()
-        share(i).wait()
-        grad_in[...] += token_buf[i % 2].astype(F32)
+    for k in range(4):
+        if k < 3:
+            returns[k].wait_recv()
+            share(k + 1).start()
+        share(k).wait()
+        grad_in[...] += token_buf[k % 2].astype(F32)
     layer_out[...] = grad_in[...].astype(BF16)
 
     output_stages[1].wait_recv()
@@ -1148,7 +1180,7 @@
     for copy in to_all + [gate_second, leaving, head_stays]:
         copy.wait()
     down_second.wait_recv()
-    for copy in returns + output_stages + head_stages + [gate_halving] + ([] if early else [down_halving]):
+    for copy in to_core + output_stages + head_stages + [gate_halving] + ([] if early else [down_halving]):
         copy.wait_send()
 
 
@@ -1180,11 +1212,12 @@
             jax.ShapeDtypeStruct(quarter[:1] + quarter[2:], BF16),
             jax.ShapeDtypeStruct(quarter, BF16),
             jax.ShapeDtypeStruct(quarter, BF16),
-            jax.ShapeDtypeStruct((RANKS - 1,) + mix.shape[1:], BF16),
+            jax.ShapeDtypeStruct((4,) + mix.shape[1:], BF16),
+            jax.ShapeDtypeStruct((4,) + mix.shape[1:], BF16),
             jax.ShapeDtypeStruct((n_ctx, slab, head_width), BF16),
         ],
         in_specs=[anywhere] + [inside] * 11 + [anywhere] * 9,
-        out_specs=[inside] * 4 + [anywhere] * 8,
+        out_specs=[inside] * 4 + [anywhere] * 9,
         scratch_shapes=[
             pltpu.VMEM(q.shape, BF16),
             pltpu.VMEM((n_ctx, 2, BLOCK, wide), F32),
@@ -1461,6 +1494,13 @@
     head = lax.div(c_index, parts)
     positions = c_index * BLOCK + jnp.arange(BLOCK, dtype=jnp.int32)
 
+    span = D // n_fsdp // 2
+    nears = [
+        lax.ppermute(
+            lax.dynamic_slice_in_dim(w, pair * span, span, 0), "fsdp", [(a, a ^ 2) for a in range(n_fsdp)]
+        )
+        for w in (w_query, key_weight, value_weight)
+    ]
     tokens_all = lax.all_gather(tokens, "ctx", axis=0, tiled=False)
     small = jnp.concatenate(
         [
@@ -1491,7 +1531,7 @@
         attn_heads, full_output, own_gate, own_up, own_down,
     ) = attention_forward(
         0, parts, n_ctx, tokens.reshape(SEQS * BLOCK, D), small, w_query, key_weight, value_weight,
-        w_output, packs,
+        w_output, nears, packs,
         lax.dynamic_index_in_dim(all_cosine, c_index, 0, keepdims=False),
         lax.dynamic_index_in_dim(all_sine, c_index, 0, keepdims=False),
         segq, codes,
@@ -1555,7 +1595,7 @@
 
     (
         input_grad, layer_out, gain_grad, output_sum, _, gate_keep, gate_came, gate_other, down_keep, down_came,
-        _, head_grads,
+        _, _, head_grads,
     ) = attention_backward(
         6, parts, n_ctx, down_early, heads_out(grad_attn, REP), q_all, kv_all, segq, codes, head_full, head_logs,
         all_cosine, all_sine, tokens.reshape(SEQS * BLOCK, D), gain_first[None],

time: 634 us -> 578 us (0.912)
  Pallas kernels: 545 us -> 483 us
    pallas_call x1, Pallas kernels: 150 us -> 125 us  [attention_backward(): pl.pallas_call(functools.partial(attention_backward_kernel, parts, n_ctx,...]
    pallas_call x1, Pallas kernels: 152 us -> 128 us  [attention_forward(): pl.pallas_call(functools.partial(attention_forward_kernel, parts, n_ctx),...]
    pallas_call x1, Pallas kernels: 153 us -> 140 us  [run_experts(): pl.pallas_call(functools.partial(experts_kernel, replicas), name='experts...]
    unnamed x53 -> x65, local copies, waits for them, and re-layouts: 15.4 us -> 15.2 us
  transfers between devices with their start and end apart: 1 -> 4, of which waited for: 0 -> 0; matrix products, arithmetic and copies ran while one was open for 5% -> 5% of each run, Pallas kernels for 24% -> 22%
where the time goes in v6:
time: 578 us; the launch traced here: 569 us
  Pallas kernels  483 us (84%)
  local copies, waits for them, and re-layouts  45.6 us (8%)
  between operations  15 us (3%)
  matrix products  12.4 us (2%)
  other arithmetic  7.1 us (1%)
    pallas_call x1, Pallas kernels, run_experts(): pl.pallas_call(functools.partial(experts_kernel, replicas), name='experts...  140 us
    pallas_call x1, Pallas kernels, attention_forward(): pl.pallas_call(functools.partial(attention_forward_kernel, parts, n_ctx),...  128 us
    pallas_call x1, Pallas kernels, attention_backward(): pl.pallas_call(functools.partial(attention_backward_kernel, parts, n_ctx,...  125 us
    pallas_call x1, Pallas kernels, final_sums(): pl.pallas_call(functools.partial(final_kernel, n_ctx), name='final_sums',...  90.3 us
    unnamed x65, local copies, waits for them, and re-layouts  15.2 us
  transfers between devices with their start and end apart: 4, of which 0 were waited for; matrix products, arithmetic and copies ran while one was open for 5% of the time, Pallas kernels for 22%

profile of v6, /device:TPU:0, one launch (start us, length us, event | category | flops | bytes accessed | tf_op | source)
XLA Modules:
  0.0 568.8 jit_solution(15058705422128165498)
XLA Ops:
  8.0 1.6 constant_dynamic-slice_fusion.5
  9.6 2.9 collective-permute-start.2
  12.5 1.6 constant_dynamic-slice_fusion.6
  14.2 2.1 collective-permute-start
  16.9 1.0 fusion.6
  18.0 1.1 copy.197.sin_ref
  19.2 1.0 copy.196.cos_ref
  21.8 1.3 copy.182.seg_ref
  23.2 2.2 constant_dynamic-slice_fusion.4
  25.4 2.7 copy.177
  28.1 1.4 copy-done.8
  30.4 2.8 copy.179
  33.1 2.7 copy.178
  38.1 127.8 %attention_forward.1 = (bf16[256,1536]{1,0:T(8,128)(2,1)}, bf16[4,32,384]{2,1,0:T(8,128)(2,1)}, bf16[4,384,1536]{2,1,0:T(8,128)(2,1)}, bf16[4,384,512]{2,1,0:T(8...) custom-call(bf16[256,1536]{1,0:T(8,128)(2,1)} %bitcast.109, ...), custom_call_target="tpu_custom_call" | custom-call | bytes 429000000 | tf_op jit(solution)/shard_map/attention_forward/pallas_call | solution.py:678
  166.0 1.6 copy.183
  167.8 4.0 multiply_reduce_fusion.2
  171.8 1.1 copy-done
  173.7 1.1 concatenate.22
  175.4 139.7 %experts.1 = (f32[256,1664]{1,0:T(8,128)}, bf16[8,256,1536]{2,1,0:T(8,128)(2,1)}, bf16[3,4,2,512,384]{4,3,2,1,0:T(8,128)(2,1)}, bf16[2,2,512,384]{3,2,1,0:T(8,12...) custom-call(bf16[256,1664]{1,0:T(8,128)(2,1)} %bitcast.114, bf16[256,1536]{1,0:T(8,128)(2,1)} %bitcast.115, ...), custom_call_target="tpu_custom_call" | custom-call | bytes 363000000 | tf_op jit(solution)/shard_map/experts/pallas_call | solution.py:337
  315.1 1.0 slice.61
  316.4 2.7 multiply_reduce_fusion
  320.3 1.4 convolution_convert_fusion
  321.9 3.6 bitcast_convert_fusion
  326.0 1.2 copy.194.g_own
  327.2 125.0 %attention_backward.1 = (bf16[256,1536]{1,0:T(8,128)(2,1)}, bf16[256,1536]{1,0:T(8,128)(2,1)}, f32[1,1536]{1,0:T(1,128)}, bf16[4,48,1536]{2,1,0:T(8,128)(2,1)}, ...) custom-call(bf16[8,3,128,128]{3,2,1,0:T(8,128)(2,1)} %copy.194.g_own, ...), custom_call_target="tpu_custom_call" | custom-call | bytes 412500000 | tf_op jit(solution)/shard_map/attention_backward/pallas_call | solution.py:1201
  452.2 1.1 multiply_bitcast_fusion
  457.5 90.3 %final_sums.1 = (bf16[8,3,2,48,512]{4,3,2,1,0:T(8,128)(2,1)}, f32[48,1536]{1,0:T(8,128)}, f32[8,128]{1,0:T(8,128)}) custom-call(f32[32,8,128]{2,1,0:T(8,128)} %bitcast.133, bf16[4,48,1536]{2,1,0:T(8,128)(2,1)} %get-tuple-element.62.output_part, bf16[3,4,2,512,384]{4,3,2,1,0:T(8,128)(2,1)} %get-tuple-element.53.grads, ...), custom_call_target="tpu_custom_call" | custom-call | bytes 264000000 | tf_op jit(solution)/shard_map/final_sums/pallas_call | solution.py:1417
  550.0 2.3 bitcast_convert_fusion.1
  552.3 2.1 copy.205
  554.3 2.1 copy.204
  556.4 2.1 copy.203
  558.5 0.9 copy.219
  (124 shorter events, 18.3 us)
Async XLA Ops:
  7.2 7.0 %copy-start.7 = (bf16[384,1536]{1,0:T(8,128)(2,1)S(1)}, bf16[384,1536]{1,0:T(8,128)(2,1)}, u32[]{:S(2)}) copy-start(bf16[384,1536]{1,0:T(8,128)(2,1)} %w_q.1) | copy-start | bytes 3538948
  7.2 9.1 %copy-start.19 = (bf16[384]{0:T(512)(128)(2,1)S(1)}, bf16[384]{0:T(512)(128)(2,1)}, u32[]{:S(2)}) copy-start(bf16[384]{0:T(512)(128)(2,1)} %param.22) | copy-start | bytes 2308
  7.2 9.1 %copy-start.20 = (bf16[384]{0:T(512)(128)(2,1)S(1)}, bf16[384]{0:T(512)(128)(2,1)}, u32[]{:S(2)}) copy-start(bf16[384]{0:T(512)(128)(2,1)} %param.27) | copy-start | bytes 2308
  7.2 9.1 %copy-start.14 = (s32[2,1024]{1,0:T(2,128)S(1)}, s32[2,1024]{1,0:T(2,128)}, u32[]{:S(2)}) copy-start(s32[2,1024]{1,0:T(2,128)} %param.17) | copy-start | bytes 24580
  7.2 9.1 %copy-start.17 = (s32[2,128,8]{1,2,0:T(8,128)S(1)}, s32[2,128,8]{1,2,0:T(8,128)}, u32[]{:S(2)}) copy-start(s32[2,128,8]{1,2,0:T(8,128)} %param.19) | copy-start | bytes 24580
  7.2 9.2 %copy-start.21 = (s32[2,128]{1,0:T(2,128)S(1)}, s32[2,128]{1,0:T(2,128)}, u32[]{:S(2)}) copy-start(s32[2,128]{1,0:T(2,128)} %param.20) | copy-start | bytes 3076
  7.2 168.2 %all-gather.3.cloned.1.call-start = ((), (), s32[]{:S(2)}) async-start(), calls=%async_computation | async-start | bytes 7077888 | tf_op jit(solution)/shard_map/all_gather | solution.py:1504
  9.6 27.7 %collective-permute-start.2 = (bf16[192,512]{1,0:T(8,128)(2,1)}, bf16[192,512]{1,0:T(8,128)(2,1)}, u32[]{:S(2)}, u32[]{:S(2)}) collective-permute-start(bf16[192,512]{1,0:T(8,128)(2,1)} %constant_dynamic-slice_fusion.5), channel_id=1, source_target_pairs={{0,2},{1,3},{2,0},{3,1},{4,6},{5,7},{6,4},{7,5},{8,10},{9,11},{10,... | collective-permute-start | bytes 589832 | tf_op jit(solution)/shard_map/ppermute | solution.py:1499
  14.2 23.1 %collective-permute-start.1 = (bf16[192,512]{1,0:T(8,128)(2,1)}, bf16[192,512]{1,0:T(8,128)(2,1)}, u32[]{:S(2)}, u32[]{:S(2)}) collective-permute-start(bf16[192,512]{1,0:T(8,128)(2,1)} %constant_dynamic-slice_fusion.6), channel_id=1, source_target_pairs={{0,2},{1,3},{2,0},{3,1},{4,6},{5,7},{6,4},{7,5},{8,10},{9,11},{10,... | collective-permute-start | bytes 589832 | tf_op jit(solution)/shard_map/ppermute | solution.py:1499
  14.2 23.1 %collective-permute-start = (bf16[192,1536]{1,0:T(8,128)(2,1)S(1)}, bf16[192,1536]{1,0:T(8,128)(2,1)S(1)}, u32[]{:S(2)}, u32[]{:S(2)}) collective-permute-start(bf16[192,1536]{1,0:T(8,128)(2,1)S(1)} %constant_dynamic-slice_fusion.7), channel_id=1, source_target_pairs={{0,2},{1,3},{2,0},{3,1},{4,6},{5,7},{6,4},{7,5},{8,10},{9,11},{10,... | collective-permute-start | bytes 1769480 | tf_op jit(solution)/shard_map/ppermute | solution.py:1499
  21.8 6.3 %slice-start = ((s8[6291456]{0:T(1024)(128)(4,1)}), s8[2097152]{0:T(1024)(128)(4,1)S(1)}, s32[]{:S(2)}) async-start(s8[6291456]{0:T(1024)(128)(4,1)} %bitcast.129), calls=%async_computation.1 | async-start | bytes 4194304
  23.2 5.0 slice-start.1
  25.4 4.2 copy-start.8
  33.1 2.8 copy-start.15
  33.1 3.5 copy-start.16
  37.3 0.8 copy-start.11
  166.0 1.7 copy-start.13
  166.0 1.8 copy-start.3
  167.6 4.2 copy-start.5
  171.8 1.1 copy-start
  315.1 4.5 slice-start.2
  316.4 2.7 copy-start.1
  316.4 2.7 copy-start.4
  316.4 3.8 slice-start.3
  320.2 1.4 copy-start.2
  320.3 1.7 copy-start.6
  453.4 2.7 copy-start.18
  556.4 2.1 copy-start.10
  558.5 1.4 copy-start.9
  558.5 2.3 copy-start.12
Sparse Core Ops, SparseCore 0:
  10.3 145.7 all-gather.2

commit v7 on v6

--- a/solution.py
+++ b/solution.py
@@ -136,6 +136,18 @@
             copy.start()
             return copy
 
+        def arrived(chip):
+            for a in range(2):
+                push(chip, a).wait_recv()
+                forward(chip, a).start()
+
+        def fetch_chip(chip):
+            for a in range(2):
+                fetch(a, 0, landed[a].at[2 * chip - 1])
+            for a in range(2):
+                forward(chip, a).wait_recv()
+                fetch(a, 1, landed[a].at[2 * chip])
+
         @pl.when(k == 0)
         def _():
             copies = [fetch(a, 0, sources[a]) for a in range(2)]
@@ -147,20 +159,17 @@
             for copy in bring:
                 copy.wait()
 
+        @pl.when(k == 1)
+        def _():
+            arrived(1)
+            arrived(2)
+            fetch_chip(1)
+
         @pl.when(k > 0)
         def _():
             for a in range(2):
-                pltpu.make_async_remote_copy(
-                    sources[a], landed[a].at[2 * k - 1], send_first.at[k, a], recv_first.at[k, a],
-                    device_id=other_chip(c, f, k), device_id_type=MESH,
-                ).wait_recv()
-                forward(k, a).start()
-            copies = [fetch(a, 0, landed[a].at[2 * k - 1]) for a in range(2)]
-            for a in range(2):
-                forward(k, a).wait_recv()
-            copies += [fetch(a, 1, landed[a].at[2 * k]) for a in range(2)]
-            for copy in copies:
-                copy.wait()
+                for s in range(2):
+                    pltpu.make_async_copy(landed[a].at[2 * k - 1 + s], now[a].at[s], load.at[a, s]).wait()
 
         for g in range(GROUPS):
             s, at = g // 2, (g % 2) * BLOCK
@@ -255,6 +264,15 @@
         to_sibling(k).start()
         for s in range(2):
             store_mix(k, s).start()
+
+        @pl.when(k == 1)
+        def _():
+            fetch_chip(2)
+
+        @pl.when(k == 2)
+        def _():
+            arrived(3)
+            fetch_chip(3)
 
         def weight_grads(e, carry):
             for m, (left, right) in enumerate(((dgate, xs), (dup, xs), (hid, gs))):
@@ -719,7 +737,7 @@
 def attention_backward_kernel(
     parts, n_ctx, early, g_own, q_ref, kv_ref, seg_ref, code_ref, full_ref, log_ref, cos_ref, sin_ref,
     tok, gain, resid_grad, residual, grads, down_in, mix, output_part, tokens_all, q_full, k_full, v_full,
-    input_grad, layer_out, gain_grad, output_sum, gate_first, gate_keep, gate_came, gate_other, down_keep, down_came,
+    input_grad, layer_out, gain_grad, output_sum, gate_first, gate_keep, gate_came, gate_other, up_came, down_keep, down_came,
     mix_core, mix_in, head_in, g_ref, total, kept, came, dq_ref, dkv_ref, dq_back, dkv_back, w_q, w_k, w_v, grad_qkv, grad_in,
     token_buf, field, head_acc, head_out, head_core, head_x, output_keep, output_came, output_x, output_pair,
     send_g, recv_g, send_q, recv_q, send_kv, recv_kv, send_mix, recv_mix, send_half, recv_half, here,
@@ -781,6 +799,10 @@
     down_halving, gate_halving = halving(2, came, 0), halving(0, gate_first, 1)
     arriving = pltpu.make_async_copy(down_in, came, here.at[10]) if early else down_halving
     arriving.start()
+    up_halving = pltpu.make_async_remote_copy(
+        grads.at[1, pl.ds((1 - mine) * half, half), 0], up_came, send_half.at[4], recv_half.at[4],
+        device_id=(flip(c, 2), f), device_id_type=MESH,
+    )
     keeping = pltpu.make_async_copy(grads.at[2, pl.ds(mine * half, half)], kept, here.at[3])
     keeping.start()
     output_stages = [
@@ -960,6 +982,7 @@
         return nothing
 
     lax.fori_loop(0, n_ctx, finish, 0)
+    up_halving.start()
     if not early:
         keeping.wait()
         down_halving.wait_recv()
@@ -1177,7 +1200,7 @@
     lax.fori_loop(0, planes, over_pair, 0)
     for copy in to_heads:
         copy.wait_send()
-    for copy in to_all + [gate_second, leaving, head_stays]:
+    for copy in to_all + [gate_second, up_halving, leaving, head_stays]:
         copy.wait()
     down_second.wait_recv()
     for copy in to_core + output_stages + head_stages + [gate_halving] + ([] if early else [down_halving]):
@@ -1210,6 +1233,7 @@
             jax.ShapeDtypeStruct(quarter, BF16),
             jax.ShapeDtypeStruct(quarter, BF16),
             jax.ShapeDtypeStruct(quarter[:1] + quarter[2:], BF16),
+            jax.ShapeDtypeStruct(half[:1] + half[2:], BF16),
             jax.ShapeDtypeStruct(quarter, BF16),
             jax.ShapeDtypeStruct(quarter, BF16),
             jax.ShapeDtypeStruct((4,) + mix.shape[1:], BF16),
@@ -1217,7 +1241,7 @@
             jax.ShapeDtypeStruct((n_ctx, slab, head_width), BF16),
         ],
         in_specs=[anywhere] + [inside] * 11 + [anywhere] * 9,
-        out_specs=[inside] * 4 + [anywhere] * 9,
+        out_specs=[inside] * 4 + [anywhere] * 10,
         scratch_shapes=[
             pltpu.VMEM(q.shape, BF16),
             pltpu.VMEM((n_ctx, 2, BLOCK, wide), F32),
@@ -1243,7 +1267,7 @@
             pltpu.VMEM((planes, 2, slab, D), BF16),
             pltpu.VMEM((planes, slab, D), BF16),
             dma((others,)), dma((others,)), dma((KEY_VALUE_HEADS,)), dma((KEY_VALUE_HEADS,)),
-            dma((n_ctx,)), dma((n_ctx,)), dma((RANKS - 1,)), dma((RANKS - 1,)), dma((4,)), dma((4,)),
+            dma((n_ctx,)), dma((n_ctx,)), dma((RANKS - 1,)), dma((RANKS - 1,)), dma((5,)), dma((5,)),
             dma((11,)), dma((3,)), dma((3,)), dma((n_ctx + 1,)), dma((n_ctx + 1,)), dma((2,)),
         ],
         compiler_params=pltpu.CompilerParams(
@@ -1257,7 +1281,7 @@
 
 
 def final_kernel(
-    n_ctx, small, output_part, grads, gate_keep, gate_came, gate_other, down_keep, down_came,
+    n_ctx, small, output_part, grads, gate_keep, gate_came, gate_other, up_came, down_keep, down_came,
     swapped, output_grad, small_sum,
     halves, landed, rest, rest_landed, last, last_landed, turned, output_in, small_in,
     send_half, recv_half, send_deep, recv_deep, send_out, recv_out, send_small, recv_small,
@@ -1285,6 +1309,7 @@
                 (grads.at[1, pl.ds(first * half, half)], halves),
                 (output_part.at[plane], output_in.at[plane]),
                 (small.at[me], small_in.at[me]),
+                (up_came, landed.at[:, 0]),
             )
         )
     ]
@@ -1297,16 +1322,12 @@
             source, target, sent, came, device_id=(flip(c, 2 * bit), f), device_id_type=MESH
         )
 
-    up_first = [
-        over(
-            grads.at[1, pl.ds((1 - first) * half, half), e], landed.at[:, e],
-            send_half.at[0, e], recv_half.at[0, e], 1,
-        )
-        for e in range(OWN)
-    ]
+    up_first = over(
+        grads.at[1, pl.ds((1 - first) * half, half), 1], landed.at[:, 1],
+        send_half.at[0, 1], recv_half.at[0, 1], 1,
+    )
     gate_second = over(gate_other, rest_landed.at[0, :, 1], send_half.at[2, 1], recv_half.at[2, 1], 2)
-    for copy in [gate_second] + up_first:
-        copy.start()
+    up_first.start()
     outputs = []
     for i in range(1, planes):
         outputs.append(
@@ -1324,8 +1345,6 @@
                 device_id=(peer_c, peer_f), device_id_type=MESH,
             )
         )
-    for copy in outputs + smalls:
-        copy.start()
 
     def plus(mine, came):
         return (mine.astype(F32) + came.astype(F32)).astype(BF16)
@@ -1369,12 +1388,9 @@
 
     for copy in loads:
         copy.wait()
-    for e in range(OWN):
-        finish(2, e)
-    finish(0, 0)
     up_second = []
-    for e in range(OWN):
-        up_first[e].wait_recv()
+
+    def second_of_up(e):
         for at in range(half):
             halves[at, e] = plus(halves[at, e], landed[at, e])
         up_second.append(
@@ -1386,6 +1402,16 @@
         up_second[e].start()
         for at in range(quarter):
             rest[1, at, e] = halves[second * quarter + at, e]
+
+    second_of_up(0)
+    gate_second.start()
+    for copy in outputs + smalls:
+        copy.start()
+    for e in range(OWN):
+        finish(2, e)
+    finish(0, 0)
+    up_first.wait_recv()
+    second_of_up(1)
     gate_second.wait_recv()
     finish(0, 1)
     for copy in outputs + smalls:
@@ -1400,12 +1426,13 @@
         finish(1, e)
     for copy in swaps:
         copy.wait()
-    for copy in smalls + outputs + sent + up_first + up_second + [gate_second]:
+    for copy in smalls + outputs + sent + up_second + [up_first, gate_second]:
         copy.wait_send()
 
 
 def final_sums(
-    cid, n_ctx, small, output_part, grads, gate_keep, gate_came, gate_other, down_keep, down_came
+    cid, n_ctx, small, output_part, grads, gate_keep, gate_came, gate_other, up_came, down_keep,
+    down_came
 ):
     anywhere = pl.BlockSpec(memory_space=pl.ANY)
     inside = pl.BlockSpec(memory_space=pltpu.VMEM)
@@ -1422,7 +1449,7 @@
             jax.ShapeDtypeStruct((slab, D), F32),
             jax.ShapeDtypeStruct(small.shape[1:], F32),
         ],
-        in_specs=[anywhere] * 8,
+        in_specs=[anywhere] * 9,
         out_specs=[anywhere] + [inside] * 2,
         scratch_shapes=[
             pltpu.VMEM(half, BF16),
@@ -1436,13 +1463,13 @@
             pltpu.VMEM(small.shape, F32),
             dma((3, OWN)), dma((3, OWN)), dma((6, OWN)), dma((6, OWN)),
             dma((planes - 1,)), dma((planes - 1,)), dma((devices - 1,)), dma((devices - 1,)),
-            dma((3 * OWN, RANKS)), dma((3 * OWN, RANKS)), dma((7,)), dma((3 * OWN,)),
+            dma((3 * OWN, RANKS)), dma((3 * OWN, RANKS)), dma((8,)), dma((3 * OWN,)),
         ],
         compiler_params=pltpu.CompilerParams(
             collective_id=cid, has_side_effects=True, vmem_limit_bytes=56 << 20
         ),
         cost_estimate=lasting(80),
-    )(small, output_part, grads, gate_keep, gate_came, gate_other, down_keep, down_came)
+    )(small, output_part, grads, gate_keep, gate_came, gate_other, up_came, down_keep, down_came)
 
 
 def rope_tables(positions):
@@ -1594,8 +1621,8 @@
     output_part = grad_output_w.astype(BF16).reshape(replicas, 2, 2, 2, rows, D)
 
     (
-        input_grad, layer_out, gain_grad, output_sum, _, gate_keep, gate_came, gate_other, down_keep, down_came,
-        _, _, head_grads,
+        input_grad, layer_out, gain_grad, output_sum, _, gate_keep, gate_came, gate_other, up_came, down_keep,
+        down_came, _, _, head_grads,
     ) = attention_backward(
         6, parts, n_ctx, down_early, heads_out(grad_attn, REP), q_all, kv_all, segq, codes, head_full, head_logs,
         all_cosine, all_sine, tokens.reshape(SEQS * BLOCK, D), gain_first[None],
@@ -1611,7 +1638,8 @@
         small_grads.reshape(n_ctx * n_fsdp, amount), ((0, 0), (0, tiles * 128 - amount))
     ).reshape(n_ctx * n_fsdp, tiles, 128)
     swapped, output_grad, small_sum = final_sums(
-        9, n_ctx, small_grads, output_sum, own_grads, gate_keep, gate_came, gate_other, down_keep, down_came
+        9, n_ctx, small_grads, output_sum, own_grads, gate_keep, gate_came, gate_other, up_came,
+        down_keep, down_came,
     )
     small_sum = small_sum.reshape(tiles * 128)[:amount].reshape(rows, EXPERTS + 2)
     head_grads = head_grads.reshape(KEY_VALUE_HEADS, parts, rows, (REP + 2) * HEAD_SIZE)

time: 578 us -> 569 us (0.984)
  Pallas kernels: 483 us -> 474 us
    pallas_call x1, Pallas kernels: 90.3 us -> 80.2 us  [final_sums(): pl.pallas_call(functools.partial(final_kernel, n_ctx), name='final_sums',...]
  transfers between devices with their start and end apart: 4 -> 4, of which waited for: 0 -> 0; matrix products, arithmetic and copies ran while one was open for 5% -> 6% of each run, Pallas kernels for 22% -> 23%
where the time goes in v7:
time: 569 us; the launch traced here: 560 us
  Pallas kernels  474 us (83%)
  local copies, waits for them, and re-layouts  45.6 us (8%)
  between operations  15 us (3%)
  matrix products  12.4 us (2%)
  other arithmetic  7.1 us (1%)
    pallas_call x1, Pallas kernels, run_experts(): pl.pallas_call(functools.partial(experts_kernel, replicas), name='experts...  138 us
    pallas_call x1, Pallas kernels, attention_backward(): pl.pallas_call(functools.partial(attention_backward_kernel, parts, n_ctx,...  128 us
    pallas_call x1, Pallas kernels, attention_forward(): pl.pallas_call(functools.partial(attention_forward_kernel, parts, n_ctx),...  128 us
    pallas_call x1, Pallas kernels, final_sums(): pl.pallas_call(functools.partial(final_kernel, n_ctx), name='final_sums',...  80.2 us
    unnamed x65, local copies, waits for them, and re-layouts  15.2 us
  transfers between devices with their start and end apart: 4, of which 0 were waited for; matrix products, arithmetic and copies ran while one was open for 6% of the time, Pallas kernels for 23%

profile of v7, /device:TPU:0, one launch (start us, length us, event | category | flops | bytes accessed | tf_op | source)
XLA Modules:
  0.0 560.2 jit_solution(14176523311858950382)
XLA Ops:
  8.0 1.6 constant_dynamic-slice_fusion.5
  9.6 2.9 collective-permute-start.2
  12.5 1.6 constant_dynamic-slice_fusion.6
  14.2 2.1 collective-permute-start
  16.9 1.0 fusion.6
  18.0 1.1 copy.197.sin_ref
  19.2 1.0 copy.196.cos_ref
  21.8 1.3 copy.182.seg_ref
  23.2 2.2 constant_dynamic-slice_fusion.4
  25.4 2.7 copy.177
  28.1 1.4 copy-done.8
  30.4 2.8 copy.179
  33.1 2.7 copy.178
  38.1 127.8 %attention_forward.1 = (bf16[256,1536]{1,0:T(8,128)(2,1)}, bf16[4,32,384]{2,1,0:T(8,128)(2,1)}, bf16[4,384,1536]{2,1,0:T(8,128)(2,1)}, bf16[4,384,512]{2,1,0:T(8...) custom-call(bf16[256,1536]{1,0:T(8,128)(2,1)} %bitcast.109, ...), custom_call_target="tpu_custom_call" | custom-call | bytes 429000000 | tf_op jit(solution)/shard_map/attention_forward/pallas_call | solution.py:696
  166.0 1.6 copy.183
  167.8 4.0 multiply_reduce_fusion.2
  171.8 1.1 copy-done
  173.7 1.1 concatenate.22
  175.4 138.3 %experts.1 = (f32[256,1664]{1,0:T(8,128)}, bf16[8,256,1536]{2,1,0:T(8,128)(2,1)}, bf16[3,4,2,512,384]{4,3,2,1,0:T(8,128)(2,1)}, bf16[2,2,512,384]{3,2,1,0:T(8,12...) custom-call(bf16[256,1664]{1,0:T(8,128)(2,1)} %bitcast.114, bf16[256,1536]{1,0:T(8,128)(2,1)} %bitcast.115, ...), custom_call_target="tpu_custom_call" | custom-call | bytes 363000000 | tf_op jit(solution)/shard_map/experts/pallas_call | solution.py:355
  313.7 1.0 slice.61
  315.0 2.7 multiply_reduce_fusion
  318.9 1.4 convolution_convert_fusion
  320.5 3.6 bitcast_convert_fusion
  324.6 1.2 copy.194.g_own
  325.8 128.0 %attention_backward.1 = (bf16[256,1536]{1,0:T(8,128)(2,1)}, bf16[256,1536]{1,0:T(8,128)(2,1)}, f32[1,1536]{1,0:T(1,128)}, bf16[4,48,1536]{2,1,0:T(8,128)(2,1)}, ...) custom-call(bf16[8,3,128,128]{3,2,1,0:T(8,128)(2,1)} %copy.194.g_own, ...), custom_call_target="tpu_custom_call" | custom-call | bytes 412500000 | tf_op jit(solution)/shard_map/attention_backward/pallas_call | solution.py:1224
  453.8 1.1 multiply_bitcast_fusion
  459.1 80.2 %final_sums.1 = (bf16[8,3,2,48,512]{4,3,2,1,0:T(8,128)(2,1)}, f32[48,1536]{1,0:T(8,128)}, f32[8,128]{1,0:T(8,128)}) custom-call(f32[32,8,128]{2,1,0:T(8,128)} %bitcast.133, bf16[4,48,1536]{2,1,0:T(8,128)(2,1)} %get-tuple-element.63.output_part, bf16[3,4,2,512,384]{4,3,2,1,0:T(8,128)(2,1)} %get-tuple-element.54.grads, ...), custom_call_target="tpu_custom_call" | custom-call | bytes 264000000 | tf_op jit(solution)/shard_map/final_sums/pallas_call | solution.py:1444
  541.5 2.3 bitcast_convert_fusion.1
  543.8 2.1 copy.205
  545.8 2.1 copy.204
  547.9 2.1 copy.203
  549.9 0.9 copy.219
  (124 shorter events, 18.3 us)
Async XLA Ops:
  7.2 7.0 %copy-start.7 = (bf16[384,1536]{1,0:T(8,128)(2,1)S(1)}, bf16[384,1536]{1,0:T(8,128)(2,1)}, u32[]{:S(2)}) copy-start(bf16[384,1536]{1,0:T(8,128)(2,1)} %w_q.1) | copy-start | bytes 3538948
  7.2 9.1 %copy-start.19 = (bf16[384]{0:T(512)(128)(2,1)S(1)}, bf16[384]{0:T(512)(128)(2,1)}, u32[]{:S(2)}) copy-start(bf16[384]{0:T(512)(128)(2,1)} %param.22) | copy-start | bytes 2308
  7.2 9.1 %copy-start.20 = (bf16[384]{0:T(512)(128)(2,1)S(1)}, bf16[384]{0:T(512)(128)(2,1)}, u32[]{:S(2)}) copy-start(bf16[384]{0:T(512)(128)(2,1)} %param.27) | copy-start | bytes 2308
  7.2 9.1 %copy-start.14 = (s32[2,1024]{1,0:T(2,128)S(1)}, s32[2,1024]{1,0:T(2,128)}, u32[]{:S(2)}) copy-start(s32[2,1024]{1,0:T(2,128)} %param.17) | copy-start | bytes 24580
  7.2 9.1 %copy-start.17 = (s32[2,128,8]{1,2,0:T(8,128)S(1)}, s32[2,128,8]{1,2,0:T(8,128)}, u32[]{:S(2)}) copy-start(s32[2,128,8]{1,2,0:T(8,128)} %param.19) | copy-start | bytes 24580
  7.2 9.2 %copy-start.21 = (s32[2,128]{1,0:T(2,128)S(1)}, s32[2,128]{1,0:T(2,128)}, u32[]{:S(2)}) copy-start(s32[2,128]{1,0:T(2,128)} %param.20) | copy-start | bytes 3076
  7.2 168.2 %all-gather.3.cloned.1.call-start = ((), (), s32[]{:S(2)}) async-start(), calls=%async_computation | async-start | bytes 7077888 | tf_op jit(solution)/shard_map/all_gather | solution.py:1531
  9.6 27.7 %collective-permute-start.2 = (bf16[192,512]{1,0:T(8,128)(2,1)}, bf16[192,512]{1,0:T(8,128)(2,1)}, u32[]{:S(2)}, u32[]{:S(2)}) collective-permute-start(bf16[192,512]{1,0:T(8,128)(2,1)} %constant_dynamic-slice_fusion.5), channel_id=1, source_target_pairs={{0,2},{1,3},{2,0},{3,1},{4,6},{5,7},{6,4},{7,5},{8,10},{9,11},{10,... | collective-permute-start | bytes 589832 | tf_op jit(solution)/shard_map/ppermute | solution.py:1526
  14.2 23.1 %collective-permute-start.1 = (bf16[192,512]{1,0:T(8,128)(2,1)}, bf16[192,512]{1,0:T(8,128)(2,1)}, u32[]{:S(2)}, u32[]{:S(2)}) collective-permute-start(bf16[192,512]{1,0:T(8,128)(2,1)} %constant_dynamic-slice_fusion.6), channel_id=1, source_target_pairs={{0,2},{1,3},{2,0},{3,1},{4,6},{5,7},{6,4},{7,5},{8,10},{9,11},{10,... | collective-permute-start | bytes 589832 | tf_op jit(solution)/shard_map/ppermute | solution.py:1526
  14.2 23.1 %collective-permute-start = (bf16[192,1536]{1,0:T(8,128)(2,1)S(1)}, bf16[192,1536]{1,0:T(8,128)(2,1)S(1)}, u32[]{:S(2)}, u32[]{:S(2)}) collective-permute-start(bf16[192,1536]{1,0:T(8,128)(2,1)S(1)} %constant_dynamic-slice_fusion.7), channel_id=1, source_target_pairs={{0,2},{1,3},{2,0},{3,1},{4,6},{5,7},{6,4},{7,5},{8,10},{9,11},{10,... | collective-permute-start | bytes 1769480 | tf_op jit(solution)/shard_map/ppermute | solution.py:1526
  21.8 6.3 %slice-start = ((s8[6291456]{0:T(1024)(128)(4,1)}), s8[2097152]{0:T(1024)(128)(4,1)S(1)}, s32[]{:S(2)}) async-start(s8[6291456]{0:T(1024)(128)(4,1)} %bitcast.129), calls=%async_computation.1 | async-start | bytes 4194304
  23.2 5.0 slice-start.1
  25.4 4.2 copy-start.8
  33.1 2.8 copy-start.15
  33.1 3.5 copy-start.16
  37.3 0.8 copy-start.11
  166.0 1.7 copy-start.13
  166.0 1.8 copy-start.3
  167.6 4.2 copy-start.5
  171.8 1.1 copy-start
  313.7 4.5 slice-start.2
  315.0 2.7 copy-start.1
  315.0 2.7 copy-start.4
  315.0 3.8 slice-start.3
  318.9 1.4 copy-start.2
  318.9 1.7 copy-start.6
  455.0 2.7 copy-start.18
  547.9 2.1 copy-start.10
  549.9 1.4 copy-start.9
  549.9 2.3 copy-start.12
Sparse Core Ops, SparseCore 0:
  10.3 145.7 all-gather.2

commit v8 on v7

--- a/solution.py
+++ b/solution.py
@@ -118,6 +118,28 @@
 
     for k, a in ((0, 0), (0, 1), (1, 0), (2, 0), (1, 1), (2, 1), (3, 0), (3, 1)):
         push(k, a).start()
+
+    stages = (eo, gi)
+
+    def leaving(m, e, stage):
+        if not apart:
+            return [pltpu.make_async_copy(stages[stage].at[:FF], grads.at[m, e], piece_sem.at[stage, 0])]
+        width = D // replicas
+        return [
+            pltpu.make_async_copy(
+                stages[stage].at[:FF, plane * width : (plane + 1) * width],
+                grads.at[m, at, e],
+                piece_sem.at[stage, at],
+            )
+            for at, plane in enumerate(plane_order(replicas))
+        ]
+
+    if apart:
+        half = replicas // 2
+        down_first = pltpu.make_async_remote_copy(
+            grads.at[2, pl.ds((1 - lax.rem(lax.div(c, 2), 2)) * half, half)], down_came,
+            send_down, recv_down, device_id=(flip(c, 2), f), device_id_type=MESH,
+        )
 
     def clear(i, carry):
         total[lax.div(i, OWN), lax.rem(i, OWN)] = jnp.zeros((FF, D), F32)
@@ -274,14 +296,38 @@
             arrived(3)
             fetch_chip(3)
 
-        def weight_grads(e, carry):
-            for m, (left, right) in enumerate(((dgate, xs), (dup, xs), (hid, gs))):
+        def down_grads(e, carry):
+            total[2, e] += lax.dot_general(
+                hid[e], gs[e], (((0,), (0,)), ((), ())), preferred_element_type=F32
+            )
+            return carry
+
+        def other_grads(e, carry):
+            for m, left in enumerate((dgate, dup)):
                 total[m, e] += lax.dot_general(
-                    left[e], right[e], (((0,), (0,)), ((), ())), preferred_element_type=F32
+                    left[e], xs[e], (((0,), (0,)), ((), ())), preferred_element_type=F32
                 )
             return carry
 
-        lax.fori_loop(0, OWN, weight_grads, 0)
+        lax.fori_loop(0, OWN, down_grads, 0)
+
+        @pl.when(k == 3)
+        def _():
+            for e in range(OWN):
+                stages[e][:FF] = total[2, e].astype(BF16)
+                for copy in leaving(2, e, e):
+                    copy.start()
+
+        lax.fori_loop(0, OWN, other_grads, 0)
+
+        @pl.when(k == 3)
+        def _():
+            for e in range(OWN):
+                for copy in leaving(2, e, e):
+                    copy.wait()
+            if apart:
+                down_first.start()
+
         to_sibling(k).wait_recv()
         sib[k] = (sib[k].astype(F32) + own[parity].astype(F32)).astype(BF16)
 
@@ -294,41 +340,17 @@
     lax.fori_loop(0, 4, chunk, 0)
     for s in range(2):
         store_mix(3, s).wait()
-    stages = (eo, gi)
-    pending = []
-    if apart:
-        half = replicas // 2
-        down_first = pltpu.make_async_remote_copy(
-            grads.at[2, pl.ds((1 - lax.rem(lax.div(c, 2), 2)) * half, half)], down_came,
-            send_down, recv_down, device_id=(flip(c, 2), f), device_id_type=MESH,
-        )
-    for i in range(3 * OWN):
-        m, e = (2, 0, 1)[i // OWN], i % OWN
+    for i in range(2 * OWN):
+        m, e = i // OWN, i % OWN
         if i >= 2:
-            for copy in pending[i - 2]:
+            for copy in leaving((i - 2) // OWN, (i - 2) % OWN, i % 2):
                 copy.wait()
-        if i == OWN + 1 and apart:
-            down_first.start()
         stages[i % 2][:FF] = total[m, e].astype(BF16)
-        pending.append([])
-        if not apart:
-            pending[i].append(
-                pltpu.make_async_copy(stages[i % 2].at[:FF], grads.at[m, e], piece_sem.at[i % 2, 0])
-            )
-        else:
-            width = D // replicas
-            for at, plane in enumerate(plane_order(replicas)):
-                pending[i].append(
-                    pltpu.make_async_copy(
-                        stages[i % 2].at[:FF, plane * width : (plane + 1) * width],
-                        grads.at[m, at, e],
-                        piece_sem.at[i % 2, at],
-                    )
-                )
-        for copy in pending[i]:
+        for copy in leaving(m, e, i % 2):
             copy.start()
-    for copy in pending[-2] + pending[-1]:
-        copy.wait()
+    for i in (2 * OWN - 2, 2 * OWN - 1):
+        for copy in leaving(i // OWN, i % OWN, i % 2):
+            copy.wait()
     for k in (2, 3):
         to_sibling(k).wait_send()
     for k in range(4):
@@ -428,6 +450,7 @@
     gate_own, up_own, down_own,
     acc, q_pack, kv_pack, o_buf, own_buf,
     send_w, recv_w, send_s, recv_s, send_e, recv_e, send_q, recv_q, send_kv, recv_kv, send_o, recv_o, here,
+    send_z, recv_z,
 ):
     c, f = lax.axis_index("ctx"), lax.axis_index("fsdp")
     head, part, pair = lax.div(c, parts), lax.rem(c, parts), lax.rem(c, 2)
@@ -486,15 +509,34 @@
     for a in range(4):
         for kind in (3, 0, 2) if a < 3 else (1, 0):
             weight(a, kind).start()
+    bit = lax.rem(lax.div(c, 2), 2)
+    half_rows = pl.ds(pl.multiple_of(bit * half, half), half)
+
+    def half_of(owner):
+        return pl.ds(pl.multiple_of(owner * rows + bit * half, half), half)
+
+    shared = [
+        pltpu.make_async_remote_copy(
+            packs[2].at[flip(f, i), :, half_rows], owns[2].at[:, half_of(f)],
+            send_e.at[i - 1, 2], recv_e.at[i - 1, 2], device_id=(c, flip(f, i)), device_id_type=MESH,
+        )
+        for i in (2, 3)
+    ]
+    onward = [
+        pltpu.make_async_remote_copy(
+            owns[2].at[:, half_of(flip(f, i))], owns[2].at[:, half_of(flip(f, i))],
+            send_z.at[i - 2], recv_z.at[i - 2], device_id=(flip(c, 2), f), device_id_type=MESH,
+        )
+        for i in (2, 3)
+    ]
     experts = [
         pltpu.make_async_remote_copy(
             packs[m].at[flip(f, i)], owns[m].at[:, my_rows], send_e.at[i - 1, m], recv_e.at[i - 1, m],
             device_id=(c, flip(f, i)), device_id_type=MESH,
         )
-        for m in range(3)
-        for i in range(1, 4)
+        for m, i in ((2, 1), (0, 1), (0, 2), (0, 3), (1, 1), (1, 2), (1, 3))
     ]
-    for copy in experts:
+    for copy in shared + experts:
         copy.start()
 
     x = tok[...].astype(F32)
@@ -579,6 +621,9 @@
     kv_stays.wait()
     for copy in to_heads:
         copy.wait_recv()
+    for came, goes in zip(shared, onward):
+        came.wait_recv()
+        goes.start()
 
     count = REP * BLOCK
     halves = half_masks(BF16)
@@ -668,9 +713,9 @@
     local[3].wait()
     for copy in stores:
         copy.wait()
-    for copy in experts:
+    for copy in experts + onward:
         copy.wait()
-    for copy in smalls + to_heads:
+    for copy in smalls + to_heads + shared:
         copy.wait_send()
     for a in range(4):
         for kind in (0, 2, 3, 4) if a < 3 else range(5):
@@ -716,7 +761,7 @@
             pltpu.VMEM((3,) + packs[0].shape[1:], BF16),
             dma((4, 5)), dma((4, 5)), dma((3,)), dma((3,)), dma((3, 3)), dma((3, 3)),
             dma((others,)), dma((others,)), dma((n_ctx - 1,)), dma((n_ctx - 1,)),
-            dma((KEY_VALUE_HEADS,)), dma((KEY_VALUE_HEADS,)), dma((14,)),
+            dma((KEY_VALUE_HEADS,)), dma((KEY_VALUE_HEADS,)), dma((14,)), dma((2,)), dma((2,)),
         ],
         compiler_params=pltpu.CompilerParams(
             collective_id=cid, has_side_effects=True, vmem_limit_bytes=56 << 20

time: 569 us -> 604 us (1.062)
  Pallas kernels: 474 us -> 509 us
    pallas_call x1, Pallas kernels: 128 us -> 155 us  [attention_backward(): pl.pallas_call(functools.partial(attention_backward_kernel, parts, n_ctx,...]
    pallas_call x1, Pallas kernels: 128 us -> 137 us  [attention_forward(): pl.pallas_call(functools.partial(attention_forward_kernel, parts, n_ctx),...]
  transfers between devices with their start and end apart: 4 -> 4, of which waited for: 0 -> 0; matrix products, arithmetic and copies ran while one was open for 6% -> 5% of each run, Pallas kernels for 23% -> 23%
where the time goes in v8:
time: 604 us; the launch traced here: 595 us
  Pallas kernels  509 us (84%)
  local copies, waits for them, and re-layouts  45.6 us (8%)
  between operations  14.8 us (2%)
  matrix products  12.4 us (2%)
  other arithmetic  7.1 us (1%)
    pallas_call x1, Pallas kernels, attention_backward(): pl.pallas_call(functools.partial(attention_backward_kernel, parts, n_ctx,...  155 us
    pallas_call x1, Pallas kernels, attention_forward(): pl.pallas_call(functools.partial(attention_forward_kernel, parts, n_ctx),...  137 us
    pallas_call x1, Pallas kernels, run_experts(): pl.pallas_call(functools.partial(experts_kernel, replicas), name='experts...  136 us
    pallas_call x1, Pallas kernels, final_sums(): pl.pallas_call(functools.partial(final_kernel, n_ctx), name='final_sums',...  80.6 us
    unnamed x65, local copies, waits for them, and re-layouts  15.2 us
  transfers between devices with their start and end apart: 4, of which 0 were waited for; matrix products, arithmetic and copies ran while one was open for 5% of the time, Pallas kernels for 23%

profile of v8, /device:TPU:0, one launch (start us, length us, event | category | flops | bytes accessed | tf_op | source)
XLA Modules:
  0.0 594.9 jit_solution(1823636953212517895)
XLA Ops:
  8.0 1.6 constant_dynamic-slice_fusion.5
  9.6 2.9 collective-permute-start.2
  12.5 1.6 constant_dynamic-slice_fusion.6
  14.2 2.1 collective-permute-start
  16.9 1.0 fusion.6
  18.0 1.1 copy.197.sin_ref
  19.2 1.0 copy.196.cos_ref
  21.8 1.3 copy.182.seg_ref
  23.2 2.2 constant_dynamic-slice_fusion.4
  25.4 2.7 copy.177
  28.1 1.4 copy-done.8
  30.4 2.8 copy.179
  33.1 2.7 copy.178
  38.1 137.5 %attention_forward.1 = (bf16[256,1536]{1,0:T(8,128)(2,1)}, bf16[4,32,384]{2,1,0:T(8,128)(2,1)}, bf16[4,384,1536]{2,1,0:T(8,128)(2,1)}, bf16[4,384,512]{2,1,0:T(8...) custom-call(bf16[256,1536]{1,0:T(8,128)(2,1)} %bitcast.109, ...), custom_call_target="tpu_custom_call" | custom-call | bytes 429000000 | tf_op jit(solution)/shard_map/attention_forward/pallas_call | solution.py:741
  175.6 1.6 copy.183
  177.5 4.0 multiply_reduce_fusion.2
  181.5 1.1 copy-done
  183.4 1.1 concatenate.22
  185.1 135.9 %experts.1 = (f32[256,1664]{1,0:T(8,128)}, bf16[8,256,1536]{2,1,0:T(8,128)(2,1)}, bf16[3,4,2,512,384]{4,3,2,1,0:T(8,128)(2,1)}, bf16[2,2,512,384]{3,2,1,0:T(8,12...) custom-call(bf16[256,1664]{1,0:T(8,128)(2,1)} %bitcast.114, bf16[256,1536]{1,0:T(8,128)(2,1)} %bitcast.115, ...), custom_call_target="tpu_custom_call" | custom-call | bytes 363000000 | tf_op jit(solution)/shard_map/experts/pallas_call | solution.py:377
  321.0 1.0 slice.61
  322.3 2.7 multiply_reduce_fusion
  326.2 1.4 convolution_convert_fusion
  327.8 3.6 bitcast_convert_fusion
  331.9 1.2 copy.194.g_own
  333.1 155.2 %attention_backward.1 = (bf16[256,1536]{1,0:T(8,128)(2,1)}, bf16[256,1536]{1,0:T(8,128)(2,1)}, f32[1,1536]{1,0:T(1,128)}, bf16[4,48,1536]{2,1,0:T(8,128)(2,1)}, ...) custom-call(bf16[8,3,128,128]{3,2,1,0:T(8,128)(2,1)} %copy.194.g_own, ...), custom_call_target="tpu_custom_call" | custom-call | bytes 412500000 | tf_op jit(solution)/shard_map/attention_backward/pallas_call | solution.py:1269
  488.3 1.1 multiply_bitcast_fusion
  493.6 80.6 %final_sums.1 = (bf16[8,3,2,48,512]{4,3,2,1,0:T(8,128)(2,1)}, f32[48,1536]{1,0:T(8,128)}, f32[8,128]{1,0:T(8,128)}) custom-call(f32[32,8,128]{2,1,0:T(8,128)} %bitcast.133, bf16[4,48,1536]{2,1,0:T(8,128)(2,1)} %get-tuple-element.63.output_part, bf16[3,4,2,512,384]{4,3,2,1,0:T(8,128)(2,1)} %get-tuple-element.54.grads, ...), custom_call_target="tpu_custom_call" | custom-call | bytes 264000000 | tf_op jit(solution)/shard_map/final_sums/pallas_call | solution.py:1489
  576.4 2.3 bitcast_convert_fusion.1
  578.7 2.1 copy.205
  580.7 2.1 copy.204
  582.8 2.1 copy.203
  584.9 0.9 copy.219
  (124 shorter events, 18.3 us)
Async XLA Ops:
  7.2 7.0 %copy-start.7 = (bf16[384,1536]{1,0:T(8,128)(2,1)S(1)}, bf16[384,1536]{1,0:T(8,128)(2,1)}, u32[]{:S(2)}) copy-start(bf16[384,1536]{1,0:T(8,128)(2,1)} %w_q.1) | copy-start | bytes 3538948
  7.2 9.1 %copy-start.19 = (bf16[384]{0:T(512)(128)(2,1)S(1)}, bf16[384]{0:T(512)(128)(2,1)}, u32[]{:S(2)}) copy-start(bf16[384]{0:T(512)(128)(2,1)} %param.22) | copy-start | bytes 2308
  7.2 9.1 %copy-start.20 = (bf16[384]{0:T(512)(128)(2,1)S(1)}, bf16[384]{0:T(512)(128)(2,1)}, u32[]{:S(2)}) copy-start(bf16[384]{0:T(512)(128)(2,1)} %param.27) | copy-start | bytes 2308
  7.2 9.1 %copy-start.14 = (s32[2,1024]{1,0:T(2,128)S(1)}, s32[2,1024]{1,0:T(2,128)}, u32[]{:S(2)}) copy-start(s32[2,1024]{1,0:T(2,128)} %param.17) | copy-start | bytes 24580
  7.2 9.1 %copy-start.17 = (s32[2,128,8]{1,2,0:T(8,128)S(1)}, s32[2,128,8]{1,2,0:T(8,128)}, u32[]{:S(2)}) copy-start(s32[2,128,8]{1,2,0:T(8,128)} %param.19) | copy-start | bytes 24580
  7.2 9.2 %copy-start.21 = (s32[2,128]{1,0:T(2,128)S(1)}, s32[2,128]{1,0:T(2,128)}, u32[]{:S(2)}) copy-start(s32[2,128]{1,0:T(2,128)} %param.20) | copy-start | bytes 3076
  7.2 177.8 %all-gather.3.cloned.1.call-start = ((), (), s32[]{:S(2)}) async-start(), calls=%async_computation | async-start | bytes 7077888 | tf_op jit(solution)/shard_map/all_gather | solution.py:1576
  9.6 27.7 %collective-permute-start.2 = (bf16[192,512]{1,0:T(8,128)(2,1)}, bf16[192,512]{1,0:T(8,128)(2,1)}, u32[]{:S(2)}, u32[]{:S(2)}) collective-permute-start(bf16[192,512]{1,0:T(8,128)(2,1)} %constant_dynamic-slice_fusion.5), channel_id=1, source_target_pairs={{0,2},{1,3},{2,0},{3,1},{4,6},{5,7},{6,4},{7,5},{8,10},{9,11},{10,... | collective-permute-start | bytes 589832 | tf_op jit(solution)/shard_map/ppermute | solution.py:1571
  14.2 23.1 %collective-permute-start.1 = (bf16[192,512]{1,0:T(8,128)(2,1)}, bf16[192,512]{1,0:T(8,128)(2,1)}, u32[]{:S(2)}, u32[]{:S(2)}) collective-permute-start(bf16[192,512]{1,0:T(8,128)(2,1)} %constant_dynamic-slice_fusion.6), channel_id=1, source_target_pairs={{0,2},{1,3},{2,0},{3,1},{4,6},{5,7},{6,4},{7,5},{8,10},{9,11},{10,... | collective-permute-start | bytes 589832 | tf_op jit(solution)/shard_map/ppermute | solution.py:1571
  14.2 23.1 %collective-permute-start = (bf16[192,1536]{1,0:T(8,128)(2,1)S(1)}, bf16[192,1536]{1,0:T(8,128)(2,1)S(1)}, u32[]{:S(2)}, u32[]{:S(2)}) collective-permute-start(bf16[192,1536]{1,0:T(8,128)(2,1)S(1)} %constant_dynamic-slice_fusion.7), channel_id=1, source_target_pairs={{0,2},{1,3},{2,0},{3,1},{4,6},{5,7},{6,4},{7,5},{8,10},{9,11},{10,... | collective-permute-start | bytes 1769480 | tf_op jit(solution)/shard_map/ppermute | solution.py:1571
  21.8 6.3 %slice-start = ((s8[6291456]{0:T(1024)(128)(4,1)}), s8[2097152]{0:T(1024)(128)(4,1)S(1)}, s32[]{:S(2)}) async-start(s8[6291456]{0:T(1024)(128)(4,1)} %bitcast.129), calls=%async_computation.1 | async-start | bytes 4194304
  23.2 5.0 slice-start.1
  25.4 4.2 copy-start.8
  33.1 2.8 copy-start.15
  33.1 3.5 copy-start.16
  37.3 0.8 copy-start.11
  175.6 1.7 copy-start.13
  175.6 1.8 copy-start.3
  177.3 4.2 copy-start.5
  181.4 1.1 copy-start
  321.0 4.5 slice-start.2
  322.3 2.7 copy-start.1
  322.3 2.7 copy-start.4
  322.3 3.8 slice-start.3
  326.2 1.4 copy-start.2
  326.2 1.7 copy-start.6
  489.5 2.7 copy-start.18
  582.8 2.1 copy-start.10
  584.8 1.4 copy-start.9
  584.9 2.3 copy-start.12
Sparse Core Ops, SparseCore 0:
  10.3 148.1 all-gather.2

commit v9 on v7

--- a/solution.py
+++ b/solution.py
@@ -49,7 +49,7 @@
 
 
 def other_chip(c, f, k):
-    pair, x = lax.div(k, 2), lax.rem(k, 2)
+    pair, x = lax.rem(k, 2), lax.div(k, 2)
     return (
         c + pair * (1 - 2 * lax.rem(c, 2)),
         f + 2 * x * (1 - 2 * lax.rem(lax.div(f, 2), 2)),
@@ -64,7 +64,7 @@
 
 
 def experts_kernel(
-    replicas, pay, cot, gate_own, up_own, down_own, after,
+    replicas, pay, cot, cot_pair, gate_own, up_own, down_own, after,
     back, mix, grads, down_came, pay_in, cot_in,
     weights, total, pay_now, cot_now, xs, gs, eo, gi, hid, dgate, dup, disp, comb,
     own, out, sib, ret, mix_now,
@@ -116,7 +116,7 @@
     def store_mix(k, s):
         return pltpu.make_async_copy(mix_now.at[s], mix.at[2 * k + s], store.at[s])
 
-    for k, a in ((0, 0), (0, 1), (1, 0), (2, 0), (1, 1), (2, 1), (3, 0), (3, 1)):
+    for k, a in ((0, 0), (0, 1), (1, 0), (2, 0), (2, 1), (3, 0), (3, 1)):
         push(k, a).start()
 
     def clear(i, carry):
@@ -137,14 +137,18 @@
             return copy
 
         def arrived(chip):
-            for a in range(2):
+            for a in range(1 if chip == 1 else 2):
                 push(chip, a).wait_recv()
                 forward(chip, a).start()
 
         def fetch_chip(chip):
-            for a in range(2):
+            if chip == 1:
+                for s in range(2):
+                    fetch(1, s, cot_pair.at[s])
+            among = range(1 if chip == 1 else 2)
+            for a in among:
                 fetch(a, 0, landed[a].at[2 * chip - 1])
-            for a in range(2):
+            for a in among:
                 forward(chip, a).wait_recv()
                 fetch(a, 1, landed[a].at[2 * chip])
 
@@ -162,7 +166,6 @@
         @pl.when(k == 1)
         def _():
             arrived(1)
-            arrived(2)
             fetch_chip(1)
 
         @pl.when(k > 0)
@@ -267,6 +270,7 @@
 
         @pl.when(k == 1)
         def _():
+            arrived(2)
             fetch_chip(2)
 
         @pl.when(k == 2)
@@ -332,7 +336,7 @@
     for k in (2, 3):
         to_sibling(k).wait_send()
     for k in range(4):
-        for a in range(2):
+        for a in range(1 if k == 1 else 2):
             push(k, a).wait_send()
             if k:
                 forward(k, a).wait_send()
@@ -345,7 +349,7 @@
         down_first.wait()
 
 
-def run_experts(cid, replicas, pay, cot, owns, after):
+def run_experts(cid, replicas, pay, cot, cot_pair, owns, after):
     width = D // replicas
     apart = width % 128 == 0
     tokens = SEQS * BLOCK
@@ -363,7 +367,7 @@
             jax.ShapeDtypeStruct((RANKS - 1, tokens, PAY), BF16),
             jax.ShapeDtypeStruct((RANKS - 1, tokens, D), BF16),
         ],
-        in_specs=[anywhere] * 6,
+        in_specs=[anywhere] * 7,
         out_specs=[inside] + [anywhere] * 5,
         scratch_shapes=[
             pltpu.VMEM((3, OWN, D, FF), BF16),
@@ -392,7 +396,7 @@
             collective_id=cid, has_side_effects=True, vmem_limit_bytes=63 << 20
         ),
         cost_estimate=lasting(110),
-    )(pay, cot, *owns, after)
+    )(pay, cot, cot_pair, *owns, after)
     if not apart:
         grads = grads.reshape(3, OWN, FF, replicas, width).transpose(0, 3, 1, 2, 4)
         grads = grads[:, jnp.array(plane_order(replicas))]
@@ -423,11 +427,12 @@
 
 
 def attention_forward_kernel(
-    parts, n_ctx, tok, small, w_q, w_k, w_v, w_o, near_q, near_k, near_v, pack0, pack1, pack2, cos_ref, sin_ref, seg_ref, code_ref,
+    parts, n_ctx, tok, small, w_q, w_k, w_v, w_o, near_q, near_k, near_v, pack0, pack1, pack2, cot, cos_ref, sin_ref, seg_ref, code_ref,
     normed, small_all, q_full, k_full, v_full, q_ref, kv_ref, full_ref, log_ref, o_back, o_full,
-    gate_own, up_own, down_own,
+    gate_own, up_own, down_own, cot_pair,
     acc, q_pack, kv_pack, o_buf, own_buf,
     send_w, recv_w, send_s, recv_s, send_e, recv_e, send_q, recv_q, send_kv, recv_kv, send_o, recv_o, here,
+    send_c, recv_c,
 ):
     c, f = lax.axis_index("ctx"), lax.axis_index("fsdp")
     head, part, pair = lax.div(c, parts), lax.rem(c, parts), lax.rem(c, 2)
@@ -497,6 +502,13 @@
     for copy in experts:
         copy.start()
 
+    cots = [
+        pltpu.make_async_remote_copy(
+            source, cot_pair.at[i], send_c.at[i], recv_c.at[i], device_id=device, device_id_type=MESH
+        )
+        for i, (source, device) in enumerate(((cot, over_pair), (cot_pair.at[0], sibling)))
+    ]
+    cots[0].start()
     x = tok[...].astype(F32)
     scale = lax.rsqrt(jnp.mean(x * x, axis=1, keepdims=True) + EPS)
     for copy in smalls:
@@ -579,6 +591,8 @@
     kv_stays.wait()
     for copy in to_heads:
         copy.wait_recv()
+    cots[0].wait_recv()
+    cots[1].start()
 
     count = REP * BLOCK
     halves = half_masks(BF16)
@@ -670,7 +684,8 @@
         copy.wait()
     for copy in experts:
         copy.wait()
-    for copy in smalls + to_heads:
+    cots[1].wait()
+    for copy in smalls + to_heads + cots[:1]:
         copy.wait_send()
     for a in range(4):
         for kind in (0, 2, 3, 4) if a < 3 else range(5):
@@ -678,7 +693,7 @@
 
 
 def attention_forward(
-    cid, parts, n_ctx, tok, small, w_q, w_k, w_v, w_o, nears, packs, cosine, sine, segq, codes
+    cid, parts, n_ctx, tok, small, w_q, w_k, w_v, w_o, nears, packs, cot, cosine, sine, segq, codes
 ):
     wide = 2 * HEAD_SIZE
     anywhere = pl.BlockSpec(memory_space=pl.ANY)
@@ -705,9 +720,10 @@
             jax.ShapeDtypeStruct(heads, F32),
             jax.ShapeDtypeStruct(heads, BF16),
             full(w_o), own, own, own,
+            jax.ShapeDtypeStruct((2,) + cot.shape, BF16),
         ],
-        in_specs=[inside] + [anywhere] * 11 + [inside] * 4,
-        out_specs=[inside] * 9 + [anywhere, inside] + [anywhere] * 3,
+        in_specs=[inside] + [anywhere] * 12 + [inside] * 4,
+        out_specs=[inside] * 9 + [anywhere, inside] + [anywhere] * 4,
         scratch_shapes=[
             pltpu.VMEM((SEQS * BLOCK, columns), F32),
             pltpu.VMEM(heads, BF16),
@@ -716,13 +732,13 @@
             pltpu.VMEM((3,) + packs[0].shape[1:], BF16),
             dma((4, 5)), dma((4, 5)), dma((3,)), dma((3,)), dma((3, 3)), dma((3, 3)),
             dma((others,)), dma((others,)), dma((n_ctx - 1,)), dma((n_ctx - 1,)),
-            dma((KEY_VALUE_HEADS,)), dma((KEY_VALUE_HEADS,)), dma((14,)),
+            dma((KEY_VALUE_HEADS,)), dma((KEY_VALUE_HEADS,)), dma((14,)), dma((2,)), dma((2,)),
         ],
         compiler_params=pltpu.CompilerParams(
             collective_id=cid, has_side_effects=True, vmem_limit_bytes=56 << 20
         ),
         cost_estimate=lasting(130),
-    )(tok, small, w_q, w_k, w_v, w_o, *nears, *packs, cosine, sine, segq, codes)
+    )(tok, small, w_q, w_k, w_v, w_o, *nears, *packs, cot, cosine, sine, segq, codes)
 
 
 def turn_back(field, cosine, sine):
@@ -877,7 +893,7 @@
     returns = [
         pltpu.make_async_remote_copy(
             shares.at[k], mix_in.at[k], send_mix.at[3 + k], recv_mix.at[3 + k],
-            device_id=(flip(c, k // 2), flip(f, 2 * (k % 2))), device_id_type=MESH,
+            device_id=(flip(c, k % 2), flip(f, 2 * (k // 2))), device_id_type=MESH,
         )
         for k in range(1, 4)
     ]
@@ -1555,10 +1571,10 @@
     all_sine = jnp.tile(all_sine, (1, 2)).reshape(n_ctx, BLOCK, 2 * HEAD_SIZE)
     (
         normed_in, small_all, full_query, full_key, full_value, q_all, kv_all, head_full, head_logs,
-        attn_heads, full_output, own_gate, own_up, own_down,
+        attn_heads, full_output, own_gate, own_up, own_down, cot_pair,
     ) = attention_forward(
         0, parts, n_ctx, tokens.reshape(SEQS * BLOCK, D), small, w_query, key_weight, value_weight,
-        w_output, nears, packs,
+        w_output, nears, packs, cotangent.reshape(SEQS * BLOCK, D),
         lax.dynamic_index_in_dim(all_cosine, c_index, 0, keepdims=False),
         lax.dynamic_index_in_dim(all_sine, c_index, 0, keepdims=False),
         segq, codes,
@@ -1591,7 +1607,7 @@
         axis=2,
     )
     back, mix_part, own_grads, down_first, down_early = run_experts(
-        2, replicas, payload.reshape(SEQS * BLOCK, PAY), cotangent.reshape(SEQS * BLOCK, D),
+        2, replicas, payload.reshape(SEQS * BLOCK, PAY), cotangent.reshape(SEQS * BLOCK, D), cot_pair,
         (own_gate, own_up, own_down), tokens_all
     )
 

time: 569 us -> 582 us (1.023)
  Pallas kernels: 474 us -> 485 us
    pallas_call x1, Pallas kernels: 128 us -> 137 us  [attention_backward(): pl.pallas_call(functools.partial(attention_backward_kernel, parts, n_ctx,...]
    unnamed x65 -> x61, local copies, waits for them, and re-layouts: 15.2 us -> 14.3 us
  transfers between devices with their start and end apart: 4 -> 4, of which waited for: 0 -> 0; matrix products, arithmetic and copies ran while one was open for 6% -> 5% of each run, Pallas kernels for 23% -> 22%
where the time goes in v9:
time: 582 us; the launch traced here: 573 us
  Pallas kernels  485 us (83%)
  local copies, waits for them, and re-layouts  44.6 us (8%)
  matrix products  15.3 us (3%)
  between operations  15 us (3%)
  other arithmetic  7.1 us (1%)
    pallas_call x1, Pallas kernels, run_experts(): pl.pallas_call(functools.partial(experts_kernel, replicas), name='experts...  139 us
    pallas_call x1, Pallas kernels, attention_backward(): pl.pallas_call(functools.partial(attention_backward_kernel, parts, n_ctx,...  137 us
    pallas_call x1, Pallas kernels, attention_forward(): pl.pallas_call(functools.partial(attention_forward_kernel, parts, n_ctx),...  128 us
    pallas_call x1, Pallas kernels, final_sums(): pl.pallas_call(functools.partial(final_kernel, n_ctx), name='final_sums',...  80.2 us
    unnamed x61, local copies, waits for them, and re-layouts  14.3 us
  transfers between devices with their start and end apart: 4, of which 0 were waited for; matrix products, arithmetic and copies ran while one was open for 5% of the time, Pallas kernels for 22%

profile of v9, /device:TPU:0, one launch (start us, length us, event | category | flops | bytes accessed | tf_op | source)
XLA Modules:
  0.0 572.7 jit_solution(18014221334976039621)
XLA Ops:
  8.0 1.6 constant_dynamic-slice_fusion.5
  9.6 2.9 collective-permute-start.2
  12.5 1.6 constant_dynamic-slice_fusion.6
  14.2 2.1 collective-permute-start
  16.9 1.0 fusion.6
  18.0 1.0 copy.197.sin_ref
  19.2 1.0 copy.196.cos_ref
  21.8 1.3 copy.182.seg_ref
  23.1 2.2 constant_dynamic-slice_fusion.4
  25.4 2.7 copy.177
  28.1 1.5 copy-done.8
  30.4 2.8 copy.179
  33.1 2.7 copy.178
  38.1 127.9 %attention_forward.1 = (bf16[256,1536]{1,0:T(8,128)(2,1)}, bf16[4,32,384]{2,1,0:T(8,128)(2,1)}, bf16[4,384,1536]{2,1,0:T(8,128)(2,1)}, bf16[4,384,512]{2,1,0:T(8...) custom-call(bf16[256,1536]{1,0:T(8,128)(2,1)} %bitcast.111, ...), custom_call_target="tpu_custom_call" | custom-call | bytes 429000000 | tf_op jit(solution)/shard_map/attention_forward/pallas_call | solution.py:711
  166.0 1.6 copy.183
  167.9 4.0 multiply_reduce_fusion.2
  171.9 1.1 copy-done
  173.8 1.1 concatenate.22
  175.5 139.4 %experts.1 = (f32[256,1664]{1,0:T(8,128)}, bf16[8,256,1536]{2,1,0:T(8,128)(2,1)}, bf16[3,4,2,512,384]{4,3,2,1,0:T(8,128)(2,1)}, bf16[2,2,512,384]{3,2,1,0:T(8,12...) custom-call(bf16[256,1664]{1,0:T(8,128)(2,1)} %bitcast.116, bf16[256,1536]{1,0:T(8,128)(2,1)} %bitcast.110, ...), custom_call_target="tpu_custom_call" | custom-call | bytes 363000000 | tf_op jit(solution)/shard_map/experts/pallas_call | solution.py:359
  314.9 0.9 slice.61
  316.1 2.7 multiply_reduce_fusion
  319.3 4.3 convolution_convert_fusion
  323.6 3.6 bitcast_convert_fusion
  327.7 1.2 copy.194.g_own
  328.9 137.5 %attention_backward.1 = (bf16[256,1536]{1,0:T(8,128)(2,1)}, bf16[256,1536]{1,0:T(8,128)(2,1)}, f32[1,1536]{1,0:T(1,128)}, bf16[4,48,1536]{2,1,0:T(8,128)(2,1)}, ...) custom-call(bf16[8,3,128,128]{3,2,1,0:T(8,128)(2,1)} %copy.194.g_own, ...), custom_call_target="tpu_custom_call" | custom-call | bytes 412500000 | tf_op jit(solution)/shard_map/attention_backward/pallas_call | solution.py:1240
  466.3 1.1 multiply_bitcast_fusion
  471.6 80.2 %final_sums.1 = (bf16[8,3,2,48,512]{4,3,2,1,0:T(8,128)(2,1)}, f32[48,1536]{1,0:T(8,128)}, f32[8,128]{1,0:T(8,128)}) custom-call(f32[32,8,128]{2,1,0:T(8,128)} %bitcast.134, bf16[4,48,1536]{2,1,0:T(8,128)(2,1)} %get-tuple-element.65.output_part, bf16[3,4,2,512,384]{4,3,2,1,0:T(8,128)(2,1)} %get-tuple-element.56.grads, ...), custom_call_target="tpu_custom_call" | custom-call | bytes 264000000 | tf_op jit(solution)/shard_map/final_sums/pallas_call | solution.py:1460
  554.0 2.3 bitcast_convert_fusion.1
  556.3 2.1 copy.205
  558.3 2.1 copy.204
  560.4 2.1 copy.203
  562.5 0.9 copy.219
  (119 shorter events, 17.4 us)
Async XLA Ops:
  7.2 7.0 %copy-start.7 = (bf16[384,1536]{1,0:T(8,128)(2,1)S(1)}, bf16[384,1536]{1,0:T(8,128)(2,1)}, u32[]{:S(2)}) copy-start(bf16[384,1536]{1,0:T(8,128)(2,1)} %w_q.1) | copy-start | bytes 3538948
  7.2 9.1 %copy-start.19 = (bf16[384]{0:T(512)(128)(2,1)S(1)}, bf16[384]{0:T(512)(128)(2,1)}, u32[]{:S(2)}) copy-start(bf16[384]{0:T(512)(128)(2,1)} %param.22) | copy-start | bytes 2308
  7.2 9.1 %copy-start.20 = (bf16[384]{0:T(512)(128)(2,1)S(1)}, bf16[384]{0:T(512)(128)(2,1)}, u32[]{:S(2)}) copy-start(bf16[384]{0:T(512)(128)(2,1)} %param.27) | copy-start | bytes 2308
  7.2 9.1 %copy-start.14 = (s32[2,1024]{1,0:T(2,128)S(1)}, s32[2,1024]{1,0:T(2,128)}, u32[]{:S(2)}) copy-start(s32[2,1024]{1,0:T(2,128)} %param.17) | copy-start | bytes 24580
  7.2 9.1 %copy-start.17 = (s32[2,128,8]{1,2,0:T(8,128)S(1)}, s32[2,128,8]{1,2,0:T(8,128)}, u32[]{:S(2)}) copy-start(s32[2,128,8]{1,2,0:T(8,128)} %param.19) | copy-start | bytes 24580
  7.2 9.2 %copy-start.21 = (s32[2,128]{1,0:T(2,128)S(1)}, s32[2,128]{1,0:T(2,128)}, u32[]{:S(2)}) copy-start(s32[2,128]{1,0:T(2,128)} %param.20) | copy-start | bytes 3076
  7.2 168.2 %all-gather.3.cloned.1.call-start = ((), (), s32[]{:S(2)}) async-start(), calls=%async_computation | async-start | bytes 7077888 | tf_op jit(solution)/shard_map/all_gather | solution.py:1547
  9.6 27.6 %collective-permute-start.2 = (bf16[192,512]{1,0:T(8,128)(2,1)}, bf16[192,512]{1,0:T(8,128)(2,1)}, u32[]{:S(2)}, u32[]{:S(2)}) collective-permute-start(bf16[192,512]{1,0:T(8,128)(2,1)} %constant_dynamic-slice_fusion.5), channel_id=1, source_target_pairs={{0,2},{1,3},{2,0},{3,1},{4,6},{5,7},{6,4},{7,5},{8,10},{9,11},{10,... | collective-permute-start | bytes 589832 | tf_op jit(solution)/shard_map/ppermute | solution.py:1542
  14.2 23.1 %collective-permute-start.1 = (bf16[192,512]{1,0:T(8,128)(2,1)}, bf16[192,512]{1,0:T(8,128)(2,1)}, u32[]{:S(2)}, u32[]{:S(2)}) collective-permute-start(bf16[192,512]{1,0:T(8,128)(2,1)} %constant_dynamic-slice_fusion.6), channel_id=1, source_target_pairs={{0,2},{1,3},{2,0},{3,1},{4,6},{5,7},{6,4},{7,5},{8,10},{9,11},{10,... | collective-permute-start | bytes 589832 | tf_op jit(solution)/shard_map/ppermute | solution.py:1542
  14.2 23.0 %collective-permute-start = (bf16[192,1536]{1,0:T(8,128)(2,1)S(1)}, bf16[192,1536]{1,0:T(8,128)(2,1)S(1)}, u32[]{:S(2)}, u32[]{:S(2)}) collective-permute-start(bf16[192,1536]{1,0:T(8,128)(2,1)S(1)} %constant_dynamic-slice_fusion.7), channel_id=1, source_target_pairs={{0,2},{1,3},{2,0},{3,1},{4,6},{5,7},{6,4},{7,5},{8,10},{9,11},{10,... | collective-permute-start | bytes 1769480 | tf_op jit(solution)/shard_map/ppermute | solution.py:1542
  21.8 6.3 %slice-start = ((s8[6291456]{0:T(1024)(128)(4,1)}), s8[2097152]{0:T(1024)(128)(4,1)S(1)}, s32[]{:S(2)}) async-start(s8[6291456]{0:T(1024)(128)(4,1)} %bitcast.130), calls=%async_computation.1 | async-start | bytes 4194304
  23.1 5.0 slice-start.1
  25.4 4.2 copy-start.8
  33.1 2.8 copy-start.15
  33.1 3.5 copy-start.16
  37.3 0.8 copy-start.11
  166.0 1.7 copy-start.13
  166.0 1.8 copy-start.4
  167.7 4.2 copy-start.5
  171.9 1.1 copy-start
  316.1 2.7 copy-start.1
  316.1 2.7 copy-start.3
  319.3 4.3 copy-start.2
  319.3 4.3 copy-start.6
  467.5 2.7 copy-start.18
  560.4 2.1 copy-start.10
  562.5 1.4 copy-start.9
  562.5 2.3 copy-start.12
Sparse Core Ops, SparseCore 0:
  10.3 153.6 all-gather.2

commit v10 on v8

--- a/solution.py
+++ b/solution.py
@@ -450,7 +450,6 @@
     gate_own, up_own, down_own,
     acc, q_pack, kv_pack, o_buf, own_buf,
     send_w, recv_w, send_s, recv_s, send_e, recv_e, send_q, recv_q, send_kv, recv_kv, send_o, recv_o, here,
-    send_z, recv_z,
 ):
     c, f = lax.axis_index("ctx"), lax.axis_index("fsdp")
     head, part, pair = lax.div(c, parts), lax.rem(c, parts), lax.rem(c, 2)
@@ -509,34 +508,15 @@
     for a in range(4):
         for kind in (3, 0, 2) if a < 3 else (1, 0):
             weight(a, kind).start()
-    bit = lax.rem(lax.div(c, 2), 2)
-    half_rows = pl.ds(pl.multiple_of(bit * half, half), half)
-
-    def half_of(owner):
-        return pl.ds(pl.multiple_of(owner * rows + bit * half, half), half)
-
-    shared = [
-        pltpu.make_async_remote_copy(
-            packs[2].at[flip(f, i), :, half_rows], owns[2].at[:, half_of(f)],
-            send_e.at[i - 1, 2], recv_e.at[i - 1, 2], device_id=(c, flip(f, i)), device_id_type=MESH,
-        )
-        for i in (2, 3)
-    ]
-    onward = [
-        pltpu.make_async_remote_copy(
-            owns[2].at[:, half_of(flip(f, i))], owns[2].at[:, half_of(flip(f, i))],
-            send_z.at[i - 2], recv_z.at[i - 2], device_id=(flip(c, 2), f), device_id_type=MESH,
-        )
-        for i in (2, 3)
-    ]
     experts = [
         pltpu.make_async_remote_copy(
             packs[m].at[flip(f, i)], owns[m].at[:, my_rows], send_e.at[i - 1, m], recv_e.at[i - 1, m],
             device_id=(c, flip(f, i)), device_id_type=MESH,
         )
-        for m, i in ((2, 1), (0, 1), (0, 2), (0, 3), (1, 1), (1, 2), (1, 3))
+        for m in range(3)
+        for i in range(1, 4)
     ]
-    for copy in shared + experts:
+    for copy in experts:
         copy.start()
 
     x = tok[...].astype(F32)
@@ -621,9 +601,6 @@
     kv_stays.wait()
     for copy in to_heads:
         copy.wait_recv()
-    for came, goes in zip(shared, onward):
-        came.wait_recv()
-        goes.start()
 
     count = REP * BLOCK
     halves = half_masks(BF16)
@@ -713,9 +690,9 @@
     local[3].wait()
     for copy in stores:
         copy.wait()
-    for copy in experts + onward:
+    for copy in experts:
         copy.wait()
-    for copy in smalls + to_heads + shared:
+    for copy in smalls + to_heads:
         copy.wait_send()
     for a in range(4):
         for kind in (0, 2, 3, 4) if a < 3 else range(5):
@@ -761,7 +738,7 @@
             pltpu.VMEM((3,) + packs[0].shape[1:], BF16),
             dma((4, 5)), dma((4, 5)), dma((3,)), dma((3,)), dma((3, 3)), dma((3, 3)),
             dma((others,)), dma((others,)), dma((n_ctx - 1,)), dma((n_ctx - 1,)),
-            dma((KEY_VALUE_HEADS,)), dma((KEY_VALUE_HEADS,)), dma((14,)), dma((2,)), dma((2,)),
+            dma((KEY_VALUE_HEADS,)), dma((KEY_VALUE_HEADS,)), dma((14,)),
         ],
         compiler_params=pltpu.CompilerParams(
             collective_id=cid, has_side_effects=True, vmem_limit_bytes=56 << 20

time: 604 us -> 568 us (0.940)
  Pallas kernels: 509 us -> 473 us
    pallas_call x1, Pallas kernels: 155 us -> 128 us  [attention_backward(): pl.pallas_call(functools.partial(attention_backward_kernel, parts, n_ctx,...]
    pallas_call x1, Pallas kernels: 137 us -> 128 us  [attention_forward(): pl.pallas_call(functools.partial(attention_forward_kernel, parts, n_ctx),...]
  transfers between devices with their start and end apart: 4 -> 4, of which waited for: 0 -> 0; matrix products, arithmetic and copies ran while one was open for 5% -> 6% of each run, Pallas kernels for 23% -> 23%
where the time goes in v10:
time: 568 us; the launch traced here: 559 us
  Pallas kernels  473 us (83%)
  local copies, waits for them, and re-layouts  45.6 us (8%)
  between operations  14.8 us (3%)
  matrix products  12.4 us (2%)
  other arithmetic  7.1 us (1%)
    pallas_call x1, Pallas kernels, run_experts(): pl.pallas_call(functools.partial(experts_kernel, replicas), name='experts...  137 us
    pallas_call x1, Pallas kernels, attention_backward(): pl.pallas_call(functools.partial(attention_backward_kernel, parts, n_ctx,...  128 us
    pallas_call x1, Pallas kernels, attention_forward(): pl.pallas_call(functools.partial(attention_forward_kernel, parts, n_ctx),...  128 us
    pallas_call x1, Pallas kernels, final_sums(): pl.pallas_call(functools.partial(final_kernel, n_ctx), name='final_sums',...  80.2 us
    unnamed x65, local copies, waits for them, and re-layouts  15.2 us
  transfers between devices with their start and end apart: 4, of which 0 were waited for; matrix products, arithmetic and copies ran while one was open for 6% of the time, Pallas kernels for 23%

profile of v10, /device:TPU:0, one launch (start us, length us, event | category | flops | bytes accessed | tf_op | source)
XLA Modules:
  0.0 558.8 jit_solution(12872386257378960485)
XLA Ops:
  8.0 1.6 constant_dynamic-slice_fusion.5
  9.6 2.9 collective-permute-start.2
  12.5 1.6 constant_dynamic-slice_fusion.6
  14.2 2.1 collective-permute-start
  16.9 1.0 fusion.6
  18.0 1.1 copy.197.sin_ref
  19.2 1.0 copy.196.cos_ref
  21.8 1.3 copy.182.seg_ref
  23.2 2.2 constant_dynamic-slice_fusion.4
  25.4 2.7 copy.177
  28.1 1.4 copy-done.8
  30.4 2.8 copy.179
  33.1 2.7 copy.178
  38.1 127.8 %attention_forward.1 = (bf16[256,1536]{1,0:T(8,128)(2,1)}, bf16[4,32,384]{2,1,0:T(8,128)(2,1)}, bf16[4,384,1536]{2,1,0:T(8,128)(2,1)}, bf16[4,384,512]{2,1,0:T(8...) custom-call(bf16[256,1536]{1,0:T(8,128)(2,1)} %bitcast.109, ...), custom_call_target="tpu_custom_call" | custom-call | bytes 429000000 | tf_op jit(solution)/shard_map/attention_forward/pallas_call | solution.py:718
  166.0 1.6 copy.183
  167.8 4.0 multiply_reduce_fusion.2
  171.8 1.1 copy-done
  173.7 1.1 concatenate.22
  175.4 137.1 %experts.1 = (f32[256,1664]{1,0:T(8,128)}, bf16[8,256,1536]{2,1,0:T(8,128)(2,1)}, bf16[3,4,2,512,384]{4,3,2,1,0:T(8,128)(2,1)}, bf16[2,2,512,384]{3,2,1,0:T(8,12...) custom-call(bf16[256,1664]{1,0:T(8,128)(2,1)} %bitcast.114, bf16[256,1536]{1,0:T(8,128)(2,1)} %bitcast.115, ...), custom_call_target="tpu_custom_call" | custom-call | bytes 363000000 | tf_op jit(solution)/shard_map/experts/pallas_call | solution.py:377
  312.6 1.0 slice.61
  313.9 2.7 multiply_reduce_fusion
  317.7 1.4 convolution_convert_fusion
  319.4 3.6 bitcast_convert_fusion
  323.5 1.2 copy.194.g_own
  324.6 128.0 %attention_backward.1 = (bf16[256,1536]{1,0:T(8,128)(2,1)}, bf16[256,1536]{1,0:T(8,128)(2,1)}, f32[1,1536]{1,0:T(1,128)}, bf16[4,48,1536]{2,1,0:T(8,128)(2,1)}, ...) custom-call(bf16[8,3,128,128]{3,2,1,0:T(8,128)(2,1)} %copy.194.g_own, ...), custom_call_target="tpu_custom_call" | custom-call | bytes 412500000 | tf_op jit(solution)/shard_map/attention_backward/pallas_call | solution.py:1246
  452.6 1.1 multiply_bitcast_fusion
  457.9 80.2 %final_sums.1 = (bf16[8,3,2,48,512]{4,3,2,1,0:T(8,128)(2,1)}, f32[48,1536]{1,0:T(8,128)}, f32[8,128]{1,0:T(8,128)}) custom-call(f32[32,8,128]{2,1,0:T(8,128)} %bitcast.133, bf16[4,48,1536]{2,1,0:T(8,128)(2,1)} %get-tuple-element.63.output_part, bf16[3,4,2,512,384]{4,3,2,1,0:T(8,128)(2,1)} %get-tuple-element.54.grads, ...), custom_call_target="tpu_custom_call" | custom-call | bytes 264000000 | tf_op jit(solution)/shard_map/final_sums/pallas_call | solution.py:1466
  540.3 2.3 bitcast_convert_fusion.1
  542.6 2.1 copy.205
  544.6 2.1 copy.204
  546.7 2.1 copy.203
  548.7 0.9 copy.219
  (124 shorter events, 18.3 us)
Async XLA Ops:
  7.2 7.0 %copy-start.7 = (bf16[384,1536]{1,0:T(8,128)(2,1)S(1)}, bf16[384,1536]{1,0:T(8,128)(2,1)}, u32[]{:S(2)}) copy-start(bf16[384,1536]{1,0:T(8,128)(2,1)} %w_q.1) | copy-start | bytes 3538948
  7.2 9.1 %copy-start.19 = (bf16[384]{0:T(512)(128)(2,1)S(1)}, bf16[384]{0:T(512)(128)(2,1)}, u32[]{:S(2)}) copy-start(bf16[384]{0:T(512)(128)(2,1)} %param.22) | copy-start | bytes 2308
  7.2 9.1 %copy-start.20 = (bf16[384]{0:T(512)(128)(2,1)S(1)}, bf16[384]{0:T(512)(128)(2,1)}, u32[]{:S(2)}) copy-start(bf16[384]{0:T(512)(128)(2,1)} %param.27) | copy-start | bytes 2308
  7.2 9.1 %copy-start.14 = (s32[2,1024]{1,0:T(2,128)S(1)}, s32[2,1024]{1,0:T(2,128)}, u32[]{:S(2)}) copy-start(s32[2,1024]{1,0:T(2,128)} %param.17) | copy-start | bytes 24580
  7.2 9.1 %copy-start.17 = (s32[2,128,8]{1,2,0:T(8,128)S(1)}, s32[2,128,8]{1,2,0:T(8,128)}, u32[]{:S(2)}) copy-start(s32[2,128,8]{1,2,0:T(8,128)} %param.19) | copy-start | bytes 24580
  7.2 9.2 %copy-start.21 = (s32[2,128]{1,0:T(2,128)S(1)}, s32[2,128]{1,0:T(2,128)}, u32[]{:S(2)}) copy-start(s32[2,128]{1,0:T(2,128)} %param.20) | copy-start | bytes 3076
  7.2 168.2 %all-gather.3.cloned.1.call-start = ((), (), s32[]{:S(2)}) async-start(), calls=%async_computation | async-start | bytes 7077888 | tf_op jit(solution)/shard_map/all_gather | solution.py:1553
  9.6 27.7 %collective-permute-start.2 = (bf16[192,512]{1,0:T(8,128)(2,1)}, bf16[192,512]{1,0:T(8,128)(2,1)}, u32[]{:S(2)}, u32[]{:S(2)}) collective-permute-start(bf16[192,512]{1,0:T(8,128)(2,1)} %constant_dynamic-slice_fusion.5), channel_id=1, source_target_pairs={{0,2},{1,3},{2,0},{3,1},{4,6},{5,7},{6,4},{7,5},{8,10},{9,11},{10,... | collective-permute-start | bytes 589832 | tf_op jit(solution)/shard_map/ppermute | solution.py:1548
  14.2 23.1 %collective-permute-start.1 = (bf16[192,512]{1,0:T(8,128)(2,1)}, bf16[192,512]{1,0:T(8,128)(2,1)}, u32[]{:S(2)}, u32[]{:S(2)}) collective-permute-start(bf16[192,512]{1,0:T(8,128)(2,1)} %constant_dynamic-slice_fusion.6), channel_id=1, source_target_pairs={{0,2},{1,3},{2,0},{3,1},{4,6},{5,7},{6,4},{7,5},{8,10},{9,11},{10,... | collective-permute-start | bytes 589832 | tf_op jit(solution)/shard_map/ppermute | solution.py:1548
  14.2 23.1 %collective-permute-start = (bf16[192,1536]{1,0:T(8,128)(2,1)S(1)}, bf16[192,1536]{1,0:T(8,128)(2,1)S(1)}, u32[]{:S(2)}, u32[]{:S(2)}) collective-permute-start(bf16[192,1536]{1,0:T(8,128)(2,1)S(1)} %constant_dynamic-slice_fusion.7), channel_id=1, source_target_pairs={{0,2},{1,3},{2,0},{3,1},{4,6},{5,7},{6,4},{7,5},{8,10},{9,11},{10,... | collective-permute-start | bytes 1769480 | tf_op jit(solution)/shard_map/ppermute | solution.py:1548
  21.8 6.3 %slice-start = ((s8[6291456]{0:T(1024)(128)(4,1)}), s8[2097152]{0:T(1024)(128)(4,1)S(1)}, s32[]{:S(2)}) async-start(s8[6291456]{0:T(1024)(128)(4,1)} %bitcast.129), calls=%async_computation.1 | async-start | bytes 4194304
  23.2 5.0 slice-start.1
  25.4 4.2 copy-start.8
  33.1 2.8 copy-start.15
  33.1 3.5 copy-start.16
  37.3 0.8 copy-start.11
  166.0 1.7 copy-start.13
  166.0 1.8 copy-start.3
  167.6 4.2 copy-start.5
  171.8 1.1 copy-start
  312.6 4.5 slice-start.2
  313.9 2.7 copy-start.1
  313.9 2.7 copy-start.4
  313.9 3.8 slice-start.3
  317.7 1.4 copy-start.2
  317.7 1.7 copy-start.6
  453.8 2.7 copy-start.18
  546.7 2.1 copy-start.10
  548.7 1.4 copy-start.9
  548.7 2.3 copy-start.12
Sparse Core Ops, SparseCore 0:
  10.3 145.7 all-gather.2
